TPU v7x, 32 devices: a whole 2x2x4 slice. The times are simulated.
32 devices in a mesh: rep: 2 (over y), fsdp: 16 (over z, x, core).
Axes of the slice: x: 2, y: 2, z: 4, core: 2. Of those that a mesh axis runs over, the one named last changes fastest.
Arguments:
- x_in: bfloat16 [2, 2048, 512], P('rep', 'fsdp'), may hold values from -8 to 8
- d_out: bfloat16 [2, 2048, 512], P('rep', 'fsdp'), may hold values from -0.375 to 0.375
- gate_weight: bfloat16 [64, 128, 128], P('fsdp'), may hold values from -0.25 to 0.25
- up_weight: bfloat16 [64, 128, 128], P('fsdp'), may hold values from -0.25 to 0.25
- down_weight: bfloat16 [64, 128, 128], P('fsdp'), may hold values from -0.125 to 0.125
- mom_gate: float32 [2, 64, 128, 128], P('rep', 'fsdp'), may hold values from -6 to 6
- mom_up: float32 [2, 64, 128, 128], P('rep', 'fsdp'), may hold values from -6 to 6
- mom_down: float32 [2, 64, 128, 128], P('rep', 'fsdp'), may hold values from -6 to 6
- band_index: int32 [3, 64, 512], P(None, 'fsdp'), may hold values from 0 to 16383, as said below
Outputs:
- res_gate: float32 [2, 64, 128, 128], P('rep', 'fsdp')
- res_up: float32 [2, 64, 128, 128], P('rep', 'fsdp')
- down_residual_blocks: float32 [2, 64, 128, 128], P('rep', 'fsdp')
- upd_gate: float32 [64, 128, 128], P('fsdp')
- upd_up: float32 [64, 128, 128], P('fsdp')
- upd_down: float32 [64, 128, 128], P('fsdp')
Inputs may be any that keep to these rules, and one draw needn't show every extreme that they name: `band_index`: each row of 512 positions of a block holds distinct values; the positions are the same for every replica group.
All inputs are finite; a program needn't handle non-finite values.
Results may differ from a plain program's by a relative error of at most 0.0028.
Values may be sent and summed in bfloat16 or wider, within the bound.
No kernel may reach another device: no remote copies, remote signals or barrier semaphores. Data moves between devices by JAX's collectives and lax.ppermute only.
A program may use at most 128 MiB of HBM per device.

v0:
```python
import jax
import jax.numpy as jnp
from jax import lax
from jax.sharding import PartitionSpec as P

momentum_decay = 0.999


def dct_table(side_len):
    freq_rows = jnp.arange(side_len, dtype=jnp.float32)[:, None]
    cell_cols = jnp.arange(side_len, dtype=jnp.float32)[None, :]
    weights = jnp.where(freq_rows == 0, jnp.sqrt(1.0 / side_len), jnp.sqrt(2.0 / side_len))
    return weights * jnp.cos(jnp.pi * (2.0 * cell_cols + 1.0) * freq_rows / (2.0 * side_len))


def forward_blocks(cosines, blocks):
    inner = jnp.matmul(cosines, blocks, precision=lax.Precision.HIGHEST)
    return jnp.matmul(inner, cosines.T, precision=lax.Precision.HIGHEST)


def inverse_blocks(cosines, coeffs):
    inner = jnp.matmul(cosines.T, coeffs, precision=lax.Precision.HIGHEST)
    return jnp.matmul(inner, cosines, precision=lax.Precision.HIGHEST)


def place_band(values, positions, side_len):
    layout = (positions.shape[0], positions.shape[1], side_len * side_len)
    matrix_ids = jnp.arange(layout[0])[:, None, None]
    span_ids = jnp.arange(layout[1])[None, :, None]
    filled = jnp.zeros(layout, values.dtype).at[matrix_ids, span_ids, positions].set(values)
    return filled.reshape(layout[0], layout[1], side_len, side_len)


def band_split(moments, gradients, band_index):
    side_len = moments.shape[2]
    updated = momentum_decay * moments + gradients
    cosines = dct_table(side_len)
    coeffs = forward_blocks(cosines, updated)
    flattened = coeffs.reshape(coeffs.shape[0], coeffs.shape[1], side_len * side_len)
    picked = jnp.take_along_axis(flattened, band_index, axis=2)
    kept_part = inverse_blocks(cosines, place_band(picked, band_index, side_len))
    return (updated - kept_part, picked)


def per_device(
    x_in, d_out, gate_weight, up_weight, down_weight, mom_gate, mom_up, mom_down, band_index
):
    x_rows = x_in[0]
    d_rows = d_out[0]
    span_side = gate_weight.shape[1]
    blk_dev = gate_weight.shape[0]
    tok_rows = x_rows.shape[0]
    shard_count = lax.axis_size("fsdp")
    row_blocks = x_rows.shape[1] // span_side
    col_blocks = blk_dev * shard_count // row_blocks
    input_row_blocks = x_rows.reshape(tok_rows, row_blocks, span_side)
    d_blocks = d_rows.reshape(tok_rows, row_blocks, span_side)
    col_parts = jnp.stack([input_row_blocks, d_blocks], axis=2)
    col_send = jnp.tile(col_parts, (1, col_blocks, 1, 1)).reshape(
        tok_rows, shard_count, blk_dev, col_parts.shape[2], span_side
    )
    col_ids_all = jnp.arange(col_blocks, dtype=jnp.int32)
    matrix_pieces = (
        lax.all_gather(gate_weight, "fsdp", axis=0, tiled=True),
        lax.all_gather(up_weight, "fsdp", axis=0, tiled=True),
        lax.all_gather(down_weight, "fsdp", axis=0, tiled=True),
    )
    count = matrix_pieces[0].shape[0]
    block_ids = jnp.arange(count, dtype=jnp.int32)
    row_ids = block_ids % row_blocks
    column_numbers = block_ids // row_blocks
    x_sel = jnp.take(input_row_blocks, row_ids, axis=1)
    selected_delta = jnp.take(d_blocks, row_ids, axis=1)
    paired = jnp.concatenate([matrix_pieces[0], matrix_pieces[1]], axis=2)
    gu_terms = jnp.einsum("tic,ice->tie", x_sel, paired, preferred_element_type=jnp.float32)
    hidden_delta_terms = jnp.einsum(
        "bpd,pud->bpu", selected_delta, matrix_pieces[2], preferred_element_type=jnp.float32
    )
    placer = (column_numbers[:, None] == col_ids_all[None, :]).astype(jnp.float32)
    gu_new = jnp.einsum("tie,if->tfe", gu_terms, placer, precision=lax.Precision.HIGHEST)
    dh_new = jnp.einsum("tie,if->tfe", hidden_delta_terms, placer, precision=lax.Precision.HIGHEST)
    gate_pre = gu_new[:, :, :span_side]
    up_pre = gu_new[:, :, span_side:]
    sigmoid_gate = jax.nn.sigmoid(gate_pre)
    hidden = (gate_pre * sigmoid_gate * up_pre).astype(jnp.bfloat16)
    d_gate = (dh_new * up_pre * sigmoid_gate * (1.0 + gate_pre * (1.0 - sigmoid_gate))).astype(
        jnp.bfloat16
    )
    d_up = (dh_new * gate_pre * sigmoid_gate).astype(jnp.bfloat16)
    act_parts = jnp.stack([d_gate, d_up, hidden], axis=2)
    act_send = jnp.repeat(act_parts, row_blocks, axis=1).reshape(
        tok_rows, shard_count, blk_dev, act_parts.shape[2], span_side
    )
    matrix_pieces = (
        lax.all_to_all(col_send, "fsdp", split_axis=1, concat_axis=0, tiled=True),
        lax.all_to_all(act_send, "fsdp", split_axis=1, concat_axis=0, tiled=True),
    )
    cols = matrix_pieces[0][:, 0]
    acts = matrix_pieces[1][:, 0]
    g_gate = jnp.einsum(
        "tic,tid->icd", cols[:, :, 0], acts[:, :, 0], preferred_element_type=jnp.float32
    )
    g_up = jnp.einsum(
        "tic,tid->icd", cols[:, :, 0], acts[:, :, 1], preferred_element_type=jnp.float32
    )
    g_down = jnp.einsum(
        "tic,tid->icd", acts[:, :, 2], cols[:, :, 1], preferred_element_type=jnp.float32
    )
    moments = jnp.stack([mom_gate[0], mom_up[0], mom_down[0]])
    gradients = jnp.stack([g_gate, g_up, g_down])
    remains, picked = band_split(moments, gradients, band_index)
    summed = jnp.sum(lax.all_gather(picked[None], "rep", axis=0, tiled=True), axis=0)
    updates = inverse_blocks(dct_table(span_side), place_band(summed, band_index, span_side))
    return (
        remains[0][None],
        remains[1][None],
        remains[2][None],
        updates[0],
        updates[1],
        updates[2],
    )


def solution(mesh):
    in_specs = (
        P("rep", "fsdp", None),
        P("rep", "fsdp", None),
        P("fsdp", None, None),
        P("fsdp", None, None),
        P("fsdp", None, None),
        P("rep", "fsdp", None, None),
        P("rep", "fsdp", None, None),
        P("rep", "fsdp", None, None),
        P(None, "fsdp", None),
    )
    out_specs = (
        P("rep", "fsdp", None, None),
        P("rep", "fsdp", None, None),
        P("rep", "fsdp", None, None),
        P("fsdp", None, None),
        P("fsdp", None, None),
        P("fsdp", None, None),
    )
    return jax.shard_map(
        per_device, mesh=mesh, in_specs=in_specs, out_specs=out_specs, check_vma=False
    )
```

profile of v0, /device:TPU:16, one launch (start us, length us, event | category | flops | bytes accessed | tf_op | source)
XLA Modules:
  0.0 483.9 jit_solution(2721960659898264828)
XLA Ops:
  7.2 0.0 all-gather.7.cloned.1.call-start
  7.2 0.7 all-gather.7.cloned.1.call-update
  7.9 0.0 all-gather.9.cloned.1.call-start
  7.9 0.7 all-gather.9.cloned.1.call-update
  8.6 1.0 copy.59
  9.7 1.0 copy.60
  10.7 3.0 reshape_tile.3
  13.8 6.2 %all-to-all-start = ((bf16[128,16,4,2,128]{0,4,2,3,1:T(8,128)(2,1)}), bf16[128,16,4,2,128]{0,4,2,3,1:T(8,128)(2,1)}, u32[]{:S(2)}, u32[]{:S(2)}) async-start(bf16[128,16,4,2,128]{0,4,2,3,1:T(8,128)(2,1)} %reshape_tile.3), calls=%async_computation | async-start | bytes 8388608 | tf_op jit(solution)/shard_map/all_to_all | solution.py:95
  19.9 0.0 all-gather.5.cloned.1.call-start
  20.0 0.7 all-gather.5.cloned.1.call-update
  20.6 0.1 copy.46
  20.8 0.1 copy.41
  20.9 2.1 gather_fusion.2
  23.1 0.9 gather_fusion.1
  24.1 75.2 %all-gather.7.cloned.1.call-done = bf16[64,128,128]{2,1,0:T(8,128)(2,1)} async-done(((bf16[4,128,128]{2,1,0:T(8,128)(2,1)}), bf16[64,128,128]{2,1,0:T(8,128)(2,1)}) %all-gather.7.cloned.1.call-update) | async-done | bytes 2097168 | tf_op jit(solution)/shard_map/all_gather | solution.py:64
  99.2 4.1 copy.43
  103.3 44.4 %all-gather.9.cloned.1.call-done = bf16[64,128,128]{2,1,0:T(8,128)(2,1)} async-done(((bf16[4,128,128]{2,1,0:T(8,128)(2,1)}), bf16[64,128,128]{2,1,0:T(8,128)(2,1)}) %all-gather.9.cloned.1.call-update) | async-done | bytes 2097168 | tf_op jit(solution)/shard_map/all_gather | solution.py:65
  147.8 4.1 copy.44
  151.8 7.4 %fusion.6 = f32[128,64,256]{0,2,1:T(8,128)} fusion(bf16[64,128,128]{1,2,0:T(8,128)(2,1)} %copy.44, bf16[64,128,128]{1,2,0:T(8,128)(2,1)} %copy.43, bf16[64,128,128]{2,1,0:T(8,128)(2,1)} %gather_fusion.2, pred[64]{0:T(512)(128)(4,1)S(1)} %compare_and_fusion), kind=kOutput, calls=%fused_computation.11 | convolution fusion | flops 546308096 | bytes 14680128 | tf_op jit(solution)/shard_map/tic,ice->tie/dot_general | solution.py:75
  159.2 9.3 %copy.47 = f32[128,64,256]{2,1,0:T(8,128)} copy(f32[128,64,256]{0,2,1:T(8,128)} %fusion.6) | data formatting | bytes 16777216 | tf_op jit(solution)/shard_map/tic,ice->tie/transpose | solution.py:75
  168.5 21.6 %all-gather.5.cloned.1.call-done = bf16[64,128,128]{2,1,0:T(8,128)(2,1)} async-done(((bf16[4,128,128]{2,1,0:T(8,128)(2,1)}), bf16[64,128,128]{2,1,0:T(8,128)(2,1)}) %all-gather.5.cloned.1.call-update) | async-done | bytes 2097168 | tf_op jit(solution)/shard_map/all_gather | solution.py:66
  190.1 0.0 copy-start
  190.1 3.4 convolution_bitcast_fusion
  193.5 0.6 copy-done
  194.1 2.8 convolution_bitcast_fusion.1
  197.0 4.4 fusion.29
  201.3 0.2 pad_maximum_fusion
  201.5 0.4 copy.48
  201.9 0.0 all-to-all-done
  201.9 4.2 broadcast_in_dim.31
  206.2 0.0 copy-start.5
  206.2 6.8 %all-to-all-start.1 = ((bf16[128,16,4,3,128]{4,0,2,3,1:T(8,128)(2,1)}), bf16[128,16,4,3,128]{4,0,2,3,1:T(8,128)(2,1)}, u32[]{:S(2)}, u32[]{:S(2)}) async-start(bf16[128,16,4,3,128]{4,0,2,3,1:T(8,128)(2,1)} %broadcast_in_dim.31), calls=%async_computation.1 | async-start | bytes 12582912 | tf_op jit(solution)/shard_map/all_to_all | solution.py:96
  213.0 0.0 copy-done.5
  213.1 0.0 copy-done.6
  213.1 0.1 multiply_reduce_fusion
  213.2 0.0 copy-done.7
  213.2 0.1 and_reduce_fusion
  213.3 6.9 %copy.39 = bf16[16,128,1,4,2,128]{1,0,5,3,4,2:T(8,128)(2,1)} copy(bf16[16,128,1,4,2,128]{1,5,3,4,0,2:T(8,128)(2,1)} %bitcast.3) | data formatting | bytes 8388608 | tf_op jit(solution)/shard_map/all_to_all | solution.py:95
  220.2 7.3 %squeeze.31 = bf16[2048,4,2,128]{0,3,1,2:T(8,128)(2,1)} reshape(bf16[16,128,1,4,2,128]{1,0,5,3,4,2:T(8,128)(2,1)} %copy.39) | data formatting | bytes 8388608 | tf_op jit(solution)/shard_map/squeeze | solution.py:98
  227.5 123.1 %all-to-all-done.1 = bf16[128,16,4,3,128]{4,0,2,3,1:T(8,128)(2,1)} async-done(((bf16[128,16,4,3,128]{4,0,2,3,1:T(8,128)(2,1)}), bf16[128,16,4,3,128]{4,0,2,3,1:T(8,128)(2,1)}, u32[]{:S(2)}, u32[]{:S(2)}) %all-to-all-start.1) | async-done | bytes 6291488 | tf_op jit(solution)/shard_map/all_to_all | solution.py:96
  350.6 4.3 copy.49
  354.9 0.0 copy-done.1
  354.9 0.7 fusion.21
  355.6 0.7 fusion.22
  356.3 0.0 copy-start.2
  356.3 0.0 copy-start.3
  356.4 0.0 copy-start.4
  356.4 0.9 fusion.23
  357.2 0.0 copy-done.2
  357.3 0.1 copy-done.3
  357.4 0.1 copy-done.4
  357.5 1.1 convolution_bitcast_fusion.4
  358.5 1.0 fusion.38
  359.5 0.3 reshape.77
  359.9 60.2 %gather_fusion = f32[6144]{0:T(1024)S(1)} fusion(f32[3,4,16384]{2,1,0:T(4,128)S(1)} %reshape.77, s32[6144]{0:T(1024)S(1)} %bitcast.133), kind=kCustom, calls=%fused_computation.2 | custom fusion | bytes 122880 | tf_op jit(solution)/shard_map/jit(take_along_axis)/gather | solution.py:40
  420.1 4.5 all-gather
  424.7 23.5 %scatter_custom_fusion.1 = f32[196608]{0:T(1024)S(1)} fusion(s32[6144]{0:T(1024)S(1)} %bitcast.146, f32[6144]{0:T(1024)S(1)} %bitcast.149, f32[]{:T(128)} %constant.75.clone.1), kind=kCustom, calls=%fused_computation.48 | custom fusion | bytes 786436
  448.1 1.1 convolution_bitcast_fusion.2
  449.2 1.0 fusion.35
  450.2 0.9 slice_bitcast_fusion.23
  451.1 23.2 %scatter_custom_fusion = f32[196608]{0:T(1024)S(1)} fusion(s32[6144]{0:T(1024)S(1)} %bitcast.147, f32[6144]{0:T(1024)S(1)} %bitcast.148, f32[]{:T(128)} %constant.75.clone.1), kind=kCustom, calls=%fused_computation.50 | custom fusion | bytes 786436
  474.3 1.1 convolution_bitcast_fusion.3
  475.4 1.0 convolution_subtract_fusion
  476.4 0.9 fusion.76
  (21 shorter events, 0.2 us)
Async XLA Ops:
  7.2 92.1 %all-gather.7.cloned.1.call-start = ((), (), s32[]{:S(2)}) async-start(), calls=%async_computation.3 | async-start | bytes 2228224 | tf_op jit(solution)/shard_map/all_gather | solution.py:64
  7.9 139.9 %all-gather.9.cloned.1.call-start = ((), (), s32[]{:S(2)}) async-start(), calls=%async_computation.4 | async-start | bytes 2228224 | tf_op jit(solution)/shard_map/all_gather | solution.py:65
  13.8 188.2 %all-to-all-start = ((bf16[128,16,4,2,128]{0,4,2,3,1:T(8,128)(2,1)}), bf16[128,16,4,2,128]{0,4,2,3,1:T(8,128)(2,1)}, u32[]{:S(2)}, u32[]{:S(2)}) async-start(bf16[128,16,4,2,128]{0,4,2,3,1:T(8,128)(2,1)} %reshape_tile.3), calls=%async_computation | async-start | bytes 8388608 | tf_op jit(solution)/shard_map/all_to_all | solution.py:95
  19.9 170.2 %all-gather.5.cloned.1.call-start = ((), (), s32[]{:S(2)}) async-start(), calls=%async_computation.2 | async-start | bytes 2228224 | tf_op jit(solution)/shard_map/all_gather | solution.py:66
  190.1 4.0 copy-start
  206.2 6.8 %copy-start.5 = (s32[3,4,512]{2,1,0:T(4,128)S(1)}, s32[3,4,512]{2,1,0:T(4,128)}, u32[]{:S(2)}) copy-start(s32[3,4,512]{2,1,0:T(4,128)} %param.19) | copy-start | bytes 73732
  206.2 6.9 %copy-start.6 = (s32[3]{0:T(128)S(1)}, s32[3]{0:T(128)}, u32[]{:S(2)}) copy-start(s32[3]{0:T(128)} %constant.93) | copy-start | bytes 40
  206.2 7.0 %copy-start.7 = (s32[3]{0:T(128)S(1)}, s32[3]{0:T(128)}, u32[]{:S(2)}) copy-start(s32[3]{0:T(128)} %constant.96) | copy-start | bytes 40
  206.2 144.4 %all-to-all-start.1 = ((bf16[128,16,4,3,128]{4,0,2,3,1:T(8,128)(2,1)}), bf16[128,16,4,3,128]{4,0,2,3,1:T(8,128)(2,1)}, u32[]{:S(2)}, u32[]{:S(2)}) async-start(bf16[128,16,4,3,128]{4,0,2,3,1:T(8,128)(2,1)} %broadcast_in_dim.31), calls=%async_computation.1 | async-start | bytes 12582912 | tf_op jit(solution)/shard_map/all_to_all | solution.py:96
  350.6 4.3 copy-start.1
  356.3 1.0 copy-start.2
  356.3 1.0 copy-start.3
  356.4 1.1 copy-start.4
Sparse Core Ops, SparseCore 0:
  10.2 89.0 all-gather.6
  101.4 46.3 all-gather.8
  149.9 40.1 all-gather.4
where the time goes:
time: 485 us; the launch traced here: 484 us
  waiting for transfers between devices  266 us (55%)
  local copies, waits for them, and re-layouts  159 us (33%)
  matrix products  26.5 us (5%)
  between operations  14.1 us (3%)
  starting transfers between devices  13.1 us (3%)
    all_to_all x1, waiting for transfers between devices, per_device(): lax.all_to_all(act_send, 'fsdp', split_axis=1, concat_axis=0, tiled=True)  123 us
    all_gather x1, waiting for transfers between devices, per_device(): lax.all_gather(gate_weight, 'fsdp', axis=0, tiled=True)  75.2 us
    gather x2, local copies, waits for them, and re-layouts, band_split(): picked = jnp.take_along_axis(flattened, band_index, axis=2)  60.2 us
    unnamed x22, local copies, waits for them, and re-layouts  47.6 us
    all_gather x1, waiting for transfers between devices, per_device(): lax.all_gather(up_weight, 'fsdp', axis=0, tiled=True)  44.4 us
    all_gather x1, waiting for transfers between devices, per_device(): lax.all_gather(down_weight, 'fsdp', axis=0, tiled=True)  21.6 us
  transfers between devices with their start and end apart: 5, of which 4 were waited for; matrix products, arithmetic and copies ran while one was open for 12% of the time, Pallas kernels for 0%

commit v1 on v0

v1 whole, which is shorter than its diff:
```python
import functools

import jax
import jax.numpy as jnp
import numpy as np
from jax import lax
from jax.experimental import pallas as pl
from jax.experimental.pallas import tpu as pltpu
from jax.sharding import PartitionSpec as P

MOMENTUM_DECAY = 0.999
LATE_FLOPS = 4 * 10**9
TABLES_FLOPS = 10**9
F32 = jnp.float32
BF16 = jnp.bfloat16


def dct_table(side):
    k = np.arange(side, dtype=np.float64)[:, None]
    n = np.arange(side, dtype=np.float64)[None, :]
    scale = np.where(k == 0, np.sqrt(1.0 / side), np.sqrt(2.0 / side))
    return (scale * np.cos(np.pi * (2.0 * n + 1.0) * k / (2.0 * side))).astype(np.float32)


def split2(value):
    hi = value.astype(BF16)
    return hi, (value - hi.astype(F32)).astype(BF16)


def dot(a, b):
    return jnp.dot(a, b, preferred_element_type=F32)


def dot_nt(a, b):
    return lax.dot_general(a, b, (((1,), (1,)), ((), ())), preferred_element_type=F32)


def dot3(a, b):
    a_hi, a_lo = split2(a)
    b_hi, b_lo = split2(b)
    left = jnp.concatenate([a_hi, a_hi, a_lo], axis=1)
    return dot(left, jnp.concatenate([b_hi, b_lo, b_hi], axis=0))


def lanes_to_rows(value, side):
    count = value.shape[1] // side
    return jnp.concatenate([value[:, i * side : (i + 1) * side] for i in range(count)], axis=0)


def decode(values, in_row_ref, cells_ref, cosines_t):
    side = cosines_t.shape[0]
    inner = []
    for b, row in enumerate(values):
        hi, lo = split2(row)
        in_row = in_row_ref[b]
        both = dot(jnp.concatenate([in_row * hi, in_row * lo], axis=0), cells_ref[b])
        inner.append(both[:side, :side] + (both[:side, side:] + both[side:, :side]))
    return dot3(cosines_t, jnp.concatenate(inner, axis=1))


def activations(wgu, wd, x, d):
    pre = dot_nt(wgu, x)
    dh = dot_nt(wd, d)
    gate, up = pre[: wd.shape[0]], pre[wd.shape[0] :]
    sig = 1.0 / (1.0 + jnp.exp(-gate))
    swish = gate * sig
    d_gate = (dh * up * sig * (1.0 + gate * (1.0 - sig))).astype(BF16)
    return d_gate, (dh * swish).astype(BF16), (swish * up).astype(BF16)


def tables_kernel(index_ref, cosines_ref, in_row_ref, in_col_ref, cells_ref):
    side = cosines_ref.shape[0]
    parts = jnp.concatenate(split2(cosines_ref[...]), axis=1)
    shift = int(np.log2(side))
    matrices, count, keep = index_ref.shape
    lines = lax.broadcasted_iota(jnp.int32, (side, keep), 0)
    for m in range(matrices):
        for i in range(count):
            b = m * count + i
            index = index_ref[m, i : i + 1, :]
            in_col = jnp.where((index & (side - 1)) == lines, 1.0, 0.0).astype(BF16)
            in_row_ref[b] = jnp.where((index >> shift) == lines, 1.0, 0.0).astype(BF16)
            in_col_ref[b] = in_col
            cells_ref[b] = dot(in_col.T, parts).astype(BF16)


def early_kernel(shards, *refs):
    xs, ds, weights = refs[:shards], refs[shards : 2 * shards], refs[2 * shards : 2 * shards + 2]
    own_ref, par_ref, wgu_ref, wd_ref, x_all, d_all, act = refs[2 * shards + 2 :]
    rows = xs[0].shape[0]
    side = own_ref.shape[1]
    count = weights[0].shape[0] // 3
    for i in range(count):
        cols = slice(i * side, (i + 1) * side)
        for p in range(2):
            gate, up, down = (weights[p][m * count + i] for m in range(3))
            wgu_ref[p * side : (p + 1) * side, cols] = gate.T
            wgu_ref[(2 + p) * side : (3 + p) * side, cols] = up.T
            wd_ref[p * side : (p + 1) * side, cols] = down
    wgu, wd = wgu_ref[...], wd_ref[...]
    for s in range(0, shards, 2):
        some = range(s, min(s + 2, shards))
        x = jnp.concatenate([xs[j][...] for j in some], axis=0)
        d = jnp.concatenate([ds[j][...] for j in some], axis=0)
        span = pl.ds(s * rows, len(some) * rows)
        x_all[span, :] = x
        d_all[span, :] = d
        d_gate, d_up, hidden = activations(wgu, wd, x, d)
        act[: 2 * side, span] = d_gate
        act[2 * side : 4 * side, span] = d_up
        act[4 * side :, span] = hidden
    g_in = dot(act[: 4 * side, :], x_all[...])
    g_out = dot(act[4 * side :, :], d_all[...])
    for m, grad in enumerate((g_in[: 2 * side], g_in[2 * side :], g_out)):
        own_ref[m] = grad[:side]
        par_ref[m] = grad[side:]


def moment_step(
    grads, mom_refs, in_row_ref, in_col_ref, cosines_ref, cosines_t_ref, moment_ref, band_ref
):
    side = cosines_ref.shape[0]
    count = mom_refs[0].shape[0]
    blocks = []
    for m in range(3):
        for i in range(count):
            piece = grads[m][:, i * side : (i + 1) * side]
            if m < 2:
                piece = piece.T
            block = MOMENTUM_DECAY * mom_refs[m][i] + piece
            moment_ref[m * count + i] = block
            blocks.append(block)
    inner = dot3(cosines_ref[...], jnp.concatenate(blocks, axis=1))
    coeffs = dot3(lanes_to_rows(inner, side), cosines_t_ref[...])
    for m in range(3):
        for i in range(count):
            b = m * count + i
            hi, lo = split2(coeffs[b * side : (b + 1) * side])
            in_col = in_col_ref[b]
            at_col = dot(jnp.concatenate([hi, lo], axis=1), jnp.concatenate([in_col, in_col], axis=0))
            band_ref[m, i : i + 1, :] = jnp.sum(
                at_col * in_row_ref[b].astype(F32), axis=0, keepdims=True
            )


def late_kernel(x_ref, d_ref, wgu_ref, wd_ref, own_ref, par_ref):
    side = own_ref.shape[1]
    x, d = x_ref[...], d_ref[...]
    d_gate, d_up, hidden = activations(wgu_ref[...], wd_ref[...], x, d)
    for m, grad in enumerate((dot(d_gate, x), dot(d_up, x), dot(hidden, d))):
        own_ref[m] = grad[:side]
        par_ref[m] = grad[side:].astype(BF16)


def moment_kernel(terms, *refs):
    grads = [sum(ref[m].astype(F32) for ref in refs[:terms]) for m in range(3)]
    moment_step(grads, refs[terms : terms + 3], *refs[terms + 3 :])


def residual_kernel(moment_ref, band_ref, in_row_ref, cells_ref, cosines_t_ref, *outs):
    side = cosines_t_ref.shape[0]
    count = outs[0].shape[0]
    pairs = [(m, i) for m in range(3) for i in range(count)]
    values = [band_ref[m, i : i + 1, :] for m, i in pairs]
    decoded = decode(values, in_row_ref, cells_ref, cosines_t_ref[...])
    for b, (m, i) in enumerate(pairs):
        kept = decoded[:, b * side : (b + 1) * side]
        outs[3][b] = kept
        outs[m][i] = moment_ref[b] - kept


def update_kernel(kept_ref, other_ref, in_row_ref, cells_ref, cosines_t_ref, *outs):
    side = cosines_t_ref.shape[0]
    count = outs[0].shape[0]
    pairs = [(m, i) for m in range(3) for i in range(count)]
    values = [
        sum(other_ref[g, m, i : i + 1, :] for g in range(other_ref.shape[0])) for m, i in pairs
    ]
    decoded = decode(values, in_row_ref, cells_ref, cosines_t_ref[...])
    for b, (m, i) in enumerate(pairs):
        outs[m][i] = kept_ref[b] + decoded[:, b * side : (b + 1) * side]


def call(kernel, out_shape, flops, *args, scratch=(), in_place={}):
    moved = sum(a.size * a.dtype.itemsize for a in args)
    specs = [
        pl.BlockSpec(memory_space=in_place.get(k, pltpu.VMEM)) for k in range(len(args))
    ]
    return pl.pallas_call(
        kernel,
        out_shape=out_shape,
        in_specs=specs,
        scratch_shapes=list(scratch),
        compiler_params=pltpu.CompilerParams(vmem_limit_bytes=24 * 1024 * 1024),
        cost_estimate=pl.CostEstimate(flops=flops, bytes_accessed=2 * moved, transcendentals=0),
    )(*args)


def ring_perms(count):
    chips = count // 2
    order = list(range(0, chips, 2)) + list(range(1, chips, 2))[::-1]
    forward = [
        (2 * order[p] + c, 2 * order[(p + 1) % chips] + c) for p in range(chips) for c in range(2)
    ]
    return forward, [(b, a) for a, b in forward], chips


def band_tables(band_index, cosines):
    blocks, keep, side = band_index.shape[0] * band_index.shape[1], band_index.shape[2], cosines.shape[0]
    return call(
        tables_kernel,
        (
            jax.ShapeDtypeStruct((blocks, side, keep), BF16),
            jax.ShapeDtypeStruct((blocks, side, keep), BF16),
            jax.ShapeDtypeStruct((blocks, keep, 2 * side), BF16),
        ),
        TABLES_FLOPS,
        band_index,
        cosines,
    )


def column_moments(x, d, weights, momenta, tables, cosines, cosines_t, shapes):
    side = weights[0].shape[1]
    rows, width = x.shape
    count = lax.axis_size("fsdp")
    swap = [(f, f ^ 1) for f in range(count)]
    forward, back, chips = ring_perms(count)

    def send(value, perm):
        return lax.ppermute(value, "fsdp", perm)

    xf, db, df, xb = send(x, forward), send(d, back), send(d, forward), send(x, back)
    xs, ds = [x, xf, xb], [d, df, db]
    own_weights = jnp.concatenate(weights, axis=0)
    partner_weights = send(own_weights, swap)
    in_row, in_col, cells = tables
    for hop in range(2, chips // 2):
        if hop == 3:
            db, in_col = lax.optimization_barrier((db, in_col))
        xf, db, df, xb = send(xf, forward), send(db, back), send(df, forward), send(xb, back)
        xs += [xf, xb]
        ds += [df, db]
    x_last, d_last = send(xf, forward), send(db, back)

    early = len(xs)
    tokens = early * rows
    part = jax.ShapeDtypeStruct((3, side, width), F32)
    own, partner, wgu, wd = call(
        functools.partial(early_kernel, early),
        (
            part,
            part,
            jax.ShapeDtypeStruct((4 * side, width), BF16),
            jax.ShapeDtypeStruct((2 * side, width), BF16),
        ),
        24 * tokens * width * side,
        *xs,
        *ds,
        own_weights,
        partner_weights,
        scratch=(
            pltpu.VMEM((tokens, width), BF16),
            pltpu.VMEM((tokens, width), BF16),
            pltpu.VMEM((6 * side, tokens), BF16),
        ),
    )
    own_late, partner_late = call(
        late_kernel,
        (part, jax.ShapeDtypeStruct(part.shape, BF16)),
        LATE_FLOPS,
        x_last,
        d_last,
        wgu,
        wd,
    )
    return call(
        functools.partial(moment_kernel, 4),
        shapes,
        10**9,
        own,
        send(partner, swap),
        own_late,
        send(partner_late, swap),
        *momenta,
        in_row,
        in_col,
        cosines,
        cosines_t,
    )


def shared_column_moments(x, d, weights, momenta, tables, cosines, cosines_t, shapes):
    gate_weight, up_weight, down_weight = weights
    own = shared_column_grads(x, d, gate_weight, up_weight, down_weight)
    return call(
        functools.partial(moment_kernel, 1), shapes, 0, own, *momenta, *tables[:2], cosines, cosines_t
    )


def shared_column_grads(x, d, gate_weight, up_weight, down_weight):
    side = gate_weight.shape[1]
    width = x.shape[1]
    blk_dev = gate_weight.shape[0]
    count = lax.axis_size("fsdp")
    share = width // side // blk_dev
    groups = [list(range(g * share, (g + 1) * share)) for g in range(count // share)]

    def whole(w):
        return lax.all_gather(w, "fsdp", axis=0, tiled=True, axis_index_groups=groups)

    gate, up = whole(gate_weight).reshape(width, side), whole(up_weight).reshape(width, side)
    down = whole(down_weight).transpose(1, 0, 2).reshape(side, width)
    x_all = lax.all_gather(x, "fsdp", axis=0, tiled=True)
    d_all = lax.all_gather(d, "fsdp", axis=0, tiled=True)
    gate_pre = jnp.dot(x_all, gate, preferred_element_type=F32)
    up_pre = jnp.dot(x_all, up, preferred_element_type=F32)
    d_hidden = jnp.dot(d_all, down.T, preferred_element_type=F32)
    sig = jax.nn.sigmoid(gate_pre)
    hidden = (gate_pre * sig * up_pre).astype(BF16)
    d_gate = (d_hidden * up_pre * sig * (1.0 + gate_pre * (1.0 - sig))).astype(BF16)
    d_up = (d_hidden * gate_pre * sig).astype(BF16)
    start = lax.rem(lax.axis_index("fsdp"), share) * blk_dev * side
    x_own = lax.dynamic_slice_in_dim(x_all, start, blk_dev * side, axis=1)
    d_own = lax.dynamic_slice_in_dim(d_all, start, blk_dev * side, axis=1)
    own = jnp.stack(
        [
            jnp.dot(d_gate.T, x_own, preferred_element_type=F32),
            jnp.dot(d_up.T, x_own, preferred_element_type=F32),
            jnp.dot(hidden.T, d_own, preferred_element_type=F32),
        ]
    )
    return own


def per_device(
    x_in, d_out, gate_weight, up_weight, down_weight, mom_gate, mom_up, mom_down, band_index
):
    side = gate_weight.shape[1]
    blk_dev = gate_weight.shape[0]
    row_blocks = x_in.shape[2] // side
    if blk_dev == row_blocks and lax.axis_size("fsdp") % 4 == 0:
        step = column_moments
    else:
        step = shared_column_moments
    cosines, cosines_t = jnp.asarray(dct_table(side)), jnp.asarray(dct_table(side).T)
    blocks = 3 * blk_dev
    dense = jax.ShapeDtypeStruct((blocks, side, side), F32)
    in_row, in_col, cells = band_tables(band_index, cosines)
    moment, band = step(
        x_in[0],
        d_out[0],
        (gate_weight, up_weight, down_weight),
        (mom_gate[0], mom_up[0], mom_down[0]),
        (in_row, in_col, cells),
        cosines,
        cosines_t,
        (dense, jax.ShapeDtypeStruct(band_index.shape, F32)),
    )
    reps = lax.axis_size("rep")
    other = jnp.stack(
        [
            lax.ppermute(band, "rep", [(r, (r + s) % reps) for r in range(reps)])
            for s in range(1, reps)
        ]
    )
    result = jax.ShapeDtypeStruct((blk_dev, side, side), F32)
    flops = 4 * 3 * blocks * side**3
    *residuals, kept = call(
        residual_kernel, (result,) * 3 + (dense,), flops, moment, band, in_row, cells, cosines_t
    )
    updates = call(
        update_kernel, (result,) * 3, flops, kept, other, in_row, cells, cosines_t
    )
    return (*(r[None] for r in residuals), *updates)


def solution(mesh):
    in_specs = (
        P("rep", "fsdp", None),
        P("rep", "fsdp", None),
        P("fsdp", None, None),
        P("fsdp", None, None),
        P("fsdp", None, None),
        P("rep", "fsdp", None, None),
        P("rep", "fsdp", None, None),
        P("rep", "fsdp", None, None),
        P(None, "fsdp", None),
    )
    out_specs = (
        P("rep", "fsdp", None, None),
        P("rep", "fsdp", None, None),
        P("rep", "fsdp", None, None),
        P("fsdp", None, None),
        P("fsdp", None, None),
        P("fsdp", None, None),
    )
    return jax.shard_map(
        per_device, mesh=mesh, in_specs=in_specs, out_specs=out_specs, check_vma=False
    )
```

time: 485 us -> 40 us (0.08)
  the two profiles are of different devices: /device:TPU:16 before, /device:TPU:0 now
where the time goes in v1:
time: 40 us; the launch traced here: 39.7 us
  starting transfers between devices  17.5 us (44%)
  Pallas kernels  9.28 us (23%)
  waiting for transfers between devices  7.75 us (19%)
  local copies, waits for them, and re-layouts  4.41 us (11%)
  between operations  0.8 us (2%)
    ppermute x17, starting transfers between devices, send(): return lax.ppermute(value, 'fsdp', perm)  15.9 us
    pallas_call x6, Pallas kernels, call(): pl.pallas_call(kernel, out_shape=out_shape, in_specs=specs, scratch_shape...  9.28 us
    ppermute x17, waiting for transfers between devices, send(): return lax.ppermute(value, 'fsdp', perm)  7.44 us
    unnamed x20, local copies, waits for them, and re-layouts  3.45 us
    ppermute x1, starting transfers between devices, per_device(): lax.ppermute(band, 'rep', [(r, (r + s) % reps) for r in range(reps)])  1.59 us
    concatenate x1, local copies, waits for them, and re-layouts, column_moments(): own_weights = jnp.concatenate(weights, axis=0)  0.97 us
  transfers between devices with their start and end apart: 18, of which 6 were waited for; matrix products, arithmetic and copies ran while one was open for 7% of the time, Pallas kernels for 15%

profile of v1, /device:TPU:0, one launch (start us, length us, event | category | flops | bytes accessed | tf_op | source)
XLA Modules:
  0.0 39.7 jit_solution(16332109520722355835)
XLA Ops:
  0.6 3.0 %collective-permute-start.7 = (bf16[128,512]{1,0:T(8,128)(2,1)}, bf16[128,512]{1,0:T(8,128)(2,1)S(1)}, u32[]{:S(2)}, u32[]{:S(2)}) collective-permute-start(bf16[128,512]{1,0:T(8,128)(2,1)} %bitcast.16), channel_id=1, source_target_pairs={{4,0},{5,1},{8,4},{9,5},{12,8},{13,9},{14,12},{15,13},{10,14},{11,... | collective-permute-start | bytes 393224 | tf_op jit(solution)/shard_map/ppermute | solution.py:231
  3.6 0.2 collective-permute-start.6
  3.8 2.0 %collective-permute-start = (bf16[128,512]{1,0:T(8,128)(2,1)}, bf16[128,512]{1,0:T(8,128)(2,1)S(1)}, u32[]{:S(2)}, u32[]{:S(2)}) collective-permute-start(bf16[128,512]{1,0:T(8,128)(2,1)} %bitcast.13), channel_id=1, source_target_pairs={{0,4},{1,5},{4,8},{5,9},{8,12},{9,13},{12,14},{13,15},{14,10},{15,... | collective-permute-start | bytes 393224 | tf_op jit(solution)/shard_map/ppermute | solution.py:231
  5.7 0.1 collective-permute-start.1
  5.8 0.9 %constant_dynamic-update-slice_fusion.2 = bf16[12,128,128]{2,1,0:T(8,128)(2,1)S(1)} fusion(bf16[4,128,128]{2,1,0:T(8,128)(2,1)} %param.13), kind=kLoop, calls=%fused_computation.2 | loop fusion | bytes 262144
  6.7 0.9 %constant_dynamic-update-slice_fusion.1 = bf16[12,128,128]{2,1,0:T(8,128)(2,1)S(1)} fusion(bf16[12,128,128]{2,1,0:T(8,128)(2,1)S(1)} %constant_dynamic-update-slice_fusion.2, bf16[4,128,128]{2,1,0:T(8,128)(2,1)} %param.14), kind=kLoop, calls=%fused_computation.1 | loop fusion | bytes 262144
  7.6 0.0 copy-start.6
  7.7 0.0 copy-start.7
  7.7 1.0 %constant_dynamic-update-slice_fusion.refs_14_ = bf16[12,128,128]{2,1,0:T(8,128)(2,1)S(1)} fusion(bf16[12,128,128]{2,1,0:T(8,128)(2,1)S(1)} %constant_dynamic-update-slice_fusion.1, bf16[4,128,128]{2,1,0:T(8,128)(2,1)} %param.15), kind=kLoop, calls=%fused_computation | loop fusion | bytes 262144 | tf_op jit(solution)/shard_map/concatenate | solution.py:235
  8.6 0.1 collective-permute-start.12
  8.7 0.0 collective-permute-done.7.refs_9_
  8.7 1.9 %collective-permute-start.9 = (bf16[128,512]{1,0:T(8,128)(2,1)S(1)}, bf16[128,512]{1,0:T(8,128)(2,1)S(1)}, u32[]{:S(2)}, u32[]{:S(2)}) collective-permute-start(bf16[128,512]{1,0:T(8,128)(2,1)S(1)} %collective-permute-done.7.refs_9_), channel_id=1, source_target_pairs={{4,0},{5,1},{8,4},{9,5},{12,8},{13,9},{14,12},{15,13},{10,14},{11,... | collective-permute-start | bytes 393224 | tf_op jit(solution)/shard_map/ppermute | solution.py:231
  10.7 0.9 %collective-permute-done.refs_1_ = bf16[128,512]{1,0:T(8,128)(2,1)S(1)} collective-permute-done((bf16[128,512]{1,0:T(8,128)(2,1)}, bf16[128,512]{1,0:T(8,128)(2,1)S(1)}, u32[]{:S(2)}, u32[]{:S(2)}) %collective-permute-start) | collective-permute-done | bytes 131104 | tf_op jit(solution)/shard_map/ppermute | solution.py:231
  11.6 0.4 %collective-permute-start.2 = (bf16[128,512]{1,0:T(8,128)(2,1)S(1)}, bf16[128,512]{1,0:T(8,128)(2,1)S(1)}, u32[]{:S(2)}, u32[]{:S(2)}) collective-permute-start(bf16[128,512]{1,0:T(8,128)(2,1)S(1)} %collective-permute-done.refs_1_), channel_id=1, source_target_pairs={{0,4},{1,5},{4,8},{5,9},{8,12},{9,13},{12,14},{13,15},{14,10},{15,... | collective-permute-start | bytes 393224 | tf_op jit(solution)/shard_map/ppermute | solution.py:231
  12.0 0.0 collective-permute-done.6.refs_8_
  12.0 1.7 %collective-permute-start.8 = (bf16[128,512]{1,0:T(8,128)(2,1)S(1)}, bf16[128,512]{1,0:T(8,128)(2,1)S(1)}, u32[]{:S(2)}, u32[]{:S(2)}) collective-permute-start(bf16[128,512]{1,0:T(8,128)(2,1)S(1)} %collective-permute-done.6.refs_8_), channel_id=1, source_target_pairs={{0,4},{1,5},{4,8},{5,9},{8,12},{9,13},{12,14},{13,15},{14,10},{15,... | collective-permute-start | bytes 393224 | tf_op jit(solution)/shard_map/ppermute | solution.py:231
  13.7 0.0 collective-permute-done.1.refs_2_
  13.7 0.3 collective-permute-start.3
  14.1 0.0 copy-start.4
  14.1 0.8 %copy-done.4 = f32[128,128]{1,0:T(8,128)S(1)} copy-done((f32[128,128]{1,0:T(8,128)S(1)}, f32[128,128]{1,0:T(8,128)}, u32[]{:S(2)}) %copy-start.4) | copy-done | bytes 65560
  14.9 0.0 copy-start.8
  14.9 0.7 %copy-done.8 = s32[3,4,512]{2,1,0:T(4,128)S(1)} copy-done((s32[3,4,512]{2,1,0:T(4,128)S(1)}, s32[3,4,512]{2,1,0:T(4,128)}, u32[]{:S(2)}) %copy-start.8) | copy-done | bytes 24600
  15.6 1.4 %shard_map.154 = (bf16[12,128,512]{2,1,0:T(8,128)(2,1)S(1)}, bf16[12,128,512]{2,1,0:T(8,128)(2,1)S(1)}, bf16[12,512,256]{2,1,0:T(8,128)(2,1)S(1)}) custom-call(s32[3,4,512]{2,1,0:T(4,128)S(1)} %copy-done.8, f32[128,128]{1,0:T(8,128)S(1)} %copy-done.4), custom_call_target="tpu_custom_call" | custom-call | flops 1000000000 | bytes 180224 | tf_op jit(solution)/shard_map/pallas_call | solution.py:189
  17.0 0.0 collective-permute-done.9.refs_11_
  17.0 1.6 %collective-permute-start.11 = (bf16[128,512]{1,0:T(8,128)(2,1)S(1)}, bf16[128,512]{1,0:T(8,128)(2,1)S(1)}, u32[]{:S(2)}, u32[]{:S(2)}) collective-permute-start(bf16[128,512]{1,0:T(8,128)(2,1)S(1)} %collective-permute-done.9.refs_11_), channel_id=1, source_target_pairs={{4,0},{5,1},{8,4},{9,5},{12,8},{13,9},{14,12},{15,13},{10,14},{11,... | collective-permute-start | bytes 393224 | tf_op jit(solution)/shard_map/ppermute | solution.py:231
  18.7 0.0 collective-permute-done.2.refs_3_
  18.7 0.4 %collective-permute-start.4 = (bf16[128,512]{1,0:T(8,128)(2,1)S(1)}, bf16[128,512]{1,0:T(8,128)(2,1)S(1)}, u32[]{:S(2)}, u32[]{:S(2)}) collective-permute-start(bf16[128,512]{1,0:T(8,128)(2,1)S(1)} %collective-permute-done.2.refs_3_), channel_id=1, source_target_pairs={{0,4},{1,5},{4,8},{5,9},{8,12},{9,13},{12,14},{13,15},{14,10},{15,... | collective-permute-start | bytes 393224 | tf_op jit(solution)/shard_map/ppermute | solution.py:231
  19.1 0.0 collective-permute-done.8.refs_10_
  19.1 1.7 %collective-permute-start.10 = (bf16[128,512]{1,0:T(8,128)(2,1)S(1)}, bf16[128,512]{1,0:T(8,128)(2,1)S(1)}, u32[]{:S(2)}, u32[]{:S(2)}) collective-permute-start(bf16[128,512]{1,0:T(8,128)(2,1)S(1)} %collective-permute-done.8.refs_10_), channel_id=1, source_target_pairs={{0,4},{1,5},{4,8},{5,9},{8,12},{9,13},{12,14},{13,15},{14,10},{15,... | collective-permute-start | bytes 393224 | tf_op jit(solution)/shard_map/ppermute | solution.py:231
  20.8 0.0 collective-permute-done.3.refs_4_
  20.8 0.3 collective-permute-start.5
  21.1 2.0 %collective-permute-done.11.refs_13_ = bf16[128,512]{1,0:T(8,128)(2,1)S(1)} collective-permute-done((bf16[128,512]{1,0:T(8,128)(2,1)S(1)}, bf16[128,512]{1,0:T(8,128)(2,1)S(1)}, u32[]{:S(2)}, u32[]{:S(2)}) %collective-permute-start.11) | collective-permute-done | bytes 131104 | tf_op jit(solution)/shard_map/ppermute | solution.py:231
  23.2 1.8 %collective-permute-start.15 = (bf16[128,512]{1,0:T(8,128)(2,1)S(1)}, bf16[128,512]{1,0:T(8,128)(2,1)S(1)}, u32[]{:S(2)}, u32[]{:S(2)}) collective-permute-start(bf16[128,512]{1,0:T(8,128)(2,1)S(1)} %collective-permute-done.11.refs_13_), channel_id=1, source_target_pairs={{4,0},{5,1},{8,4},{9,5},{12,8},{13,9},{14,12},{15,13},{10,14},{11,... | collective-permute-start | bytes 393224 | tf_op jit(solution)/shard_map/ppermute | solution.py:231
  25.0 0.0 collective-permute-done.4.refs_5_
  25.0 0.2 collective-permute-start.14
  25.2 1.3 %collective-permute-done.10.refs_12_ = bf16[128,512]{1,0:T(8,128)(2,1)S(1)} collective-permute-done((bf16[128,512]{1,0:T(8,128)(2,1)S(1)}, bf16[128,512]{1,0:T(8,128)(2,1)S(1)}, u32[]{:S(2)}, u32[]{:S(2)}) %collective-permute-start.10) | collective-permute-done | bytes 131104 | tf_op jit(solution)/shard_map/ppermute | solution.py:231
  26.4 0.0 collective-permute-done.5.refs_6_
  26.4 0.0 collective-permute-done.12.refs_15_
  26.5 0.0 copy-done.6
  26.5 0.0 copy-done.7
  26.5 1.9 %shard_map.155 = (f32[3,128,512]{2,1,0:T(8,128)S(1)}, f32[3,128,512]{2,1,0:T(8,128)S(1)}, bf16[512,512]{1,0:T(8,128)(2,1)S(1)}, bf16[256,512]{1,0:T(8,128)(2,1)S(1)}) custom-call(bf16[128,512]{1,0:T(8,128)(2,1)S(1)} %bitcast.15, bf16[128,512]{1,0:T(8,128)(2,1)S(1)} %collective-permute-done.refs_1_, bf16[128,512]{1,0:T(8,128)(2,1)S(1)} %collective-permute-done.1.refs_2_, ...), custom_call_target="tpu_custom_call" | custom-call | flops 1409286144 | bytes 5242880 | tf_op jit(solution)/shard_map/pallas_call | solution.py:189
  28.4 0.1 collective-permute-start.13
  28.4 0.0 collective-permute-done.15.d_ref
  28.5 1.5 %collective-permute-done.14.x_ref = bf16[128,512]{1,0:T(8,128)(2,1)S(1)} collective-permute-done((bf16[128,512]{1,0:T(8,128)(2,1)S(1)}, bf16[128,512]{1,0:T(8,128)(2,1)S(1)}, u32[]{:S(2)}, u32[]{:S(2)}) %collective-permute-start.14) | collective-permute-done | bytes 131104 | tf_op jit(solution)/shard_map/ppermute | solution.py:231
  29.9 0.0 copy-start
  29.9 0.0 copy-start.1
  29.9 0.0 copy-start.2
  29.9 0.0 copy-start.3
  29.9 0.0 copy-start.5
  30.0 0.8 %shard_map.156 = (f32[3,128,512]{2,1,0:T(8,128)S(1)}, bf16[3,128,512]{2,1,0:T(8,128)(2,1)S(1)}) custom-call(bf16[128,512]{1,0:T(8,128)(2,1)S(1)} %collective-permute-done.14.x_ref, bf16[128,512]{1,0:T(8,128)(2,1)S(1)} %collective-permute-done.15.d_ref, bf16[512,512]{1,0:T(8,128)(2,1)S(1)} %get-tuple-element.30.wgu_ref, ...), custom_call_target="tpu_custom_call" | custom-call | flops 4000000000 | bytes 2097152 | tf_op jit(solution)/shard_map/pallas_call | solution.py:189
  30.7 0.1 collective-permute-start.16
  30.8 1.7 %collective-permute-done.16.refs_3_ = bf16[3,128,512]{2,1,0:T(8,128)(2,1)S(1)} collective-permute-done((bf16[3,128,512]{2,1,0:T(8,128)(2,1)S(1)}, bf16[3,128,512]{2,1,0:T(8,128)(2,1)S(1)}, u32[]{:S(2)}, u32[]{:S(2)}) %collective-permute-start.16) | collective-permute-done | bytes 393248 | tf_op jit(solution)/shard_map/ppermute | solution.py:231
  32.5 0.0 collective-permute-done.13.refs_1_
  32.5 0.0 copy-done
  32.5 0.0 copy-done.1
  32.5 0.0 copy-done.2
  32.5 0.0 copy-done.3
  32.5 0.0 copy-done.5
  32.6 1.3 %shard_map.157 = (f32[12,128,128]{2,1,0:T(8,128)S(1)}, f32[3,4,512]{2,1,0:T(4,128)S(1)}) custom-call(f32[3,128,512]{2,1,0:T(8,128)S(1)} %get-tuple-element.28.refs_0_, f32[3,128,512]{2,1,0:T(8,128)S(1)} %collective-permute-done.13.refs_1_, f32[3,128,512]{2,1,0:T(8,128)S(1)} %get-tuple-element.32.refs_2_, ...), custom_call_target="tpu_custom_call" | custom-call | flops 1000000000 | bytes 13631488 | tf_op jit(solution)/shard_map/pallas_call | solution.py:189
  33.8 1.6 %collective-permute-start.17 = (f32[3,4,512]{2,1,0:T(4,128)S(1)}, f32[3,4,512]{2,1,0:T(4,128)S(1)}, u32[]{:S(2)}, u32[]{:S(2)}) collective-permute-start(f32[3,4,512]{2,1,0:T(4,128)S(1)} %get-tuple-element.37.band_ref), channel_id=1, source_target_pairs={{0,16},{16,0},{1,17},{17,1},{2,18},{18,2},{3,19},{19,3},{4,20},{20... | collective-permute-start | bytes 73736 | tf_op jit(solution)/shard_map/ppermute | solution.py:363
  35.4 2.0 %shard_map.158 = (f32[4,128,128]{2,1,0:T(8,128)}, f32[4,128,128]{2,1,0:T(8,128)}, f32[4,128,128]{2,1,0:T(8,128)}, f32[12,128,128]{2,1,0:T(8,128)S(1)}) custom-call(f32[12,128,128]{2,1,0:T(8,128)S(1)} %get-tuple-element.36.moment_ref, f32[3,4,512]{2,1,0:T(4,128)S(1)} %get-tuple-element.37.band_ref, ...), custom_call_target="tpu_custom_call" | custom-call | flops 301989888 | bytes 11190272 | tf_op jit(solution)/shard_map/pallas_call | solution.py:189
  37.4 0.3 collective-permute-done.17
  37.7 2.0 %shard_map.159 = (f32[4,128,128]{2,1,0:T(8,128)}, f32[4,128,128]{2,1,0:T(8,128)}, f32[4,128,128]{2,1,0:T(8,128)}) custom-call(f32[12,128,128]{2,1,0:T(8,128)S(1)} %get-tuple-element.42.kept_ref, f32[1,3,4,512]{3,2,1,0:T(4,128)S(1)} %bitcast.12, bf16[12,128,512]{2,1,0:T(8,128)(2,1)S(1)} %get-tuple-element.34.refs_7_.in_row_ref, ...), custom_call_target="tpu_custom_call" | custom-call | flops 301989888 | bytes 11190272 | tf_op jit(solution)/shard_map/pallas_call | solution.py:189
Async XLA Ops:
  0.6 8.1 %collective-permute-start.7 = (bf16[128,512]{1,0:T(8,128)(2,1)}, bf16[128,512]{1,0:T(8,128)(2,1)S(1)}, u32[]{:S(2)}, u32[]{:S(2)}) collective-permute-start(bf16[128,512]{1,0:T(8,128)(2,1)} %bitcast.16), channel_id=1, source_target_pairs={{4,0},{5,1},{8,4},{9,5},{12,8},{13,9},{14,12},{15,13},{10,14},{11,... | collective-permute-start | bytes 393224 | tf_op jit(solution)/shard_map/ppermute | solution.py:231
  3.6 8.4 %collective-permute-start.6 = (bf16[128,512]{1,0:T(8,128)(2,1)}, bf16[128,512]{1,0:T(8,128)(2,1)S(1)}, u32[]{:S(2)}, u32[]{:S(2)}) collective-permute-start(bf16[128,512]{1,0:T(8,128)(2,1)} %bitcast.17), channel_id=1, source_target_pairs={{0,4},{1,5},{4,8},{5,9},{8,12},{9,13},{12,14},{13,15},{14,10},{15,... | collective-permute-start | bytes 393224 | tf_op jit(solution)/shard_map/ppermute | solution.py:231
  3.8 7.8 %collective-permute-start = (bf16[128,512]{1,0:T(8,128)(2,1)}, bf16[128,512]{1,0:T(8,128)(2,1)S(1)}, u32[]{:S(2)}, u32[]{:S(2)}) collective-permute-start(bf16[128,512]{1,0:T(8,128)(2,1)} %bitcast.13), channel_id=1, source_target_pairs={{0,4},{1,5},{4,8},{5,9},{8,12},{9,13},{12,14},{13,15},{14,10},{15,... | collective-permute-start | bytes 393224 | tf_op jit(solution)/shard_map/ppermute | solution.py:231
  5.7 8.0 %collective-permute-start.1 = (bf16[128,512]{1,0:T(8,128)(2,1)}, bf16[128,512]{1,0:T(8,128)(2,1)S(1)}, u32[]{:S(2)}, u32[]{:S(2)}) collective-permute-start(bf16[128,512]{1,0:T(8,128)(2,1)} %bitcast.14), channel_id=1, source_target_pairs={{4,0},{5,1},{8,4},{9,5},{12,8},{13,9},{14,12},{15,13},{10,14},{11,... | collective-permute-start | bytes 393224 | tf_op jit(solution)/shard_map/ppermute | solution.py:231
  7.6 18.8 %copy-start.6 = (bf16[1,128,512]{2,1,0:T(8,128)(2,1)S(1)}, bf16[1,128,512]{2,1,0:T(8,128)(2,1)}, u32[]{:S(2)}) copy-start(bf16[1,128,512]{2,1,0:T(8,128)(2,1)} %param.11) | copy-start | bytes 393220
  7.7 18.8 %copy-start.7 = (bf16[1,128,512]{2,1,0:T(8,128)(2,1)S(1)}, bf16[1,128,512]{2,1,0:T(8,128)(2,1)}, u32[]{:S(2)}) copy-start(bf16[1,128,512]{2,1,0:T(8,128)(2,1)} %param.12) | copy-start | bytes 393220
  8.6 17.8 %collective-permute-start.12 = (bf16[12,128,128]{2,1,0:T(8,128)(2,1)S(1)}, bf16[12,128,128]{2,1,0:T(8,128)(2,1)S(1)}, u32[]{:S(2)}, u32[]{:S(2)}) collective-permute-start(bf16[12,128,128]{2,1,0:T(8,128)(2,1)S(1)} %constant_dynamic-update-slice_fusion.refs_14_), channel_id=1, source_target_pairs={{0,1},{1,0},{2,3},{3,2},{4,5},{5,4},{6,7},{7,6},{8,9},{9,8},{10,11... | collective-permute-start | bytes 1179656 | tf_op jit(solution)/shard_map/ppermute | solution.py:231
  8.7 8.3 %collective-permute-start.9 = (bf16[128,512]{1,0:T(8,128)(2,1)S(1)}, bf16[128,512]{1,0:T(8,128)(2,1)S(1)}, u32[]{:S(2)}, u32[]{:S(2)}) collective-permute-start(bf16[128,512]{1,0:T(8,128)(2,1)S(1)} %collective-permute-done.7.refs_9_), channel_id=1, source_target_pairs={{4,0},{5,1},{8,4},{9,5},{12,8},{13,9},{14,12},{15,13},{10,14},{11,... | collective-permute-start | bytes 393224 | tf_op jit(solution)/shard_map/ppermute | solution.py:231
  11.6 7.1 %collective-permute-start.2 = (bf16[128,512]{1,0:T(8,128)(2,1)S(1)}, bf16[128,512]{1,0:T(8,128)(2,1)S(1)}, u32[]{:S(2)}, u32[]{:S(2)}) collective-permute-start(bf16[128,512]{1,0:T(8,128)(2,1)S(1)} %collective-permute-done.refs_1_), channel_id=1, source_target_pairs={{0,4},{1,5},{4,8},{5,9},{8,12},{9,13},{12,14},{13,15},{14,10},{15,... | collective-permute-start | bytes 393224 | tf_op jit(solution)/shard_map/ppermute | solution.py:231
  12.0 7.1 %collective-permute-start.8 = (bf16[128,512]{1,0:T(8,128)(2,1)S(1)}, bf16[128,512]{1,0:T(8,128)(2,1)S(1)}, u32[]{:S(2)}, u32[]{:S(2)}) collective-permute-start(bf16[128,512]{1,0:T(8,128)(2,1)S(1)} %collective-permute-done.6.refs_8_), channel_id=1, source_target_pairs={{0,4},{1,5},{4,8},{5,9},{8,12},{9,13},{12,14},{13,15},{14,10},{15,... | collective-permute-start | bytes 393224 | tf_op jit(solution)/shard_map/ppermute | solution.py:231
  13.7 7.1 %collective-permute-start.3 = (bf16[128,512]{1,0:T(8,128)(2,1)S(1)}, bf16[128,512]{1,0:T(8,128)(2,1)S(1)}, u32[]{:S(2)}, u32[]{:S(2)}) collective-permute-start(bf16[128,512]{1,0:T(8,128)(2,1)S(1)} %collective-permute-done.1.refs_2_), channel_id=1, source_target_pairs={{4,0},{5,1},{8,4},{9,5},{12,8},{13,9},{14,12},{15,13},{10,14},{11,... | collective-permute-start | bytes 393224 | tf_op jit(solution)/shard_map/ppermute | solution.py:231
  14.1 0.8 %copy-start.4 = (f32[128,128]{1,0:T(8,128)S(1)}, f32[128,128]{1,0:T(8,128)}, u32[]{:S(2)}) copy-start(f32[128,128]{1,0:T(8,128)} %constant.4.clone.cosines_ref.refs_9_) | copy-start | bytes 196612
  14.9 0.7 %copy-start.8 = (s32[3,4,512]{2,1,0:T(4,128)S(1)}, s32[3,4,512]{2,1,0:T(4,128)}, u32[]{:S(2)}) copy-start(s32[3,4,512]{2,1,0:T(4,128)} %index_ref.1) | copy-start | bytes 73732
  17.0 6.1 %collective-permute-start.11 = (bf16[128,512]{1,0:T(8,128)(2,1)S(1)}, bf16[128,512]{1,0:T(8,128)(2,1)S(1)}, u32[]{:S(2)}, u32[]{:S(2)}) collective-permute-start(bf16[128,512]{1,0:T(8,128)(2,1)S(1)} %collective-permute-done.9.refs_11_), channel_id=1, source_target_pairs={{4,0},{5,1},{8,4},{9,5},{12,8},{13,9},{14,12},{15,13},{10,14},{11,... | collective-permute-start | bytes 393224 | tf_op jit(solution)/shard_map/ppermute | solution.py:231
  18.7 6.3 %collective-permute-start.4 = (bf16[128,512]{1,0:T(8,128)(2,1)S(1)}, bf16[128,512]{1,0:T(8,128)(2,1)S(1)}, u32[]{:S(2)}, u32[]{:S(2)}) collective-permute-start(bf16[128,512]{1,0:T(8,128)(2,1)S(1)} %collective-permute-done.2.refs_3_), channel_id=1, source_target_pairs={{0,4},{1,5},{4,8},{5,9},{8,12},{9,13},{12,14},{13,15},{14,10},{15,... | collective-permute-start | bytes 393224 | tf_op jit(solution)/shard_map/ppermute | solution.py:231
  19.1 7.3 %collective-permute-start.10 = (bf16[128,512]{1,0:T(8,128)(2,1)S(1)}, bf16[128,512]{1,0:T(8,128)(2,1)S(1)}, u32[]{:S(2)}, u32[]{:S(2)}) collective-permute-start(bf16[128,512]{1,0:T(8,128)(2,1)S(1)} %collective-permute-done.8.refs_10_), channel_id=1, source_target_pairs={{0,4},{1,5},{4,8},{5,9},{8,12},{9,13},{12,14},{13,15},{14,10},{15,... | collective-permute-start | bytes 393224 | tf_op jit(solution)/shard_map/ppermute | solution.py:231
  20.8 5.7 %collective-permute-start.5 = (bf16[128,512]{1,0:T(8,128)(2,1)S(1)}, bf16[128,512]{1,0:T(8,128)(2,1)S(1)}, u32[]{:S(2)}, u32[]{:S(2)}) collective-permute-start(bf16[128,512]{1,0:T(8,128)(2,1)S(1)} %collective-permute-done.3.refs_4_), channel_id=1, source_target_pairs={{4,0},{5,1},{8,4},{9,5},{12,8},{13,9},{14,12},{15,13},{10,14},{11,... | collective-permute-start | bytes 393224 | tf_op jit(solution)/shard_map/ppermute | solution.py:231
  23.2 5.3 %collective-permute-start.15 = (bf16[128,512]{1,0:T(8,128)(2,1)S(1)}, bf16[128,512]{1,0:T(8,128)(2,1)S(1)}, u32[]{:S(2)}, u32[]{:S(2)}) collective-permute-start(bf16[128,512]{1,0:T(8,128)(2,1)S(1)} %collective-permute-done.11.refs_13_), channel_id=1, source_target_pairs={{4,0},{5,1},{8,4},{9,5},{12,8},{13,9},{14,12},{15,13},{10,14},{11,... | collective-permute-start | bytes 393224 | tf_op jit(solution)/shard_map/ppermute | solution.py:231
  25.0 5.0 %collective-permute-start.14 = (bf16[128,512]{1,0:T(8,128)(2,1)S(1)}, bf16[128,512]{1,0:T(8,128)(2,1)S(1)}, u32[]{:S(2)}, u32[]{:S(2)}) collective-permute-start(bf16[128,512]{1,0:T(8,128)(2,1)S(1)} %collective-permute-done.4.refs_5_), channel_id=1, source_target_pairs={{0,4},{1,5},{4,8},{5,9},{8,12},{9,13},{12,14},{13,15},{14,10},{15,... | collective-permute-start | bytes 393224 | tf_op jit(solution)/shard_map/ppermute | solution.py:231
  28.4 4.2 %collective-permute-start.13 = (f32[3,128,512]{2,1,0:T(8,128)S(1)}, f32[3,128,512]{2,1,0:T(8,128)S(1)}, u32[]{:S(2)}, u32[]{:S(2)}) collective-permute-start(f32[3,128,512]{2,1,0:T(8,128)S(1)} %get-tuple-element.29), channel_id=1, source_target_pairs={{0,1},{1,0},{2,3},{3,2},{4,5},{5,4},{6,7},{7,6},{8,9},{9,8},{10,11... | collective-permute-start | bytes 2359304 | tf_op jit(solution)/shard_map/ppermute | solution.py:231
  29.9 2.6 %copy-start = (f32[128,128]{1,0:T(8,128)S(1)}, f32[128,128]{1,0:T(8,128)}, u32[]{:S(2)}) copy-start(f32[128,128]{1,0:T(8,128)} %constant.5.clone.refs_10_.cosines_t_ref) | copy-start | bytes 196612
  29.9 2.6 %copy-start.1 = (f32[1,4,128,128]{3,2,1,0:T(8,128)S(1)}, f32[1,4,128,128]{3,2,1,0:T(8,128)}, u32[]{:S(2)}) copy-start(f32[1,4,128,128]{3,2,1,0:T(8,128)} %param.16) | copy-start | bytes 786436
  29.9 2.6 %copy-start.2 = (f32[1,4,128,128]{3,2,1,0:T(8,128)S(1)}, f32[1,4,128,128]{3,2,1,0:T(8,128)}, u32[]{:S(2)}) copy-start(f32[1,4,128,128]{3,2,1,0:T(8,128)} %param.17) | copy-start | bytes 786436
  29.9 2.6 %copy-start.3 = (f32[1,4,128,128]{3,2,1,0:T(8,128)S(1)}, f32[1,4,128,128]{3,2,1,0:T(8,128)}, u32[]{:S(2)}) copy-start(f32[1,4,128,128]{3,2,1,0:T(8,128)} %param.18) | copy-start | bytes 786436
  29.9 2.6 %copy-start.5 = (f32[128,128]{1,0:T(8,128)S(1)}, f32[128,128]{1,0:T(8,128)}, u32[]{:S(2)}) copy-start(f32[128,128]{1,0:T(8,128)} %constant.4.clone.cosines_ref.refs_9_) | copy-start | bytes 196612
  30.7 1.8 %collective-permute-start.16 = (bf16[3,128,512]{2,1,0:T(8,128)(2,1)S(1)}, bf16[3,128,512]{2,1,0:T(8,128)(2,1)S(1)}, u32[]{:S(2)}, u32[]{:S(2)}) collective-permute-start(bf16[3,128,512]{2,1,0:T(8,128)(2,1)S(1)} %get-tuple-element.33), channel_id=1, source_target_pairs={{0,1},{1,0},{2,3},{3,2},{4,5},{5,4},{6,7},{7,6},{8,9},{9,8},{10,11... | collective-permute-start | bytes 1179656 | tf_op jit(solution)/shard_map/ppermute | solution.py:231
  33.8 3.9 %collective-permute-start.17 = (f32[3,4,512]{2,1,0:T(4,128)S(1)}, f32[3,4,512]{2,1,0:T(4,128)S(1)}, u32[]{:S(2)}, u32[]{:S(2)}) collective-permute-start(f32[3,4,512]{2,1,0:T(4,128)S(1)} %get-tuple-element.37.band_ref), channel_id=1, source_target_pairs={{0,16},{16,0},{1,17},{17,1},{2,18},{18,2},{3,19},{19,3},{4,20},{20... | collective-permute-start | bytes 73736 | tf_op jit(solution)/shard_map/ppermute | solution.py:363

commit v2 on v1

--- a/solution.py
+++ b/solution.py
@@ -11,6 +11,7 @@
 MOMENTUM_DECAY = 0.999
 LATE_FLOPS = 4 * 10**9
 TABLES_FLOPS = 10**9
+PAUSE_FLOPS = 10**9
 F32 = jnp.float32
 BF16 = jnp.bfloat16
 
@@ -45,17 +46,6 @@
 def lanes_to_rows(value, side):
     count = value.shape[1] // side
     return jnp.concatenate([value[:, i * side : (i + 1) * side] for i in range(count)], axis=0)
-
-
-def decode(values, in_row_ref, cells_ref, cosines_t):
-    side = cosines_t.shape[0]
-    inner = []
-    for b, row in enumerate(values):
-        hi, lo = split2(row)
-        in_row = in_row_ref[b]
-        both = dot(jnp.concatenate([in_row * hi, in_row * lo], axis=0), cells_ref[b])
-        inner.append(both[:side, :side] + (both[:side, side:] + both[side:, :side]))
-    return dot3(cosines_t, jnp.concatenate(inner, axis=1))
 
 
 def activations(wgu, wd, x, d):
@@ -68,9 +58,8 @@
     return d_gate, (dh * swish).astype(BF16), (swish * up).astype(BF16)
 
 
-def tables_kernel(index_ref, cosines_ref, in_row_ref, in_col_ref, cells_ref):
-    side = cosines_ref.shape[0]
-    parts = jnp.concatenate(split2(cosines_ref[...]), axis=1)
+def tables_kernel(index_ref, _, in_row_ref, in_col_ref, in_col_t_ref, mask_ref):
+    side = mask_ref.shape[1]
     shift = int(np.log2(side))
     matrices, count, keep = index_ref.shape
     lines = lax.broadcasted_iota(jnp.int32, (side, keep), 0)
@@ -78,46 +67,63 @@
         for i in range(count):
             b = m * count + i
             index = index_ref[m, i : i + 1, :]
+            in_row = jnp.where((index >> shift) == lines, 1.0, 0.0).astype(BF16)
             in_col = jnp.where((index & (side - 1)) == lines, 1.0, 0.0).astype(BF16)
-            in_row_ref[b] = jnp.where((index >> shift) == lines, 1.0, 0.0).astype(BF16)
+            in_col_t = in_col.T
+            in_row_ref[b] = in_row
             in_col_ref[b] = in_col
-            cells_ref[b] = dot(in_col.T, parts).astype(BF16)
-
-
-def early_kernel(shards, *refs):
-    xs, ds, weights = refs[:shards], refs[shards : 2 * shards], refs[2 * shards : 2 * shards + 2]
-    own_ref, par_ref, wgu_ref, wd_ref, x_all, d_all, act = refs[2 * shards + 2 :]
-    rows = xs[0].shape[0]
-    side = own_ref.shape[1]
-    count = weights[0].shape[0] // 3
-    for i in range(count):
-        cols = slice(i * side, (i + 1) * side)
-        for p in range(2):
-            gate, up, down = (weights[p][m * count + i] for m in range(3))
-            wgu_ref[p * side : (p + 1) * side, cols] = gate.T
-            wgu_ref[(2 + p) * side : (3 + p) * side, cols] = up.T
-            wd_ref[p * side : (p + 1) * side, cols] = down
-    wgu, wd = wgu_ref[...], wd_ref[...]
-    for s in range(0, shards, 2):
-        some = range(s, min(s + 2, shards))
+            in_col_t_ref[b] = in_col_t
+            mask_ref[b] = dot(in_row, in_col_t).astype(BF16)
+
+
+def pause_kernel(out_ref):
+    out_ref[...] = jnp.zeros_like(out_ref)
+
+
+def column_grads(xs, ds, wgu, wd, x_all, d_all, act):
+    rows, half = xs[0].shape[0], wd.shape[0]
+    for s in range(0, len(xs), 2):
+        some = range(s, min(s + 2, len(xs)))
         x = jnp.concatenate([xs[j][...] for j in some], axis=0)
         d = jnp.concatenate([ds[j][...] for j in some], axis=0)
         span = pl.ds(s * rows, len(some) * rows)
         x_all[span, :] = x
         d_all[span, :] = d
         d_gate, d_up, hidden = activations(wgu, wd, x, d)
-        act[: 2 * side, span] = d_gate
-        act[2 * side : 4 * side, span] = d_up
-        act[4 * side :, span] = hidden
-    g_in = dot(act[: 4 * side, :], x_all[...])
-    g_out = dot(act[4 * side :, :], d_all[...])
-    for m, grad in enumerate((g_in[: 2 * side], g_in[2 * side :], g_out)):
+        act[:half, span] = d_gate
+        act[half : 2 * half, span] = d_up
+        act[2 * half :, span] = hidden
+    g_in = dot(act[: 2 * half, :], x_all[...])
+    return g_in[:half], g_in[half:], dot(act[2 * half :, :], d_all[...])
+
+
+def early_kernel(shards, *refs):
+    xs, ds, weights = refs[:shards], refs[shards : 2 * shards], refs[2 * shards : 2 * shards + 6]
+    own_ref, par_ref, wgu_ref, wd_ref, *scratch = refs[2 * shards + 7 :]
+    count, side, _ = weights[0].shape
+    for i in range(count):
+        cols = slice(i * side, (i + 1) * side)
+        for p in range(2):
+            gate, up, down = (ref[i] for ref in weights[3 * p : 3 * p + 3])
+            wgu_ref[p * side : (p + 1) * side, cols] = gate.T
+            wgu_ref[(2 + p) * side : (3 + p) * side, cols] = up.T
+            wd_ref[p * side : (p + 1) * side, cols] = down
+    for m, grad in enumerate(column_grads(xs, ds, wgu_ref[...], wd_ref[...], *scratch)):
         own_ref[m] = grad[:side]
         par_ref[m] = grad[side:]
 
 
+def middle_kernel(shards, *refs):
+    xs, ds = refs[:shards], refs[shards : 2 * shards]
+    wgu_ref, wd_ref, own_in, par_in, own_ref, par_ref, *scratch = refs[2 * shards :]
+    side = own_ref.shape[1]
+    for m, grad in enumerate(column_grads(xs, ds, wgu_ref[...], wd_ref[...], *scratch)):
+        own_ref[m] = own_in[m] + grad[:side]
+        par_ref[m] = par_in[m] + grad[side:]
+
+
 def moment_step(
-    grads, mom_refs, in_row_ref, in_col_ref, cosines_ref, cosines_t_ref, moment_ref, band_ref
+    grads, mom_refs, in_row_ref, in_col_ref, mask_ref, cosines_ref, cosines_t_ref, moment_ref, kept_ref, band_ref
 ):
     side = cosines_ref.shape[0]
     count = mom_refs[0].shape[0]
@@ -135,7 +141,9 @@
     for m in range(3):
         for i in range(count):
             b = m * count + i
-            hi, lo = split2(coeffs[b * side : (b + 1) * side])
+            block = coeffs[b * side : (b + 1) * side]
+            kept_ref[b] = block * mask_ref[b].astype(F32)
+            hi, lo = split2(block)
             in_col = in_col_ref[b]
             at_col = dot(jnp.concatenate([hi, lo], axis=1), jnp.concatenate([in_col, in_col], axis=0))
             band_ref[m, i : i + 1, :] = jnp.sum(
@@ -157,28 +165,37 @@
     moment_step(grads, refs[terms : terms + 3], *refs[terms + 3 :])
 
 
-def residual_kernel(moment_ref, band_ref, in_row_ref, cells_ref, cosines_t_ref, *outs):
+def residual_kernel(moment_ref, kept_ref, in_col_t_ref, cosines_ref, cosines_t_ref, *outs):
+    *residuals, decoded_ref, cells_ref = outs
+    side = cosines_ref.shape[0]
+    count = residuals[0].shape[0]
+    blocks = range(3 * count)
+    cosines = cosines_ref[...]
+    inner = dot3(jnp.concatenate([kept_ref[b] for b in blocks], axis=0), cosines)
+    inner = jnp.concatenate([inner[b * side : (b + 1) * side] for b in blocks], axis=1)
+    decoded = dot3(cosines_t_ref[...], inner)
+    for b in blocks:
+        kept = decoded[:, b * side : (b + 1) * side]
+        decoded_ref[b] = kept
+        residuals[b // count][b % count] = moment_ref[b] - kept
+    parts = jnp.concatenate(split2(cosines), axis=1)
+    for b in blocks:
+        cells_ref[b] = dot(in_col_t_ref[b], parts).astype(BF16)
+
+
+def update_kernel(decoded_ref, other_ref, in_row_ref, cells_ref, cosines_t_ref, *outs):
     side = cosines_t_ref.shape[0]
     count = outs[0].shape[0]
-    pairs = [(m, i) for m in range(3) for i in range(count)]
-    values = [band_ref[m, i : i + 1, :] for m, i in pairs]
-    decoded = decode(values, in_row_ref, cells_ref, cosines_t_ref[...])
-    for b, (m, i) in enumerate(pairs):
-        kept = decoded[:, b * side : (b + 1) * side]
-        outs[3][b] = kept
-        outs[m][i] = moment_ref[b] - kept
-
-
-def update_kernel(kept_ref, other_ref, in_row_ref, cells_ref, cosines_t_ref, *outs):
-    side = cosines_t_ref.shape[0]
-    count = outs[0].shape[0]
-    pairs = [(m, i) for m in range(3) for i in range(count)]
-    values = [
-        sum(other_ref[g, m, i : i + 1, :] for g in range(other_ref.shape[0])) for m, i in pairs
-    ]
-    decoded = decode(values, in_row_ref, cells_ref, cosines_t_ref[...])
-    for b, (m, i) in enumerate(pairs):
-        outs[m][i] = kept_ref[b] + decoded[:, b * side : (b + 1) * side]
+    inner = []
+    for b in range(3 * count):
+        m, i = b // count, b % count
+        hi, lo = split2(sum(other_ref[g, m, i : i + 1, :] for g in range(other_ref.shape[0])))
+        in_row = in_row_ref[b]
+        both = dot(jnp.concatenate([in_row * hi, in_row * lo], axis=0), cells_ref[b])
+        inner.append(both[:side, :side] + (both[:side, side:] + both[side:, :side]))
+    update = dot3(cosines_t_ref[...], jnp.concatenate(inner, axis=1))
+    for b in range(3 * count):
+        outs[b // count][b % count] = decoded_ref[b] + update[:, b * side : (b + 1) * side]
 
 
 def call(kernel, out_shape, flops, *args, scratch=(), in_place={}):
@@ -205,22 +222,24 @@
     return forward, [(b, a) for a, b in forward], chips
 
 
-def band_tables(band_index, cosines):
-    blocks, keep, side = band_index.shape[0] * band_index.shape[1], band_index.shape[2], cosines.shape[0]
+def band_tables(band_index, side, ahead):
+    blocks, keep = band_index.shape[0] * band_index.shape[1], band_index.shape[2]
     return call(
         tables_kernel,
         (
             jax.ShapeDtypeStruct((blocks, side, keep), BF16),
             jax.ShapeDtypeStruct((blocks, side, keep), BF16),
-            jax.ShapeDtypeStruct((blocks, keep, 2 * side), BF16),
+            jax.ShapeDtypeStruct((blocks, keep, side), BF16),
+            jax.ShapeDtypeStruct((blocks, side, side), BF16),
         ),
         TABLES_FLOPS,
         band_index,
-        cosines,
-    )
-
-
-def column_moments(x, d, weights, momenta, tables, cosines, cosines_t, shapes):
+        ahead,
+        in_place={1: pl.ANY},
+    )
+
+
+def column_moments(x, d, weights, momenta, band_index, cosines, cosines_t, shapes):
     side = weights[0].shape[1]
     rows, width = x.shape
     count = lax.axis_size("fsdp")
@@ -232,20 +251,35 @@
 
     xf, db, df, xb = send(x, forward), send(d, back), send(d, forward), send(x, back)
     xs, ds = [x, xf, xb], [d, df, db]
-    own_weights = jnp.concatenate(weights, axis=0)
-    partner_weights = send(own_weights, swap)
-    in_row, in_col, cells = tables
-    for hop in range(2, chips // 2):
-        if hop == 3:
-            db, in_col = lax.optimization_barrier((db, in_col))
+    partner_weights = [send(w, swap) for w in weights]
+    pause = call(pause_kernel, jax.ShapeDtypeStruct((8, 128), F32), PAUSE_FLOPS)
+    db, pause = lax.optimization_barrier((db, pause))
+    arrived = []
+
+    def with_weight(value):
+        if len(arrived) == len(partner_weights):
+            return value
+        value, weight = lax.optimization_barrier((value, partner_weights[len(arrived)]))
+        arrived.append(weight)
+        return value
+
+    for _ in range(chips // 2 - 2):
+        db = with_weight(db)
         xf, db, df, xb = send(xf, forward), send(db, back), send(df, forward), send(xb, back)
         xs += [xf, xb]
         ds += [df, db]
-    x_last, d_last = send(xf, forward), send(db, back)
-
-    early = len(xs)
-    tokens = early * rows
+    x_last, d_last = send(xf, forward), send(with_weight(db), back)
+    partner_weights[: len(arrived)] = arrived
+
+    def scratch(shards):
+        return (
+            pltpu.VMEM((shards * rows, width), BF16),
+            pltpu.VMEM((shards * rows, width), BF16),
+            pltpu.VMEM((6 * side, shards * rows), BF16),
+        )
+
     part = jax.ShapeDtypeStruct((3, side, width), F32)
+    early = len(xs) - 2
     own, partner, wgu, wd = call(
         functools.partial(early_kernel, early),
         (
@@ -254,16 +288,25 @@
             jax.ShapeDtypeStruct((4 * side, width), BF16),
             jax.ShapeDtypeStruct((2 * side, width), BF16),
         ),
-        24 * tokens * width * side,
-        *xs,
-        *ds,
-        own_weights,
-        partner_weights,
-        scratch=(
-            pltpu.VMEM((tokens, width), BF16),
-            pltpu.VMEM((tokens, width), BF16),
-            pltpu.VMEM((6 * side, tokens), BF16),
-        ),
+        24 * early * rows * width * side,
+        *xs[:early],
+        *ds[:early],
+        *weights,
+        *partner_weights,
+        pause,
+        scratch=scratch(early),
+    )
+    own, partner = call(
+        functools.partial(middle_kernel, 2),
+        (part, part),
+        24 * 2 * rows * width * side,
+        *xs[early:],
+        *ds[early:],
+        wgu,
+        wd,
+        own,
+        partner,
+        scratch=scratch(2),
     )
     own_late, partner_late = call(
         late_kernel,
@@ -274,7 +317,8 @@
         wgu,
         wd,
     )
-    return call(
+    in_row, in_col, in_col_t, mask = band_tables(band_index, side, own_late)
+    moments = call(
         functools.partial(moment_kernel, 4),
         shapes,
         10**9,
@@ -285,17 +329,30 @@
         *momenta,
         in_row,
         in_col,
+        mask,
         cosines,
         cosines_t,
     )
-
-
-def shared_column_moments(x, d, weights, momenta, tables, cosines, cosines_t, shapes):
+    return moments, in_row, in_col_t
+
+
+def shared_column_moments(x, d, weights, momenta, band_index, cosines, cosines_t, shapes):
     gate_weight, up_weight, down_weight = weights
     own = shared_column_grads(x, d, gate_weight, up_weight, down_weight)
-    return call(
-        functools.partial(moment_kernel, 1), shapes, 0, own, *momenta, *tables[:2], cosines, cosines_t
-    )
+    in_row, in_col, in_col_t, mask = band_tables(band_index, cosines.shape[0], own)
+    moments = call(
+        functools.partial(moment_kernel, 1),
+        shapes,
+        0,
+        own,
+        *momenta,
+        in_row,
+        in_col,
+        mask,
+        cosines,
+        cosines_t,
+    )
+    return moments, in_row, in_col_t
 
 
 def shared_column_grads(x, d, gate_weight, up_weight, down_weight):
@@ -346,16 +403,15 @@
     cosines, cosines_t = jnp.asarray(dct_table(side)), jnp.asarray(dct_table(side).T)
     blocks = 3 * blk_dev
     dense = jax.ShapeDtypeStruct((blocks, side, side), F32)
-    in_row, in_col, cells = band_tables(band_index, cosines)
-    moment, band = step(
+    (moment, kept, band), in_row, in_col_t = step(
         x_in[0],
         d_out[0],
         (gate_weight, up_weight, down_weight),
         (mom_gate[0], mom_up[0], mom_down[0]),
-        (in_row, in_col, cells),
+        band_index,
         cosines,
         cosines_t,
-        (dense, jax.ShapeDtypeStruct(band_index.shape, F32)),
+        (dense, dense, jax.ShapeDtypeStruct(band_index.shape, F32)),
     )
     reps = lax.axis_size("rep")
     other = jnp.stack(
@@ -366,11 +422,18 @@
     )
     result = jax.ShapeDtypeStruct((blk_dev, side, side), F32)
     flops = 4 * 3 * blocks * side**3
-    *residuals, kept = call(
-        residual_kernel, (result,) * 3 + (dense,), flops, moment, band, in_row, cells, cosines_t
+    *residuals, decoded, cells = call(
+        residual_kernel,
+        (result,) * 3 + (dense, jax.ShapeDtypeStruct((*in_col_t.shape[:2], 2 * side), BF16)),
+        flops,
+        moment,
+        kept,
+        in_col_t,
+        cosines,
+        cosines_t,
     )
     updates = call(
-        update_kernel, (result,) * 3, flops, kept, other, in_row, cells, cosines_t
+        update_kernel, (result,) * 3, flops, decoded, other, in_row, cells, cosines_t
     )
     return (*(r[None] for r in residuals), *updates)
 

time: 40 us -> 37.2 us (0.930)
  local copies, waits for them, and re-layouts: 4.41 us -> 0.06 us
  waiting for transfers between devices: 7.75 us -> 10.4 us
  starting transfers between devices: 17.5 us -> 16.6 us
    unnamed x20 -> x22, local copies, waits for them, and re-layouts: 3.45 us -> 0.06 us
    ppermute x17 -> x19, waiting for transfers between devices: 7.44 us -> 9.69 us  [send(): return lax.ppermute(value, 'fsdp', perm)]
    concatenate x1 -> x0, local copies, waits for them, and re-layouts: 0.97 us -> none  [column_moments(): own_weights = jnp.concatenate(weights, axis=0)]
    ppermute x17 -> x19, starting transfers between devices: 15.9 us -> 15 us  [send(): return lax.ppermute(value, 'fsdp', perm)]
    ppermute x1, waiting for transfers between devices: 0.31 us -> 0.73 us  [per_device(): lax.ppermute(band, 'rep', [(r, (r + s) % reps) for r in range(reps)])]
    pallas_call x6 -> x8, Pallas kernels: 9.28 us -> 9.16 us  [call(): pl.pallas_call(kernel, out_shape=out_shape, in_specs=specs, scratch_shape...]
  transfers between devices with their start and end apart: 18 -> 20, of which waited for: 6 -> 13; matrix products, arithmetic and copies ran while one was open for 7% -> 0% of each run, Pallas kernels for 15% -> 16%
where the time goes in v2:
time: 37.2 us; the launch traced here: 37 us
  starting transfers between devices  16.6 us (45%)
  waiting for transfers between devices  10.4 us (28%)
  Pallas kernels  9.16 us (25%)
  between operations  0.83 us (2%)
    ppermute x19, starting transfers between devices, send(): return lax.ppermute(value, 'fsdp', perm)  15 us
    ppermute x19, waiting for transfers between devices, send(): return lax.ppermute(value, 'fsdp', perm)  9.69 us
    pallas_call x8, Pallas kernels, call(): pl.pallas_call(kernel, out_shape=out_shape, in_specs=specs, scratch_shape...  9.16 us
    ppermute x1, starting transfers between devices, per_device(): lax.ppermute(band, 'rep', [(r, (r + s) % reps) for r in range(reps)])  1.59 us
  transfers between devices with their start and end apart: 20, of which 13 were waited for; matrix products, arithmetic and copies ran while one was open for 0% of the time, Pallas kernels for 16%

profile of v2, /device:TPU:0, one launch (start us, length us, event | category | flops | bytes accessed | tf_op | source)
XLA Modules:
  0.0 37.0 jit_solution(12154531820753608285)
XLA Ops:
  0.6 3.0 %collective-permute-start.9 = (bf16[128,512]{1,0:T(8,128)(2,1)}, bf16[128,512]{1,0:T(8,128)(2,1)S(1)}, u32[]{:S(2)}, u32[]{:S(2)}) collective-permute-start(bf16[128,512]{1,0:T(8,128)(2,1)} %bitcast.16), channel_id=1, source_target_pairs={{4,0},{5,1},{8,4},{9,5},{12,8},{13,9},{14,12},{15,13},{10,14},{11,... | collective-permute-start | bytes 393224 | tf_op jit(solution)/shard_map/ppermute | solution.py:250
  3.6 0.0 collective-permute-start.10
  3.6 0.0 copy-start.6
  3.6 0.0 copy-start.7
  3.7 0.2 collective-permute-start
  3.9 1.8 %collective-permute-start.3 = (bf16[128,512]{1,0:T(8,128)(2,1)}, bf16[128,512]{1,0:T(8,128)(2,1)S(1)}, u32[]{:S(2)}, u32[]{:S(2)}) collective-permute-start(bf16[128,512]{1,0:T(8,128)(2,1)} %bitcast.14), channel_id=1, source_target_pairs={{4,0},{5,1},{8,4},{9,5},{12,8},{13,9},{14,12},{15,13},{10,14},{11,... | collective-permute-start | bytes 393224 | tf_op jit(solution)/shard_map/ppermute | solution.py:250
  5.7 0.2 collective-permute-start.6
  5.9 1.7 %collective-permute-done.9.refs_7_ = bf16[128,512]{1,0:T(8,128)(2,1)S(1)} collective-permute-done((bf16[128,512]{1,0:T(8,128)(2,1)}, bf16[128,512]{1,0:T(8,128)(2,1)S(1)}, u32[]{:S(2)}, u32[]{:S(2)}) %collective-permute-start.9) | collective-permute-done | bytes 131104 | tf_op jit(solution)/shard_map/ppermute | solution.py:250
  7.6 0.0 copy-done.8
  7.6 0.0 collective-permute-start.12
  7.6 0.0 collective-permute-done.10.refs_13_
  7.6 1.8 %collective-permute-start.11 = (bf16[128,512]{1,0:T(8,128)(2,1)S(1)}, bf16[128,512]{1,0:T(8,128)(2,1)S(1)}, u32[]{:S(2)}, u32[]{:S(2)}) collective-permute-start(bf16[128,512]{1,0:T(8,128)(2,1)S(1)} %collective-permute-done.9.refs_7_), channel_id=1, source_target_pairs={{4,0},{5,1},{8,4},{9,5},{12,8},{13,9},{14,12},{15,13},{10,14},{11,... | collective-permute-start | bytes 393224 | tf_op jit(solution)/shard_map/ppermute | solution.py:250
  9.4 0.8 %collective-permute-done.refs_1_ = bf16[128,512]{1,0:T(8,128)(2,1)S(1)} collective-permute-done((bf16[128,512]{1,0:T(8,128)(2,1)}, bf16[128,512]{1,0:T(8,128)(2,1)S(1)}, u32[]{:S(2)}, u32[]{:S(2)}) %collective-permute-start) | collective-permute-done | bytes 131104 | tf_op jit(solution)/shard_map/ppermute | solution.py:250
  10.2 0.2 collective-permute-start.1
  10.4 0.0 collective-permute-done.3.refs_2_
  10.4 1.8 %collective-permute-start.4 = (bf16[128,512]{1,0:T(8,128)(2,1)S(1)}, bf16[128,512]{1,0:T(8,128)(2,1)S(1)}, u32[]{:S(2)}, u32[]{:S(2)}) collective-permute-start(bf16[128,512]{1,0:T(8,128)(2,1)S(1)} %collective-permute-done.3.refs_2_), channel_id=1, source_target_pairs={{4,0},{5,1},{8,4},{9,5},{12,8},{13,9},{14,12},{15,13},{10,14},{11,... | collective-permute-start | bytes 393224 | tf_op jit(solution)/shard_map/ppermute | solution.py:250
  12.2 0.8 %collective-permute-done.6.refs_6_ = bf16[128,512]{1,0:T(8,128)(2,1)S(1)} collective-permute-done((bf16[128,512]{1,0:T(8,128)(2,1)}, bf16[128,512]{1,0:T(8,128)(2,1)S(1)}, u32[]{:S(2)}, u32[]{:S(2)}) %collective-permute-start.6) | collective-permute-done | bytes 131104 | tf_op jit(solution)/shard_map/ppermute | solution.py:250
  13.0 0.2 collective-permute-start.7
  13.2 0.0 collective-permute-done.12.refs_14_
  13.2 0.0 copy-done.9
  13.2 0.0 collective-permute-start.14
  13.2 0.8 %collective-permute-done.11.refs_9_ = bf16[128,512]{1,0:T(8,128)(2,1)S(1)} collective-permute-done((bf16[128,512]{1,0:T(8,128)(2,1)S(1)}, bf16[128,512]{1,0:T(8,128)(2,1)S(1)}, u32[]{:S(2)}, u32[]{:S(2)}) %collective-permute-start.11) | collective-permute-done | bytes 131104 | tf_op jit(solution)/shard_map/ppermute | solution.py:250
  14.0 1.7 %collective-permute-start.13 = (bf16[128,512]{1,0:T(8,128)(2,1)S(1)}, bf16[128,512]{1,0:T(8,128)(2,1)S(1)}, u32[]{:S(2)}, u32[]{:S(2)}) collective-permute-start(bf16[128,512]{1,0:T(8,128)(2,1)S(1)} %collective-permute-done.11.refs_9_), channel_id=1, source_target_pairs={{4,0},{5,1},{8,4},{9,5},{12,8},{13,9},{14,12},{15,13},{10,14},{11,... | collective-permute-start | bytes 393224 | tf_op jit(solution)/shard_map/ppermute | solution.py:250
  15.7 0.2 collective-permute-done.1.refs_3_
  15.9 0.2 collective-permute-start.2
  16.1 0.3 collective-permute-done.4.refs_4_
  16.4 1.7 %collective-permute-start.5 = (bf16[128,512]{1,0:T(8,128)(2,1)S(1)}, bf16[128,512]{1,0:T(8,128)(2,1)S(1)}, u32[]{:S(2)}, u32[]{:S(2)}) collective-permute-start(bf16[128,512]{1,0:T(8,128)(2,1)S(1)} %collective-permute-done.4.refs_4_), channel_id=1, source_target_pairs={{4,0},{5,1},{8,4},{9,5},{12,8},{13,9},{14,12},{15,13},{10,14},{11,... | collective-permute-start | bytes 393224 | tf_op jit(solution)/shard_map/ppermute | solution.py:250
  18.1 0.5 %collective-permute-done.7.refs_8_ = bf16[128,512]{1,0:T(8,128)(2,1)S(1)} collective-permute-done((bf16[128,512]{1,0:T(8,128)(2,1)S(1)}, bf16[128,512]{1,0:T(8,128)(2,1)S(1)}, u32[]{:S(2)}, u32[]{:S(2)}) %collective-permute-start.7) | collective-permute-done | bytes 131104 | tf_op jit(solution)/shard_map/ppermute | solution.py:250
  18.6 0.1 collective-permute-start.8
  18.7 0.0 collective-permute-done.14.refs_15_
  18.7 1.2 %collective-permute-done.13.refs_3_ = bf16[128,512]{1,0:T(8,128)(2,1)S(1)} collective-permute-done((bf16[128,512]{1,0:T(8,128)(2,1)S(1)}, bf16[128,512]{1,0:T(8,128)(2,1)S(1)}, u32[]{:S(2)}, u32[]{:S(2)}) %collective-permute-start.13) | collective-permute-done | bytes 131104 | tf_op jit(solution)/shard_map/ppermute | solution.py:250
  19.9 1.9 %collective-permute-start.17 = (bf16[128,512]{1,0:T(8,128)(2,1)S(1)}, bf16[128,512]{1,0:T(8,128)(2,1)S(1)}, u32[]{:S(2)}, u32[]{:S(2)}) collective-permute-start(bf16[128,512]{1,0:T(8,128)(2,1)S(1)} %collective-permute-done.13.refs_3_), channel_id=1, source_target_pairs={{4,0},{5,1},{8,4},{9,5},{12,8},{13,9},{14,12},{15,13},{10,14},{11,... | collective-permute-start | bytes 393224 | tf_op jit(solution)/shard_map/ppermute | solution.py:250
  21.8 0.4 %collective-permute-done.2.refs_0_ = bf16[128,512]{1,0:T(8,128)(2,1)S(1)} collective-permute-done((bf16[128,512]{1,0:T(8,128)(2,1)S(1)}, bf16[128,512]{1,0:T(8,128)(2,1)S(1)}, u32[]{:S(2)}, u32[]{:S(2)}) %collective-permute-start.2) | collective-permute-done | bytes 131104 | tf_op jit(solution)/shard_map/ppermute | solution.py:250
  22.2 0.0 collective-permute-start.16
  22.2 0.0 copy-done.5
  22.2 0.0 copy-done.6
  22.3 0.0 copy-done.7
  22.3 1.5 %shard_map.155 = (f32[3,128,512]{2,1,0:T(8,128)S(1)}, f32[3,128,512]{2,1,0:T(8,128)S(1)}, bf16[512,512]{1,0:T(8,128)(2,1)S(1)}, bf16[256,512]{1,0:T(8,128)(2,1)S(1)}) custom-call(bf16[128,512]{1,0:T(8,128)(2,1)S(1)} %bitcast.15, bf16[128,512]{1,0:T(8,128)(2,1)S(1)} %collective-permute-done.refs_1_, bf16[128,512]{1,0:T(8,128)(2,1)S(1)} %collective-permute-done.3.refs_2_, ...), custom_call_target="tpu_custom_call" | custom-call | flops 1006632960 | bytes 4202496 | tf_op jit(solution)/shard_map/pallas_call | solution.py:206
  23.8 0.0 collective-permute-done.5.refs_1_
  23.8 1.2 %collective-permute-done.8.refs_2_ = bf16[128,512]{1,0:T(8,128)(2,1)S(1)} collective-permute-done((bf16[128,512]{1,0:T(8,128)(2,1)S(1)}, bf16[128,512]{1,0:T(8,128)(2,1)S(1)}, u32[]{:S(2)}, u32[]{:S(2)}) %collective-permute-start.8) | collective-permute-done | bytes 131104 | tf_op jit(solution)/shard_map/ppermute | solution.py:250
  25.0 0.9 %shard_map.156 = (f32[3,128,512]{2,1,0:T(8,128)S(1)}, f32[3,128,512]{2,1,0:T(8,128)S(1)}) custom-call(bf16[128,512]{1,0:T(8,128)(2,1)S(1)} %collective-permute-done.2.refs_0_, bf16[128,512]{1,0:T(8,128)(2,1)S(1)} %collective-permute-done.5.refs_1_, bf16[128,512]{1,0:T(8,128)(2,1)S(1)} %collective-permute-done.8.refs_2_, ...), custom_call_target="tpu_custom_call" | custom-call | flops 402653184 | bytes 5767168 | tf_op jit(solution)/shard_map/pallas_call | solution.py:206
  25.9 0.0 copy-start.10
  25.9 0.1 collective-permute-start.15
  26.0 1.2 %collective-permute-done.16.x_ref = bf16[128,512]{1,0:T(8,128)(2,1)S(1)} collective-permute-done((bf16[128,512]{1,0:T(8,128)(2,1)S(1)}, bf16[128,512]{1,0:T(8,128)(2,1)S(1)}, u32[]{:S(2)}, u32[]{:S(2)}) %collective-permute-start.16) | collective-permute-done | bytes 131104 | tf_op jit(solution)/shard_map/ppermute | solution.py:250
  27.2 0.0 collective-permute-done.17.d_ref
  27.2 0.8 %shard_map.157 = (f32[3,128,512]{2,1,0:T(8,128)S(1)}, bf16[3,128,512]{2,1,0:T(8,128)(2,1)S(1)}) custom-call(bf16[128,512]{1,0:T(8,128)(2,1)S(1)} %collective-permute-done.16.x_ref, bf16[128,512]{1,0:T(8,128)(2,1)S(1)} %collective-permute-done.17.d_ref, bf16[512,512]{1,0:T(8,128)(2,1)S(1)} %get-tuple-element.44.refs_4_.wgu_ref, ...), custom_call_target="tpu_custom_call" | custom-call | flops 4000000000 | bytes 2097152 | tf_op jit(solution)/shard_map/pallas_call | solution.py:206
  28.0 0.1 collective-permute-start.18
  28.0 0.0 copy-done.10
  28.1 0.0 copy-start
  28.1 0.0 copy-start.1
  28.1 0.0 copy-start.2
  28.1 0.0 copy-start.3
  28.1 0.0 copy-start.4
  28.1 1.1 %shard_map.158 = (bf16[12,128,512]{2,1,0:T(8,128)(2,1)S(1)}, bf16[12,128,512]{2,1,0:T(8,128)(2,1)S(1)}, bf16[12,512,128]{2,1,0:T(8,128)(2,1)S(1)}, bf16[12,128,128]{2,1,0:T(8,128)(2,1)S(1)}) custom-call(s32[3,4,512]{2,1,0:T(4,128)S(1)} %copy-done.10, f32[3,128,512]{2,1,0:T(8,128)S(1)} %get-tuple-element.51._.refs_2_), custom_call_target="tpu_custom_call" | custom-call | flops 1000000000 | bytes 1622016 | tf_op jit(solution)/shard_map/pallas_call | solution.py:206
  29.2 0.5 %collective-permute-done.18.refs_3_ = bf16[3,128,512]{2,1,0:T(8,128)(2,1)S(1)} collective-permute-done((bf16[3,128,512]{2,1,0:T(8,128)(2,1)S(1)}, bf16[3,128,512]{2,1,0:T(8,128)(2,1)S(1)}, u32[]{:S(2)}, u32[]{:S(2)}) %collective-permute-start.18) | collective-permute-done | bytes 393248 | tf_op jit(solution)/shard_map/ppermute | solution.py:250
  29.8 0.0 collective-permute-done.15.refs_1_
  29.8 0.0 copy-done
  29.8 0.0 copy-done.1
  29.8 0.0 copy-done.2
  29.8 1.3 %shard_map.159 = (f32[12,128,128]{2,1,0:T(8,128)S(1)}, f32[12,128,128]{2,1,0:T(8,128)S(1)}, f32[3,4,512]{2,1,0:T(4,128)S(1)}) custom-call(f32[3,128,512]{2,1,0:T(8,128)S(1)} %get-tuple-element.48.refs_0_, f32[3,128,512]{2,1,0:T(8,128)S(1)} %collective-permute-done.15.refs_1_, f32[3,128,512]{2,1,0:T(8,128)S(1)} %get-tuple-element.51._.refs_2_, ...), custom_call_target="tpu_custom_call" | custom-call | flops 1000000000 | bytes 14417920 | tf_op jit(solution)/shard_map/pallas_call | solution.py:206
  31.1 1.6 %collective-permute-start.19 = (f32[3,4,512]{2,1,0:T(4,128)S(1)}, f32[3,4,512]{2,1,0:T(4,128)S(1)}, u32[]{:S(2)}, u32[]{:S(2)}) collective-permute-start(f32[3,4,512]{2,1,0:T(4,128)S(1)} %get-tuple-element.63), channel_id=1, source_target_pairs={{0,16},{16,0},{1,17},{17,1},{2,18},{18,2},{3,19},{19,3},{4,20},{20... | collective-permute-start | bytes 73736 | tf_op jit(solution)/shard_map/ppermute | solution.py:419
  32.7 1.6 %shard_map.160 = (f32[4,128,128]{2,1,0:T(8,128)}, f32[4,128,128]{2,1,0:T(8,128)}, f32[4,128,128]{2,1,0:T(8,128)}, f32[12,128,128]{2,1,0:T(8,128)S(1)}, bf16[12,512,256]{2,1,0:T(8,128)(2,1)S(1)}) custom-call(f32[12,128,128]{2,1,0:T(8,128)S(1)} %get-tuple-element.56.moment_ref, f32[12,128,128]{2,1,0:T(8,128)S(1)} %get-tuple-element.57.kept_ref, ...), custom_call_target="tpu_custom_call" | custom-call | flops 301989888 | bytes 6553600 | tf_op jit(solution)/shard_map/pallas_call | solution.py:206
  34.3 0.7 %collective-permute-done.19 = f32[3,4,512]{2,1,0:T(4,128)S(1)} collective-permute-done((f32[3,4,512]{2,1,0:T(4,128)S(1)}, f32[3,4,512]{2,1,0:T(4,128)S(1)}, u32[]{:S(2)}, u32[]{:S(2)}) %collective-permute-start.19) | collective-permute-done | bytes 24608 | tf_op jit(solution)/shard_map/ppermute | solution.py:419
  35.0 2.0 %shard_map.161 = (f32[4,128,128]{2,1,0:T(8,128)}, f32[4,128,128]{2,1,0:T(8,128)}, f32[4,128,128]{2,1,0:T(8,128)}) custom-call(f32[12,128,128]{2,1,0:T(8,128)S(1)} %get-tuple-element.62.decoded_ref, f32[1,3,4,512]{3,2,1,0:T(4,128)S(1)} %bitcast.12, bf16[12,128,512]{2,1,0:T(8,128)(2,1)S(1)} %get-tuple-element.53.refs_7_.in_row_ref, ...), custom_call_target="tpu_custom_call" | custom-call | flops 301989888 | bytes 11190272 | tf_op jit(solution)/shard_map/pallas_call | solution.py:206
  (6 shorter events, 0.0 us)
Async XLA Ops:
  0.6 7.0 %collective-permute-start.9 = (bf16[128,512]{1,0:T(8,128)(2,1)}, bf16[128,512]{1,0:T(8,128)(2,1)S(1)}, u32[]{:S(2)}, u32[]{:S(2)}) collective-permute-start(bf16[128,512]{1,0:T(8,128)(2,1)} %bitcast.16), channel_id=1, source_target_pairs={{4,0},{5,1},{8,4},{9,5},{12,8},{13,9},{14,12},{15,13},{10,14},{11,... | collective-permute-start | bytes 393224 | tf_op jit(solution)/shard_map/ppermute | solution.py:250
  3.6 4.0 %collective-permute-start.10 = (bf16[4,128,128]{2,1,0:T(8,128)(2,1)}, bf16[4,128,128]{2,1,0:T(8,128)(2,1)S(1)}, u32[]{:S(2)}, u32[]{:S(2)}) collective-permute-start(bf16[4,128,128]{2,1,0:T(8,128)(2,1)} %refs_10_.2), channel_id=1, source_target_pairs={{0,1},{1,0},{2,3},{3,2},{4,5},{5,4},{6,7},{7,6},{8,9},{9,8},{10,11... | collective-permute-start | bytes 393224 | tf_op jit(solution)/shard_map/ppermute | solution.py:250
  3.6 4.0 %copy-start.8 = (bf16[4,128,128]{2,1,0:T(8,128)(2,1)S(1)}, bf16[4,128,128]{2,1,0:T(8,128)(2,1)}, u32[]{:S(2)}) copy-start(bf16[4,128,128]{2,1,0:T(8,128)(2,1)} %refs_11_.2) | copy-start | bytes 393220
  3.6 9.6 %copy-start.9 = (bf16[4,128,128]{2,1,0:T(8,128)(2,1)S(1)}, bf16[4,128,128]{2,1,0:T(8,128)(2,1)}, u32[]{:S(2)}) copy-start(bf16[4,128,128]{2,1,0:T(8,128)(2,1)} %refs_12_.1) | copy-start | bytes 393220
  3.6 18.6 %copy-start.5 = (bf16[1,128,512]{2,1,0:T(8,128)(2,1)S(1)}, bf16[1,128,512]{2,1,0:T(8,128)(2,1)}, u32[]{:S(2)}) copy-start(bf16[1,128,512]{2,1,0:T(8,128)(2,1)} %param.11) | copy-start | bytes 393220
  3.6 18.6 %copy-start.6 = (bf16[1,128,512]{2,1,0:T(8,128)(2,1)S(1)}, bf16[1,128,512]{2,1,0:T(8,128)(2,1)}, u32[]{:S(2)}) copy-start(bf16[1,128,512]{2,1,0:T(8,128)(2,1)} %param.12) | copy-start | bytes 393220
  3.6 18.6 %copy-start.7 = (bf16[4,128,128]{2,1,0:T(8,128)(2,1)S(1)}, bf16[4,128,128]{2,1,0:T(8,128)(2,1)}, u32[]{:S(2)}) copy-start(bf16[4,128,128]{2,1,0:T(8,128)(2,1)} %refs_10_.2) | copy-start | bytes 393220
  3.7 6.6 %collective-permute-start = (bf16[128,512]{1,0:T(8,128)(2,1)}, bf16[128,512]{1,0:T(8,128)(2,1)S(1)}, u32[]{:S(2)}, u32[]{:S(2)}) collective-permute-start(bf16[128,512]{1,0:T(8,128)(2,1)} %bitcast.13), channel_id=1, source_target_pairs={{0,4},{1,5},{4,8},{5,9},{8,12},{9,13},{12,14},{13,15},{14,10},{15,... | collective-permute-start | bytes 393224 | tf_op jit(solution)/shard_map/ppermute | solution.py:250
  3.9 6.5 %collective-permute-start.3 = (bf16[128,512]{1,0:T(8,128)(2,1)}, bf16[128,512]{1,0:T(8,128)(2,1)S(1)}, u32[]{:S(2)}, u32[]{:S(2)}) collective-permute-start(bf16[128,512]{1,0:T(8,128)(2,1)} %bitcast.14), channel_id=1, source_target_pairs={{4,0},{5,1},{8,4},{9,5},{12,8},{13,9},{14,12},{15,13},{10,14},{11,... | collective-permute-start | bytes 393224 | tf_op jit(solution)/shard_map/ppermute | solution.py:250
  5.7 7.3 %collective-permute-start.6 = (bf16[128,512]{1,0:T(8,128)(2,1)}, bf16[128,512]{1,0:T(8,128)(2,1)S(1)}, u32[]{:S(2)}, u32[]{:S(2)}) collective-permute-start(bf16[128,512]{1,0:T(8,128)(2,1)} %bitcast.17), channel_id=1, source_target_pairs={{0,4},{1,5},{4,8},{5,9},{8,12},{9,13},{12,14},{13,15},{14,10},{15,... | collective-permute-start | bytes 393224 | tf_op jit(solution)/shard_map/ppermute | solution.py:250
  7.6 5.6 %collective-permute-start.12 = (bf16[4,128,128]{2,1,0:T(8,128)(2,1)S(1)}, bf16[4,128,128]{2,1,0:T(8,128)(2,1)S(1)}, u32[]{:S(2)}, u32[]{:S(2)}) collective-permute-start(bf16[4,128,128]{2,1,0:T(8,128)(2,1)S(1)} %copy-done.8), channel_id=1, source_target_pairs={{0,1},{1,0},{2,3},{3,2},{4,5},{5,4},{6,7},{7,6},{8,9},{9,8},{10,11... | collective-permute-start | bytes 393224 | tf_op jit(solution)/shard_map/ppermute | solution.py:250
  7.6 6.3 %collective-permute-start.11 = (bf16[128,512]{1,0:T(8,128)(2,1)S(1)}, bf16[128,512]{1,0:T(8,128)(2,1)S(1)}, u32[]{:S(2)}, u32[]{:S(2)}) collective-permute-start(bf16[128,512]{1,0:T(8,128)(2,1)S(1)} %collective-permute-done.9.refs_7_), channel_id=1, source_target_pairs={{4,0},{5,1},{8,4},{9,5},{12,8},{13,9},{14,12},{15,13},{10,14},{11,... | collective-permute-start | bytes 393224 | tf_op jit(solution)/shard_map/ppermute | solution.py:250
  10.2 5.7 %collective-permute-start.1 = (bf16[128,512]{1,0:T(8,128)(2,1)S(1)}, bf16[128,512]{1,0:T(8,128)(2,1)S(1)}, u32[]{:S(2)}, u32[]{:S(2)}) collective-permute-start(bf16[128,512]{1,0:T(8,128)(2,1)S(1)} %collective-permute-done.refs_1_), channel_id=1, source_target_pairs={{0,4},{1,5},{4,8},{5,9},{8,12},{9,13},{12,14},{13,15},{14,10},{15,... | collective-permute-start | bytes 393224 | tf_op jit(solution)/shard_map/ppermute | solution.py:250
  10.4 6.0 %collective-permute-start.4 = (bf16[128,512]{1,0:T(8,128)(2,1)S(1)}, bf16[128,512]{1,0:T(8,128)(2,1)S(1)}, u32[]{:S(2)}, u32[]{:S(2)}) collective-permute-start(bf16[128,512]{1,0:T(8,128)(2,1)S(1)} %collective-permute-done.3.refs_2_), channel_id=1, source_target_pairs={{4,0},{5,1},{8,4},{9,5},{12,8},{13,9},{14,12},{15,13},{10,14},{11,... | collective-permute-start | bytes 393224 | tf_op jit(solution)/shard_map/ppermute | solution.py:250
  13.0 5.6 %collective-permute-start.7 = (bf16[128,512]{1,0:T(8,128)(2,1)S(1)}, bf16[128,512]{1,0:T(8,128)(2,1)S(1)}, u32[]{:S(2)}, u32[]{:S(2)}) collective-permute-start(bf16[128,512]{1,0:T(8,128)(2,1)S(1)} %collective-permute-done.6.refs_6_), channel_id=1, source_target_pairs={{0,4},{1,5},{4,8},{5,9},{8,12},{9,13},{12,14},{13,15},{14,10},{15,... | collective-permute-start | bytes 393224 | tf_op jit(solution)/shard_map/ppermute | solution.py:250
  13.2 5.5 %collective-permute-start.14 = (bf16[4,128,128]{2,1,0:T(8,128)(2,1)S(1)}, bf16[4,128,128]{2,1,0:T(8,128)(2,1)S(1)}, u32[]{:S(2)}, u32[]{:S(2)}) collective-permute-start(bf16[4,128,128]{2,1,0:T(8,128)(2,1)S(1)} %copy-done.9), channel_id=1, source_target_pairs={{0,1},{1,0},{2,3},{3,2},{4,5},{5,4},{6,7},{7,6},{8,9},{9,8},{10,11... | collective-permute-start | bytes 393224 | tf_op jit(solution)/shard_map/ppermute | solution.py:250
  14.0 5.9 %collective-permute-start.13 = (bf16[128,512]{1,0:T(8,128)(2,1)S(1)}, bf16[128,512]{1,0:T(8,128)(2,1)S(1)}, u32[]{:S(2)}, u32[]{:S(2)}) collective-permute-start(bf16[128,512]{1,0:T(8,128)(2,1)S(1)} %collective-permute-done.11.refs_9_), channel_id=1, source_target_pairs={{4,0},{5,1},{8,4},{9,5},{12,8},{13,9},{14,12},{15,13},{10,14},{11,... | collective-permute-start | bytes 393224 | tf_op jit(solution)/shard_map/ppermute | solution.py:250
  15.9 6.3 %collective-permute-start.2 = (bf16[128,512]{1,0:T(8,128)(2,1)S(1)}, bf16[128,512]{1,0:T(8,128)(2,1)S(1)}, u32[]{:S(2)}, u32[]{:S(2)}) collective-permute-start(bf16[128,512]{1,0:T(8,128)(2,1)S(1)} %collective-permute-done.1.refs_3_), channel_id=1, source_target_pairs={{0,4},{1,5},{4,8},{5,9},{8,12},{9,13},{12,14},{13,15},{14,10},{15,... | collective-permute-start | bytes 393224 | tf_op jit(solution)/shard_map/ppermute | solution.py:250
  16.4 7.4 %collective-permute-start.5 = (bf16[128,512]{1,0:T(8,128)(2,1)S(1)}, bf16[128,512]{1,0:T(8,128)(2,1)S(1)}, u32[]{:S(2)}, u32[]{:S(2)}) collective-permute-start(bf16[128,512]{1,0:T(8,128)(2,1)S(1)} %collective-permute-done.4.refs_4_), channel_id=1, source_target_pairs={{4,0},{5,1},{8,4},{9,5},{12,8},{13,9},{14,12},{15,13},{10,14},{11,... | collective-permute-start | bytes 393224 | tf_op jit(solution)/shard_map/ppermute | solution.py:250
  18.6 6.5 %collective-permute-start.8 = (bf16[128,512]{1,0:T(8,128)(2,1)S(1)}, bf16[128,512]{1,0:T(8,128)(2,1)S(1)}, u32[]{:S(2)}, u32[]{:S(2)}) collective-permute-start(bf16[128,512]{1,0:T(8,128)(2,1)S(1)} %collective-permute-done.7.refs_8_), channel_id=1, source_target_pairs={{0,4},{1,5},{4,8},{5,9},{8,12},{9,13},{12,14},{13,15},{14,10},{15,... | collective-permute-start | bytes 393224 | tf_op jit(solution)/shard_map/ppermute | solution.py:250
  19.9 7.3 %collective-permute-start.17 = (bf16[128,512]{1,0:T(8,128)(2,1)S(1)}, bf16[128,512]{1,0:T(8,128)(2,1)S(1)}, u32[]{:S(2)}, u32[]{:S(2)}) collective-permute-start(bf16[128,512]{1,0:T(8,128)(2,1)S(1)} %collective-permute-done.13.refs_3_), channel_id=1, source_target_pairs={{4,0},{5,1},{8,4},{9,5},{12,8},{13,9},{14,12},{15,13},{10,14},{11,... | collective-permute-start | bytes 393224 | tf_op jit(solution)/shard_map/ppermute | solution.py:250
  22.2 5.0 %collective-permute-start.16 = (bf16[128,512]{1,0:T(8,128)(2,1)S(1)}, bf16[128,512]{1,0:T(8,128)(2,1)S(1)}, u32[]{:S(2)}, u32[]{:S(2)}) collective-permute-start(bf16[128,512]{1,0:T(8,128)(2,1)S(1)} %collective-permute-done.2.refs_0_), channel_id=1, source_target_pairs={{0,4},{1,5},{4,8},{5,9},{8,12},{9,13},{12,14},{13,15},{14,10},{15,... | collective-permute-start | bytes 393224 | tf_op jit(solution)/shard_map/ppermute | solution.py:250
  25.9 2.1 %copy-start.10 = (s32[3,4,512]{2,1,0:T(4,128)S(1)}, s32[3,4,512]{2,1,0:T(4,128)}, u32[]{:S(2)}) copy-start(s32[3,4,512]{2,1,0:T(4,128)} %index_ref.1) | copy-start | bytes 73732
  25.9 3.8 %collective-permute-start.15 = (f32[3,128,512]{2,1,0:T(8,128)S(1)}, f32[3,128,512]{2,1,0:T(8,128)S(1)}, u32[]{:S(2)}, u32[]{:S(2)}) collective-permute-start(f32[3,128,512]{2,1,0:T(8,128)S(1)} %get-tuple-element.49), channel_id=1, source_target_pairs={{0,1},{1,0},{2,3},{3,2},{4,5},{5,4},{6,7},{7,6},{8,9},{9,8},{10,11... | collective-permute-start | bytes 2359304 | tf_op jit(solution)/shard_map/ppermute | solution.py:250
  28.0 1.8 %collective-permute-start.18 = (bf16[3,128,512]{2,1,0:T(8,128)(2,1)S(1)}, bf16[3,128,512]{2,1,0:T(8,128)(2,1)S(1)}, u32[]{:S(2)}, u32[]{:S(2)}) collective-permute-start(bf16[3,128,512]{2,1,0:T(8,128)(2,1)S(1)} %get-tuple-element.52), channel_id=1, source_target_pairs={{0,1},{1,0},{2,3},{3,2},{4,5},{5,4},{6,7},{7,6},{8,9},{9,8},{10,11... | collective-permute-start | bytes 1179656 | tf_op jit(solution)/shard_map/ppermute | solution.py:250
  28.1 1.7 %copy-start = (f32[128,128]{1,0:T(8,128)S(1)}, f32[128,128]{1,0:T(8,128)}, u32[]{:S(2)}) copy-start(f32[128,128]{1,0:T(8,128)} %constant.5.clone.refs_11_.cosines_t_ref) | copy-start | bytes 196612
  28.1 1.7 %copy-start.1 = (f32[1,4,128,128]{3,2,1,0:T(8,128)S(1)}, f32[1,4,128,128]{3,2,1,0:T(8,128)}, u32[]{:S(2)}) copy-start(f32[1,4,128,128]{3,2,1,0:T(8,128)} %param.16) | copy-start | bytes 786436
  28.1 1.7 %copy-start.2 = (f32[1,4,128,128]{3,2,1,0:T(8,128)S(1)}, f32[1,4,128,128]{3,2,1,0:T(8,128)}, u32[]{:S(2)}) copy-start(f32[1,4,128,128]{3,2,1,0:T(8,128)} %param.17) | copy-start | bytes 786436
  28.1 1.7 %copy-start.3 = (f32[1,4,128,128]{3,2,1,0:T(8,128)S(1)}, f32[1,4,128,128]{3,2,1,0:T(8,128)}, u32[]{:S(2)}) copy-start(f32[1,4,128,128]{3,2,1,0:T(8,128)} %param.18) | copy-start | bytes 786436
  28.1 1.7 %copy-start.4 = (f32[128,128]{1,0:T(8,128)S(1)}, f32[128,128]{1,0:T(8,128)}, u32[]{:S(2)}) copy-start(f32[128,128]{1,0:T(8,128)} %constant.4.clone.refs_10_.cosines_ref) | copy-start | bytes 196612
  31.1 3.9 %collective-permute-start.19 = (f32[3,4,512]{2,1,0:T(4,128)S(1)}, f32[3,4,512]{2,1,0:T(4,128)S(1)}, u32[]{:S(2)}, u32[]{:S(2)}) collective-permute-start(f32[3,4,512]{2,1,0:T(4,128)S(1)} %get-tuple-element.63), channel_id=1, source_target_pairs={{0,16},{16,0},{1,17},{17,1},{2,18},{18,2},{3,19},{19,3},{4,20},{20... | collective-permute-start | bytes 73736 | tf_op jit(solution)/shard_map/ppermute | solution.py:419

commit v3 on v2

--- a/solution.py
+++ b/solution.py
@@ -9,8 +9,8 @@
 from jax.sharding import PartitionSpec as P
 
 MOMENTUM_DECAY = 0.999
-LATE_FLOPS = 4 * 10**9
-TABLES_FLOPS = 10**9
+
+TABLES_FLOPS = 10**10
 PAUSE_FLOPS = 10**9
 F32 = jnp.float32
 BF16 = jnp.bfloat16
@@ -58,7 +58,8 @@
     return d_gate, (dh * swish).astype(BF16), (swish * up).astype(BF16)
 
 
-def tables_kernel(index_ref, _, in_row_ref, in_col_ref, in_col_t_ref, mask_ref):
+def tables_kernel(index_ref, *refs):
+    in_row_ref, in_col_ref, in_col_t_ref, mask_ref = refs[-4:]
     side = mask_ref.shape[1]
     shift = int(np.log2(side))
     matrices, count, keep = index_ref.shape
@@ -151,18 +152,20 @@
             )
 
 
-def late_kernel(x_ref, d_ref, wgu_ref, wd_ref, own_ref, par_ref):
+def late_kernel(*refs):
+    xs, ds, wgu_ref, wd_ref, own_ref, got_ref = refs[:2], refs[2:4], *refs[4:8]
     side = own_ref.shape[1]
-    x, d = x_ref[...], d_ref[...]
-    d_gate, d_up, hidden = activations(wgu_ref[...], wd_ref[...], x, d)
-    for m, grad in enumerate((dot(d_gate, x), dot(d_up, x), dot(hidden, d))):
-        own_ref[m] = grad[:side]
-        par_ref[m] = grad[side:].astype(BF16)
-
-
-def moment_kernel(terms, *refs):
-    grads = [sum(ref[m].astype(F32) for ref in refs[:terms]) for m in range(3)]
-    moment_step(grads, refs[terms : terms + 3], *refs[terms + 3 :])
+    x = jnp.concatenate([ref[...] for ref in xs], axis=0)
+    d = jnp.concatenate([ref[...] for ref in ds], axis=0)
+    wgu = jnp.concatenate([wgu_ref[:side, :], wgu_ref[2 * side : 3 * side, :]], axis=0)
+    d_gate, d_up, hidden = activations(wgu, wd_ref[:side, :], x, d)
+    late = (dot(d_gate, x), dot(d_up, x), dot(hidden, d))
+    grads = [late[m] + (own_ref[m] + got_ref[m]) for m in range(3)]
+    moment_step(grads, refs[8:11], *refs[11:])
+
+
+def moment_kernel(grad_ref, *refs):
+    moment_step([grad_ref[m] for m in range(3)], refs[:3], *refs[3:])
 
 
 def residual_kernel(moment_ref, kept_ref, in_col_t_ref, cosines_ref, cosines_t_ref, *outs):
@@ -222,7 +225,7 @@
     return forward, [(b, a) for a, b in forward], chips
 
 
-def band_tables(band_index, side, ahead):
+def band_tables(band_index, side, *ahead):
     blocks, keep = band_index.shape[0] * band_index.shape[1], band_index.shape[2]
     return call(
         tables_kernel,
@@ -234,8 +237,8 @@
         ),
         TABLES_FLOPS,
         band_index,
-        ahead,
-        in_place={1: pl.ANY},
+        *ahead,
+        in_place=dict.fromkeys(range(1, 1 + len(ahead)), pl.ANY),
     )
 
 
@@ -308,24 +311,21 @@
         partner,
         scratch=scratch(2),
     )
-    own_late, partner_late = call(
+    got = send(partner, swap)
+    x_swap, d_swap = send(x_last, swap), send(d_last, swap)
+    in_row, in_col, in_col_t, mask = band_tables(band_index, side, x_last, d_last)
+    moments = call(
         late_kernel,
-        (part, jax.ShapeDtypeStruct(part.shape, BF16)),
-        LATE_FLOPS,
+        shapes,
+        10**9,
         x_last,
+        x_swap,
         d_last,
+        d_swap,
         wgu,
         wd,
-    )
-    in_row, in_col, in_col_t, mask = band_tables(band_index, side, own_late)
-    moments = call(
-        functools.partial(moment_kernel, 4),
-        shapes,
-        10**9,
         own,
-        send(partner, swap),
-        own_late,
-        send(partner_late, swap),
+        got,
         *momenta,
         in_row,
         in_col,
@@ -341,7 +341,7 @@
     own = shared_column_grads(x, d, gate_weight, up_weight, down_weight)
     in_row, in_col, in_col_t, mask = band_tables(band_index, cosines.shape[0], own)
     moments = call(
-        functools.partial(moment_kernel, 1),
+        moment_kernel,
         shapes,
         0,
         own,

time: 37.2 us -> 36.7 us (0.987)
  waiting for transfers between devices: 10.4 us -> 9.83 us
  starting transfers between devices: 16.6 us -> 17 us
    ppermute x19 -> x20, waiting for transfers between devices: 9.69 us -> 9.1 us  [send(): return lax.ppermute(value, 'fsdp', perm)]
    ppermute x19 -> x20, starting transfers between devices: 15 us -> 15.4 us  [send(): return lax.ppermute(value, 'fsdp', perm)]
    pallas_call x8 -> x7, Pallas kernels: 9.16 us -> 8.85 us  [call(): pl.pallas_call(kernel, out_shape=out_shape, in_specs=specs, scratch_shape...]
  transfers between devices with their start and end apart: 20 -> 21, of which waited for: 13 -> 12; matrix products, arithmetic and copies ran while one was open for 0% -> 0% of each run, Pallas kernels for 16% -> 14%
where the time goes in v3:
time: 36.7 us; the launch traced here: 36.6 us
  starting transfers between devices  17 us (46%)
  waiting for transfers between devices  9.83 us (27%)
  Pallas kernels  8.85 us (24%)
  between operations  0.84 us (2%)
    ppermute x20, starting transfers between devices, send(): return lax.ppermute(value, 'fsdp', perm)  15.4 us
    ppermute x20, waiting for transfers between devices, send(): return lax.ppermute(value, 'fsdp', perm)  9.1 us
    pallas_call x7, Pallas kernels, call(): pl.pallas_call(kernel, out_shape=out_shape, in_specs=specs, scratch_shape...  8.85 us
    ppermute x1, starting transfers between devices, per_device(): lax.ppermute(band, 'rep', [(r, (r + s) % reps) for r in range(reps)])  1.58 us
  transfers between devices with their start and end apart: 21, of which 12 were waited for; matrix products, arithmetic and copies ran while one was open for 0% of the time, Pallas kernels for 14%

profile of v3, /device:TPU:0, one launch (start us, length us, event | category | flops | bytes accessed | tf_op | source)
XLA Modules:
  0.0 36.6 jit_solution(18177386061616797142)
XLA Ops:
  0.6 3.0 %collective-permute-start.5 = (bf16[128,512]{1,0:T(8,128)(2,1)}, bf16[128,512]{1,0:T(8,128)(2,1)S(1)}, u32[]{:S(2)}, u32[]{:S(2)}) collective-permute-start(bf16[128,512]{1,0:T(8,128)(2,1)} %bitcast.16), channel_id=1, source_target_pairs={{4,0},{5,1},{8,4},{9,5},{12,8},{13,9},{14,12},{15,13},{10,14},{11,... | collective-permute-start | bytes 393224 | tf_op jit(solution)/shard_map/ppermute | solution.py:253
  3.6 0.0 collective-permute-start.6
  3.6 0.0 copy-start.6
  3.6 0.0 copy-start.7
  3.7 0.2 collective-permute-start
  3.9 1.8 %collective-permute-start.13 = (bf16[128,512]{1,0:T(8,128)(2,1)}, bf16[128,512]{1,0:T(8,128)(2,1)S(1)}, u32[]{:S(2)}, u32[]{:S(2)}) collective-permute-start(bf16[128,512]{1,0:T(8,128)(2,1)} %bitcast.14), channel_id=1, source_target_pairs={{4,0},{5,1},{8,4},{9,5},{12,8},{13,9},{14,12},{15,13},{10,14},{11,... | collective-permute-start | bytes 393224 | tf_op jit(solution)/shard_map/ppermute | solution.py:253
  5.7 0.2 collective-permute-start.15
  5.9 1.7 %collective-permute-done.5.refs_7_ = bf16[128,512]{1,0:T(8,128)(2,1)S(1)} collective-permute-done((bf16[128,512]{1,0:T(8,128)(2,1)}, bf16[128,512]{1,0:T(8,128)(2,1)S(1)}, u32[]{:S(2)}, u32[]{:S(2)}) %collective-permute-start.5) | collective-permute-done | bytes 131104 | tf_op jit(solution)/shard_map/ppermute | solution.py:253
  7.6 0.0 copy-done.8
  7.6 0.0 collective-permute-start.8
  7.6 0.0 collective-permute-done.6.refs_13_
  7.6 1.8 %collective-permute-start.7 = (bf16[128,512]{1,0:T(8,128)(2,1)S(1)}, bf16[128,512]{1,0:T(8,128)(2,1)S(1)}, u32[]{:S(2)}, u32[]{:S(2)}) collective-permute-start(bf16[128,512]{1,0:T(8,128)(2,1)S(1)} %collective-permute-done.5.refs_7_), channel_id=1, source_target_pairs={{4,0},{5,1},{8,4},{9,5},{12,8},{13,9},{14,12},{15,13},{10,14},{11,... | collective-permute-start | bytes 393224 | tf_op jit(solution)/shard_map/ppermute | solution.py:253
  9.4 0.8 %collective-permute-done.refs_1_ = bf16[128,512]{1,0:T(8,128)(2,1)S(1)} collective-permute-done((bf16[128,512]{1,0:T(8,128)(2,1)}, bf16[128,512]{1,0:T(8,128)(2,1)S(1)}, u32[]{:S(2)}, u32[]{:S(2)}) %collective-permute-start) | collective-permute-done | bytes 131104 | tf_op jit(solution)/shard_map/ppermute | solution.py:253
  10.2 0.2 collective-permute-start.1
  10.4 0.0 collective-permute-done.13.refs_2_
  10.4 1.8 %collective-permute-start.14 = (bf16[128,512]{1,0:T(8,128)(2,1)S(1)}, bf16[128,512]{1,0:T(8,128)(2,1)S(1)}, u32[]{:S(2)}, u32[]{:S(2)}) collective-permute-start(bf16[128,512]{1,0:T(8,128)(2,1)S(1)} %collective-permute-done.13.refs_2_), channel_id=1, source_target_pairs={{4,0},{5,1},{8,4},{9,5},{12,8},{13,9},{14,12},{15,13},{10,14},{11,... | collective-permute-start | bytes 393224 | tf_op jit(solution)/shard_map/ppermute | solution.py:253
  12.2 0.8 %collective-permute-done.15.refs_6_ = bf16[128,512]{1,0:T(8,128)(2,1)S(1)} collective-permute-done((bf16[128,512]{1,0:T(8,128)(2,1)}, bf16[128,512]{1,0:T(8,128)(2,1)S(1)}, u32[]{:S(2)}, u32[]{:S(2)}) %collective-permute-start.15) | collective-permute-done | bytes 131104 | tf_op jit(solution)/shard_map/ppermute | solution.py:253
  13.0 0.2 collective-permute-start.16
  13.2 0.0 collective-permute-done.8.refs_14_
  13.2 0.0 copy-done.9
  13.2 0.0 collective-permute-start.10
  13.2 0.8 %collective-permute-done.7.refs_9_ = bf16[128,512]{1,0:T(8,128)(2,1)S(1)} collective-permute-done((bf16[128,512]{1,0:T(8,128)(2,1)S(1)}, bf16[128,512]{1,0:T(8,128)(2,1)S(1)}, u32[]{:S(2)}, u32[]{:S(2)}) %collective-permute-start.7) | collective-permute-done | bytes 131104 | tf_op jit(solution)/shard_map/ppermute | solution.py:253
  14.0 1.7 %collective-permute-start.9 = (bf16[128,512]{1,0:T(8,128)(2,1)S(1)}, bf16[128,512]{1,0:T(8,128)(2,1)S(1)}, u32[]{:S(2)}, u32[]{:S(2)}) collective-permute-start(bf16[128,512]{1,0:T(8,128)(2,1)S(1)} %collective-permute-done.7.refs_9_), channel_id=1, source_target_pairs={{4,0},{5,1},{8,4},{9,5},{12,8},{13,9},{14,12},{15,13},{10,14},{11,... | collective-permute-start | bytes 393224 | tf_op jit(solution)/shard_map/ppermute | solution.py:253
  15.7 0.2 collective-permute-done.1.refs_3_
  15.9 0.2 collective-permute-start.2
  16.1 0.3 collective-permute-done.14.refs_4_
  16.4 1.7 %collective-permute-start.17 = (bf16[128,512]{1,0:T(8,128)(2,1)S(1)}, bf16[128,512]{1,0:T(8,128)(2,1)S(1)}, u32[]{:S(2)}, u32[]{:S(2)}) collective-permute-start(bf16[128,512]{1,0:T(8,128)(2,1)S(1)} %collective-permute-done.14.refs_4_), channel_id=1, source_target_pairs={{4,0},{5,1},{8,4},{9,5},{12,8},{13,9},{14,12},{15,13},{10,14},{11,... | collective-permute-start | bytes 393224 | tf_op jit(solution)/shard_map/ppermute | solution.py:253
  18.1 0.5 %collective-permute-done.16.refs_8_ = bf16[128,512]{1,0:T(8,128)(2,1)S(1)} collective-permute-done((bf16[128,512]{1,0:T(8,128)(2,1)S(1)}, bf16[128,512]{1,0:T(8,128)(2,1)S(1)}, u32[]{:S(2)}, u32[]{:S(2)}) %collective-permute-start.16) | collective-permute-done | bytes 131104 | tf_op jit(solution)/shard_map/ppermute | solution.py:253
  18.6 0.1 collective-permute-start.18
  18.7 0.0 collective-permute-done.10.refs_15_
  18.7 1.2 %collective-permute-done.9.refs_3_ = bf16[128,512]{1,0:T(8,128)(2,1)S(1)} collective-permute-done((bf16[128,512]{1,0:T(8,128)(2,1)S(1)}, bf16[128,512]{1,0:T(8,128)(2,1)S(1)}, u32[]{:S(2)}, u32[]{:S(2)}) %collective-permute-start.9) | collective-permute-done | bytes 131104 | tf_op jit(solution)/shard_map/ppermute | solution.py:253
  19.9 1.9 %collective-permute-start.11 = (bf16[128,512]{1,0:T(8,128)(2,1)S(1)}, bf16[128,512]{1,0:T(8,128)(2,1)S(1)}, u32[]{:S(2)}, u32[]{:S(2)}) collective-permute-start(bf16[128,512]{1,0:T(8,128)(2,1)S(1)} %collective-permute-done.9.refs_3_), channel_id=1, source_target_pairs={{4,0},{5,1},{8,4},{9,5},{12,8},{13,9},{14,12},{15,13},{10,14},{11,... | collective-permute-start | bytes 393224 | tf_op jit(solution)/shard_map/ppermute | solution.py:253
  21.8 0.4 %collective-permute-done.2.refs_0_ = bf16[128,512]{1,0:T(8,128)(2,1)S(1)} collective-permute-done((bf16[128,512]{1,0:T(8,128)(2,1)S(1)}, bf16[128,512]{1,0:T(8,128)(2,1)S(1)}, u32[]{:S(2)}, u32[]{:S(2)}) %collective-permute-start.2) | collective-permute-done | bytes 131104 | tf_op jit(solution)/shard_map/ppermute | solution.py:253
  22.2 0.0 collective-permute-start.3
  22.2 0.0 copy-done.5
  22.2 0.0 copy-done.6
  22.3 0.0 copy-done.7
  22.3 1.5 %shard_map.155 = (f32[3,128,512]{2,1,0:T(8,128)S(1)}, f32[3,128,512]{2,1,0:T(8,128)S(1)}, bf16[512,512]{1,0:T(8,128)(2,1)S(1)}, bf16[256,512]{1,0:T(8,128)(2,1)S(1)}) custom-call(bf16[128,512]{1,0:T(8,128)(2,1)S(1)} %bitcast.15, bf16[128,512]{1,0:T(8,128)(2,1)S(1)} %collective-permute-done.refs_1_, bf16[128,512]{1,0:T(8,128)(2,1)S(1)} %collective-permute-done.13.refs_2_, ...), custom_call_target="tpu_custom_call" | custom-call | flops 1006632960 | bytes 4202496 | tf_op jit(solution)/shard_map/pallas_call | solution.py:209
  23.8 0.0 copy-start.10
  23.8 0.0 collective-permute-done.17.refs_1_
  23.8 1.2 %collective-permute-done.18.refs_2_ = bf16[128,512]{1,0:T(8,128)(2,1)S(1)} collective-permute-done((bf16[128,512]{1,0:T(8,128)(2,1)S(1)}, bf16[128,512]{1,0:T(8,128)(2,1)S(1)}, u32[]{:S(2)}, u32[]{:S(2)}) %collective-permute-start.18) | collective-permute-done | bytes 131104 | tf_op jit(solution)/shard_map/ppermute | solution.py:253
  25.0 0.9 %shard_map.156 = (f32[3,128,512]{2,1,0:T(8,128)S(1)}, f32[3,128,512]{2,1,0:T(8,128)S(1)}) custom-call(bf16[128,512]{1,0:T(8,128)(2,1)S(1)} %collective-permute-done.2.refs_0_, bf16[128,512]{1,0:T(8,128)(2,1)S(1)} %collective-permute-done.17.refs_1_, bf16[128,512]{1,0:T(8,128)(2,1)S(1)} %collective-permute-done.18.refs_2_, ...), custom_call_target="tpu_custom_call" | custom-call | flops 402653184 | bytes 5767168 | tf_op jit(solution)/shard_map/pallas_call | solution.py:209
  25.9 0.0 copy-start
  25.9 0.0 copy-start.1
  25.9 0.0 copy-start.2
  26.0 0.0 copy-start.3
  26.0 0.0 copy-start.4
  26.0 0.1 collective-permute-start.19
  26.1 1.1 %collective-permute-done.3.refs_0_ = bf16[128,512]{1,0:T(8,128)(2,1)S(1)} collective-permute-done((bf16[128,512]{1,0:T(8,128)(2,1)S(1)}, bf16[128,512]{1,0:T(8,128)(2,1)S(1)}, u32[]{:S(2)}, u32[]{:S(2)}) %collective-permute-start.3) | collective-permute-done | bytes 131104 | tf_op jit(solution)/shard_map/ppermute | solution.py:253
  27.2 0.0 collective-permute-start.4
  27.2 0.0 collective-permute-done.11.refs_1_.refs_2_
  27.2 0.5 %collective-permute-start.12 = (bf16[128,512]{1,0:T(8,128)(2,1)S(1)}, bf16[128,512]{1,0:T(8,128)(2,1)S(1)}, u32[]{:S(2)}, u32[]{:S(2)}) collective-permute-start(bf16[128,512]{1,0:T(8,128)(2,1)S(1)} %collective-permute-done.11.refs_1_.refs_2_), channel_id=1, source_target_pairs={{0,1},{1,0},{2,3},{3,2},{4,5},{5,4},{6,7},{7,6},{8,9},{9,8},{10,11... | collective-permute-start | bytes 393224 | tf_op jit(solution)/shard_map/ppermute | solution.py:253
  27.7 0.0 copy-done.10
  27.7 1.1 %shard_map.157 = (bf16[12,128,512]{2,1,0:T(8,128)(2,1)S(1)}, bf16[12,128,512]{2,1,0:T(8,128)(2,1)S(1)}, bf16[12,512,128]{2,1,0:T(8,128)(2,1)S(1)}, bf16[12,128,128]{2,1,0:T(8,128)(2,1)S(1)}) custom-call(s32[3,4,512]{2,1,0:T(4,128)S(1)} %copy-done.10, bf16[128,512]{1,0:T(8,128)(2,1)S(1)} %collective-permute-done.3.refs_0_, ...), custom_call_target="tpu_custom_call" | custom-call | flops 10000000000 | bytes 573440 | tf_op jit(solution)/shard_map/pallas_call | solution.py:209
  28.8 0.0 collective-permute-done.4.refs_1_
  28.8 0.0 collective-permute-done.12.refs_3_
  28.8 0.0 collective-permute-done.19.refs_7_
  28.9 0.0 copy-done
  28.9 0.0 copy-done.1
  28.9 1.8 %shard_map.158 = (f32[12,128,128]{2,1,0:T(8,128)S(1)}, f32[12,128,128]{2,1,0:T(8,128)S(1)}, f32[3,4,512]{2,1,0:T(4,128)S(1)}) custom-call(bf16[128,512]{1,0:T(8,128)(2,1)S(1)} %collective-permute-done.3.refs_0_, bf16[128,512]{1,0:T(8,128)(2,1)S(1)} %collective-permute-done.4.refs_1_, bf16[128,512]{1,0:T(8,128)(2,1)S(1)} %collective-permute-done.11.refs_1_.refs_2_, ...), custom_call_target="tpu_custom_call" | custom-call | flops 1000000000 | bytes 14680064 | tf_op jit(solution)/shard_map/pallas_call | solution.py:209
  30.7 1.6 %collective-permute-start.20 = (f32[3,4,512]{2,1,0:T(4,128)S(1)}, f32[3,4,512]{2,1,0:T(4,128)S(1)}, u32[]{:S(2)}, u32[]{:S(2)}) collective-permute-start(f32[3,4,512]{2,1,0:T(4,128)S(1)} %get-tuple-element.59), channel_id=1, source_target_pairs={{0,16},{16,0},{1,17},{17,1},{2,18},{18,2},{3,19},{19,3},{4,20},{20... | collective-permute-start | bytes 73736 | tf_op jit(solution)/shard_map/ppermute | solution.py:419
  32.3 1.6 %shard_map.159 = (f32[4,128,128]{2,1,0:T(8,128)}, f32[4,128,128]{2,1,0:T(8,128)}, f32[4,128,128]{2,1,0:T(8,128)}, f32[12,128,128]{2,1,0:T(8,128)S(1)}, bf16[12,512,256]{2,1,0:T(8,128)(2,1)S(1)}) custom-call(f32[12,128,128]{2,1,0:T(8,128)S(1)} %get-tuple-element.52.moment_ref, f32[12,128,128]{2,1,0:T(8,128)S(1)} %get-tuple-element.53.kept_ref, ...), custom_call_target="tpu_custom_call" | custom-call | flops 301989888 | bytes 6553600 | tf_op jit(solution)/shard_map/pallas_call | solution.py:209
  33.9 0.7 %collective-permute-done.20 = f32[3,4,512]{2,1,0:T(4,128)S(1)} collective-permute-done((f32[3,4,512]{2,1,0:T(4,128)S(1)}, f32[3,4,512]{2,1,0:T(4,128)S(1)}, u32[]{:S(2)}, u32[]{:S(2)}) %collective-permute-start.20) | collective-permute-done | bytes 24608 | tf_op jit(solution)/shard_map/ppermute | solution.py:419
  34.6 2.0 %shard_map.160 = (f32[4,128,128]{2,1,0:T(8,128)}, f32[4,128,128]{2,1,0:T(8,128)}, f32[4,128,128]{2,1,0:T(8,128)}) custom-call(f32[12,128,128]{2,1,0:T(8,128)S(1)} %get-tuple-element.58.decoded_ref, f32[1,3,4,512]{3,2,1,0:T(4,128)S(1)} %bitcast.12, bf16[12,128,512]{2,1,0:T(8,128)(2,1)S(1)} %get-tuple-element.49.refs_11_.in_row_ref, ...), custom_call_target="tpu_custom_call" | custom-call | flops 301989888 | bytes 11190272 | tf_op jit(solution)/shard_map/pallas_call | solution.py:209
  (7 shorter events, 0.0 us)
Async XLA Ops:
  0.6 7.0 %collective-permute-start.5 = (bf16[128,512]{1,0:T(8,128)(2,1)}, bf16[128,512]{1,0:T(8,128)(2,1)S(1)}, u32[]{:S(2)}, u32[]{:S(2)}) collective-permute-start(bf16[128,512]{1,0:T(8,128)(2,1)} %bitcast.16), channel_id=1, source_target_pairs={{4,0},{5,1},{8,4},{9,5},{12,8},{13,9},{14,12},{15,13},{10,14},{11,... | collective-permute-start | bytes 393224 | tf_op jit(solution)/shard_map/ppermute | solution.py:253
  3.6 4.0 %collective-permute-start.6 = (bf16[4,128,128]{2,1,0:T(8,128)(2,1)}, bf16[4,128,128]{2,1,0:T(8,128)(2,1)S(1)}, u32[]{:S(2)}, u32[]{:S(2)}) collective-permute-start(bf16[4,128,128]{2,1,0:T(8,128)(2,1)} %refs_10_.1), channel_id=1, source_target_pairs={{0,1},{1,0},{2,3},{3,2},{4,5},{5,4},{6,7},{7,6},{8,9},{9,8},{10,11... | collective-permute-start | bytes 393224 | tf_op jit(solution)/shard_map/ppermute | solution.py:253
  3.6 4.0 %copy-start.8 = (bf16[4,128,128]{2,1,0:T(8,128)(2,1)S(1)}, bf16[4,128,128]{2,1,0:T(8,128)(2,1)}, u32[]{:S(2)}) copy-start(bf16[4,128,128]{2,1,0:T(8,128)(2,1)} %refs_11_.1) | copy-start | bytes 393220
  3.6 9.6 %copy-start.9 = (bf16[4,128,128]{2,1,0:T(8,128)(2,1)S(1)}, bf16[4,128,128]{2,1,0:T(8,128)(2,1)}, u32[]{:S(2)}) copy-start(bf16[4,128,128]{2,1,0:T(8,128)(2,1)} %refs_12_.1) | copy-start | bytes 393220
  3.6 18.6 %copy-start.5 = (bf16[1,128,512]{2,1,0:T(8,128)(2,1)S(1)}, bf16[1,128,512]{2,1,0:T(8,128)(2,1)}, u32[]{:S(2)}) copy-start(bf16[1,128,512]{2,1,0:T(8,128)(2,1)} %param.11) | copy-start | bytes 393220
  3.6 18.6 %copy-start.6 = (bf16[1,128,512]{2,1,0:T(8,128)(2,1)S(1)}, bf16[1,128,512]{2,1,0:T(8,128)(2,1)}, u32[]{:S(2)}) copy-start(bf16[1,128,512]{2,1,0:T(8,128)(2,1)} %param.12) | copy-start | bytes 393220
  3.6 18.6 %copy-start.7 = (bf16[4,128,128]{2,1,0:T(8,128)(2,1)S(1)}, bf16[4,128,128]{2,1,0:T(8,128)(2,1)}, u32[]{:S(2)}) copy-start(bf16[4,128,128]{2,1,0:T(8,128)(2,1)} %refs_10_.1) | copy-start | bytes 393220
  3.7 6.6 %collective-permute-start = (bf16[128,512]{1,0:T(8,128)(2,1)}, bf16[128,512]{1,0:T(8,128)(2,1)S(1)}, u32[]{:S(2)}, u32[]{:S(2)}) collective-permute-start(bf16[128,512]{1,0:T(8,128)(2,1)} %bitcast.13), channel_id=1, source_target_pairs={{0,4},{1,5},{4,8},{5,9},{8,12},{9,13},{12,14},{13,15},{14,10},{15,... | collective-permute-start | bytes 393224 | tf_op jit(solution)/shard_map/ppermute | solution.py:253
  3.9 6.5 %collective-permute-start.13 = (bf16[128,512]{1,0:T(8,128)(2,1)}, bf16[128,512]{1,0:T(8,128)(2,1)S(1)}, u32[]{:S(2)}, u32[]{:S(2)}) collective-permute-start(bf16[128,512]{1,0:T(8,128)(2,1)} %bitcast.14), channel_id=1, source_target_pairs={{4,0},{5,1},{8,4},{9,5},{12,8},{13,9},{14,12},{15,13},{10,14},{11,... | collective-permute-start | bytes 393224 | tf_op jit(solution)/shard_map/ppermute | solution.py:253
  5.7 7.3 %collective-permute-start.15 = (bf16[128,512]{1,0:T(8,128)(2,1)}, bf16[128,512]{1,0:T(8,128)(2,1)S(1)}, u32[]{:S(2)}, u32[]{:S(2)}) collective-permute-start(bf16[128,512]{1,0:T(8,128)(2,1)} %bitcast.17), channel_id=1, source_target_pairs={{0,4},{1,5},{4,8},{5,9},{8,12},{9,13},{12,14},{13,15},{14,10},{15,... | collective-permute-start | bytes 393224 | tf_op jit(solution)/shard_map/ppermute | solution.py:253
  7.6 5.6 %collective-permute-start.8 = (bf16[4,128,128]{2,1,0:T(8,128)(2,1)S(1)}, bf16[4,128,128]{2,1,0:T(8,128)(2,1)S(1)}, u32[]{:S(2)}, u32[]{:S(2)}) collective-permute-start(bf16[4,128,128]{2,1,0:T(8,128)(2,1)S(1)} %copy-done.8), channel_id=1, source_target_pairs={{0,1},{1,0},{2,3},{3,2},{4,5},{5,4},{6,7},{7,6},{8,9},{9,8},{10,11... | collective-permute-start | bytes 393224 | tf_op jit(solution)/shard_map/ppermute | solution.py:253
  7.6 6.3 %collective-permute-start.7 = (bf16[128,512]{1,0:T(8,128)(2,1)S(1)}, bf16[128,512]{1,0:T(8,128)(2,1)S(1)}, u32[]{:S(2)}, u32[]{:S(2)}) collective-permute-start(bf16[128,512]{1,0:T(8,128)(2,1)S(1)} %collective-permute-done.5.refs_7_), channel_id=1, source_target_pairs={{4,0},{5,1},{8,4},{9,5},{12,8},{13,9},{14,12},{15,13},{10,14},{11,... | collective-permute-start | bytes 393224 | tf_op jit(solution)/shard_map/ppermute | solution.py:253
  10.2 5.7 %collective-permute-start.1 = (bf16[128,512]{1,0:T(8,128)(2,1)S(1)}, bf16[128,512]{1,0:T(8,128)(2,1)S(1)}, u32[]{:S(2)}, u32[]{:S(2)}) collective-permute-start(bf16[128,512]{1,0:T(8,128)(2,1)S(1)} %collective-permute-done.refs_1_), channel_id=1, source_target_pairs={{0,4},{1,5},{4,8},{5,9},{8,12},{9,13},{12,14},{13,15},{14,10},{15,... | collective-permute-start | bytes 393224 | tf_op jit(solution)/shard_map/ppermute | solution.py:253
  10.4 6.0 %collective-permute-start.14 = (bf16[128,512]{1,0:T(8,128)(2,1)S(1)}, bf16[128,512]{1,0:T(8,128)(2,1)S(1)}, u32[]{:S(2)}, u32[]{:S(2)}) collective-permute-start(bf16[128,512]{1,0:T(8,128)(2,1)S(1)} %collective-permute-done.13.refs_2_), channel_id=1, source_target_pairs={{4,0},{5,1},{8,4},{9,5},{12,8},{13,9},{14,12},{15,13},{10,14},{11,... | collective-permute-start | bytes 393224 | tf_op jit(solution)/shard_map/ppermute | solution.py:253
  13.0 5.6 %collective-permute-start.16 = (bf16[128,512]{1,0:T(8,128)(2,1)S(1)}, bf16[128,512]{1,0:T(8,128)(2,1)S(1)}, u32[]{:S(2)}, u32[]{:S(2)}) collective-permute-start(bf16[128,512]{1,0:T(8,128)(2,1)S(1)} %collective-permute-done.15.refs_6_), channel_id=1, source_target_pairs={{0,4},{1,5},{4,8},{5,9},{8,12},{9,13},{12,14},{13,15},{14,10},{15,... | collective-permute-start | bytes 393224 | tf_op jit(solution)/shard_map/ppermute | solution.py:253
  13.2 5.5 %collective-permute-start.10 = (bf16[4,128,128]{2,1,0:T(8,128)(2,1)S(1)}, bf16[4,128,128]{2,1,0:T(8,128)(2,1)S(1)}, u32[]{:S(2)}, u32[]{:S(2)}) collective-permute-start(bf16[4,128,128]{2,1,0:T(8,128)(2,1)S(1)} %copy-done.9), channel_id=1, source_target_pairs={{0,1},{1,0},{2,3},{3,2},{4,5},{5,4},{6,7},{7,6},{8,9},{9,8},{10,11... | collective-permute-start | bytes 393224 | tf_op jit(solution)/shard_map/ppermute | solution.py:253
  14.0 5.9 %collective-permute-start.9 = (bf16[128,512]{1,0:T(8,128)(2,1)S(1)}, bf16[128,512]{1,0:T(8,128)(2,1)S(1)}, u32[]{:S(2)}, u32[]{:S(2)}) collective-permute-start(bf16[128,512]{1,0:T(8,128)(2,1)S(1)} %collective-permute-done.7.refs_9_), channel_id=1, source_target_pairs={{4,0},{5,1},{8,4},{9,5},{12,8},{13,9},{14,12},{15,13},{10,14},{11,... | collective-permute-start | bytes 393224 | tf_op jit(solution)/shard_map/ppermute | solution.py:253
  15.9 6.3 %collective-permute-start.2 = (bf16[128,512]{1,0:T(8,128)(2,1)S(1)}, bf16[128,512]{1,0:T(8,128)(2,1)S(1)}, u32[]{:S(2)}, u32[]{:S(2)}) collective-permute-start(bf16[128,512]{1,0:T(8,128)(2,1)S(1)} %collective-permute-done.1.refs_3_), channel_id=1, source_target_pairs={{0,4},{1,5},{4,8},{5,9},{8,12},{9,13},{12,14},{13,15},{14,10},{15,... | collective-permute-start | bytes 393224 | tf_op jit(solution)/shard_map/ppermute | solution.py:253
  16.4 7.4 %collective-permute-start.17 = (bf16[128,512]{1,0:T(8,128)(2,1)S(1)}, bf16[128,512]{1,0:T(8,128)(2,1)S(1)}, u32[]{:S(2)}, u32[]{:S(2)}) collective-permute-start(bf16[128,512]{1,0:T(8,128)(2,1)S(1)} %collective-permute-done.14.refs_4_), channel_id=1, source_target_pairs={{4,0},{5,1},{8,4},{9,5},{12,8},{13,9},{14,12},{15,13},{10,14},{11,... | collective-permute-start | bytes 393224 | tf_op jit(solution)/shard_map/ppermute | solution.py:253
  18.6 6.5 %collective-permute-start.18 = (bf16[128,512]{1,0:T(8,128)(2,1)S(1)}, bf16[128,512]{1,0:T(8,128)(2,1)S(1)}, u32[]{:S(2)}, u32[]{:S(2)}) collective-permute-start(bf16[128,512]{1,0:T(8,128)(2,1)S(1)} %collective-permute-done.16.refs_8_), channel_id=1, source_target_pairs={{0,4},{1,5},{4,8},{5,9},{8,12},{9,13},{12,14},{13,15},{14,10},{15,... | collective-permute-start | bytes 393224 | tf_op jit(solution)/shard_map/ppermute | solution.py:253
  19.9 7.3 %collective-permute-start.11 = (bf16[128,512]{1,0:T(8,128)(2,1)S(1)}, bf16[128,512]{1,0:T(8,128)(2,1)S(1)}, u32[]{:S(2)}, u32[]{:S(2)}) collective-permute-start(bf16[128,512]{1,0:T(8,128)(2,1)S(1)} %collective-permute-done.9.refs_3_), channel_id=1, source_target_pairs={{4,0},{5,1},{8,4},{9,5},{12,8},{13,9},{14,12},{15,13},{10,14},{11,... | collective-permute-start | bytes 393224 | tf_op jit(solution)/shard_map/ppermute | solution.py:253
  22.2 5.0 %collective-permute-start.3 = (bf16[128,512]{1,0:T(8,128)(2,1)S(1)}, bf16[128,512]{1,0:T(8,128)(2,1)S(1)}, u32[]{:S(2)}, u32[]{:S(2)}) collective-permute-start(bf16[128,512]{1,0:T(8,128)(2,1)S(1)} %collective-permute-done.2.refs_0_), channel_id=1, source_target_pairs={{0,4},{1,5},{4,8},{5,9},{8,12},{9,13},{12,14},{13,15},{14,10},{15,... | collective-permute-start | bytes 393224 | tf_op jit(solution)/shard_map/ppermute | solution.py:253
  23.8 3.9 %copy-start.10 = (s32[3,4,512]{2,1,0:T(4,128)S(1)}, s32[3,4,512]{2,1,0:T(4,128)}, u32[]{:S(2)}) copy-start(s32[3,4,512]{2,1,0:T(4,128)} %index_ref.1) | copy-start | bytes 73732
  25.9 2.9 %copy-start = (f32[128,128]{1,0:T(8,128)S(1)}, f32[128,128]{1,0:T(8,128)}, u32[]{:S(2)}) copy-start(f32[128,128]{1,0:T(8,128)} %constant.5.clone.refs_15_.cosines_t_ref) | copy-start | bytes 196612
  25.9 2.9 %copy-start.1 = (f32[128,128]{1,0:T(8,128)S(1)}, f32[128,128]{1,0:T(8,128)}, u32[]{:S(2)}) copy-start(f32[128,128]{1,0:T(8,128)} %constant.4.clone.refs_14_.cosines_ref) | copy-start | bytes 196612
  25.9 2.9 %copy-start.2 = (f32[1,4,128,128]{3,2,1,0:T(8,128)S(1)}, f32[1,4,128,128]{3,2,1,0:T(8,128)}, u32[]{:S(2)}) copy-start(f32[1,4,128,128]{3,2,1,0:T(8,128)} %param.16) | copy-start | bytes 786436
  26.0 2.9 %copy-start.3 = (f32[1,4,128,128]{3,2,1,0:T(8,128)S(1)}, f32[1,4,128,128]{3,2,1,0:T(8,128)}, u32[]{:S(2)}) copy-start(f32[1,4,128,128]{3,2,1,0:T(8,128)} %param.17) | copy-start | bytes 786436
  26.0 2.9 %copy-start.4 = (f32[1,4,128,128]{3,2,1,0:T(8,128)S(1)}, f32[1,4,128,128]{3,2,1,0:T(8,128)}, u32[]{:S(2)}) copy-start(f32[1,4,128,128]{3,2,1,0:T(8,128)} %param.18) | copy-start | bytes 786436
  26.0 2.9 %collective-permute-start.19 = (f32[3,128,512]{2,1,0:T(8,128)S(1)}, f32[3,128,512]{2,1,0:T(8,128)S(1)}, u32[]{:S(2)}, u32[]{:S(2)}) collective-permute-start(f32[3,128,512]{2,1,0:T(8,128)S(1)} %get-tuple-element.48), channel_id=1, source_target_pairs={{0,1},{1,0},{2,3},{3,2},{4,5},{5,4},{6,7},{7,6},{8,9},{9,8},{10,11... | collective-permute-start | bytes 2359304 | tf_op jit(solution)/shard_map/ppermute | solution.py:253
  27.2 1.6 %collective-permute-start.4 = (bf16[128,512]{1,0:T(8,128)(2,1)S(1)}, bf16[128,512]{1,0:T(8,128)(2,1)S(1)}, u32[]{:S(2)}, u32[]{:S(2)}) collective-permute-start(bf16[128,512]{1,0:T(8,128)(2,1)S(1)} %collective-permute-done.3.refs_0_), channel_id=1, source_target_pairs={{0,1},{1,0},{2,3},{3,2},{4,5},{5,4},{6,7},{7,6},{8,9},{9,8},{10,11... | collective-permute-start | bytes 393224 | tf_op jit(solution)/shard_map/ppermute | solution.py:253
  27.2 1.6 %collective-permute-start.12 = (bf16[128,512]{1,0:T(8,128)(2,1)S(1)}, bf16[128,512]{1,0:T(8,128)(2,1)S(1)}, u32[]{:S(2)}, u32[]{:S(2)}) collective-permute-start(bf16[128,512]{1,0:T(8,128)(2,1)S(1)} %collective-permute-done.11.refs_1_.refs_2_), channel_id=1, source_target_pairs={{0,1},{1,0},{2,3},{3,2},{4,5},{5,4},{6,7},{7,6},{8,9},{9,8},{10,11... | collective-permute-start | bytes 393224 | tf_op jit(solution)/shard_map/ppermute | solution.py:253
  30.7 3.9 %collective-permute-start.20 = (f32[3,4,512]{2,1,0:T(4,128)S(1)}, f32[3,4,512]{2,1,0:T(4,128)S(1)}, u32[]{:S(2)}, u32[]{:S(2)}) collective-permute-start(f32[3,4,512]{2,1,0:T(4,128)S(1)} %get-tuple-element.59), channel_id=1, source_target_pairs={{0,16},{16,0},{1,17},{17,1},{2,18},{18,2},{3,19},{19,3},{4,20},{20... | collective-permute-start | bytes 73736 | tf_op jit(solution)/shard_map/ppermute | solution.py:419

commit v4 on v3

--- a/solution.py
+++ b/solution.py
@@ -10,7 +10,8 @@
 
 MOMENTUM_DECAY = 0.999
 
-TABLES_FLOPS = 10**10
+TABLES_FLOPS = 10**9
+LAST_FLOPS = 10**10
 PAUSE_FLOPS = 10**9
 F32 = jnp.float32
 BF16 = jnp.bfloat16
@@ -77,8 +78,18 @@
             mask_ref[b] = dot(in_row, in_col_t).astype(BF16)
 
 
-def pause_kernel(out_ref):
-    out_ref[...] = jnp.zeros_like(out_ref)
+def pause_kernel(*refs):
+    refs[-1][...] = jnp.zeros_like(refs[-1])
+
+
+def pause(flops, *ahead):
+    return call(
+        pause_kernel,
+        jax.ShapeDtypeStruct((8, 128), F32),
+        flops,
+        *ahead,
+        in_place=dict.fromkeys(range(len(ahead)), pl.ANY),
+    )
 
 
 def column_grads(xs, ds, wgu, wd, x_all, d_all, act):
@@ -123,20 +134,16 @@
         par_ref[m] = par_in[m] + grad[side:]
 
 
-def moment_step(
-    grads, mom_refs, in_row_ref, in_col_ref, mask_ref, cosines_ref, cosines_t_ref, moment_ref, kept_ref, band_ref
-):
+def block_of(grads, m, i, side):
+    piece = grads[m][:, i * side : (i + 1) * side]
+    return piece.T if m < 2 else piece
+
+
+def moment_step(blocks, in_row_ref, in_col_ref, mask_ref, cosines_ref, cosines_t_ref, moment_ref, kept_ref, band_ref):
     side = cosines_ref.shape[0]
-    count = mom_refs[0].shape[0]
-    blocks = []
-    for m in range(3):
-        for i in range(count):
-            piece = grads[m][:, i * side : (i + 1) * side]
-            if m < 2:
-                piece = piece.T
-            block = MOMENTUM_DECAY * mom_refs[m][i] + piece
-            moment_ref[m * count + i] = block
-            blocks.append(block)
+    count = len(blocks) // 3
+    for b, block in enumerate(blocks):
+        moment_ref[b] = block
     inner = dot3(cosines_ref[...], jnp.concatenate(blocks, axis=1))
     coeffs = dot3(lanes_to_rows(inner, side), cosines_t_ref[...])
     for m in range(3):
@@ -152,20 +159,42 @@
             )
 
 
-def late_kernel(*refs):
-    xs, ds, wgu_ref, wd_ref, own_ref, got_ref = refs[:2], refs[2:4], *refs[4:8]
-    side = own_ref.shape[1]
-    x = jnp.concatenate([ref[...] for ref in xs], axis=0)
-    d = jnp.concatenate([ref[...] for ref in ds], axis=0)
+def late_grads(x_ref, d_ref, wgu_ref, wd_ref, add_ref):
+    side = add_ref.shape[1]
+    x, d = x_ref[...], d_ref[...]
     wgu = jnp.concatenate([wgu_ref[:side, :], wgu_ref[2 * side : 3 * side, :]], axis=0)
     d_gate, d_up, hidden = activations(wgu, wd_ref[:side, :], x, d)
-    late = (dot(d_gate, x), dot(d_up, x), dot(hidden, d))
-    grads = [late[m] + (own_ref[m] + got_ref[m]) for m in range(3)]
-    moment_step(grads, refs[8:11], *refs[11:])
-
-
-def moment_kernel(grad_ref, *refs):
-    moment_step([grad_ref[m] for m in range(3)], refs[:3], *refs[3:])
+    return [add_ref[m] + late for m, late in enumerate((dot(d_gate, x), dot(d_up, x), dot(hidden, d)))]
+
+
+def base_kernel(x_ref, d_ref, wgu_ref, wd_ref, own_ref, mg_ref, mu_ref, md_ref, base_ref):
+    grads = late_grads(x_ref, d_ref, wgu_ref, wd_ref, own_ref)
+    count, side, _ = mg_ref.shape
+    for m, mom_ref in enumerate((mg_ref, mu_ref, md_ref)):
+        for i in range(count):
+            base_ref[m * count + i] = MOMENTUM_DECAY * mom_ref[i] + block_of(grads, m, i, side)
+
+
+def late_kernel(_, x_ref, d_ref, wgu_ref, wd_ref, got_ref, base_ref, *refs):
+    grads = late_grads(x_ref, d_ref, wgu_ref, wd_ref, got_ref)
+    blocks, side, _ = base_ref.shape
+    count = blocks // 3
+    moment_step(
+        [base_ref[b] + block_of(grads, b // count, b % count, side) for b in range(blocks)], *refs
+    )
+
+
+def moment_kernel(grad_ref, mg_ref, mu_ref, md_ref, *refs):
+    count, side, _ = mg_ref.shape
+    grads = [grad_ref[m] for m in range(3)]
+    moment_step(
+        [
+            MOMENTUM_DECAY * mom_ref[i] + block_of(grads, m, i, side)
+            for m, mom_ref in enumerate((mg_ref, mu_ref, md_ref))
+            for i in range(count)
+        ],
+        *refs,
+    )
 
 
 def residual_kernel(moment_ref, kept_ref, in_col_t_ref, cosines_ref, cosines_t_ref, *outs):
@@ -186,9 +215,11 @@
         cells_ref[b] = dot(in_col_t_ref[b], parts).astype(BF16)
 
 
-def update_kernel(decoded_ref, other_ref, in_row_ref, cells_ref, cosines_t_ref, *outs):
+def update_kernel(decoded_ref, other_ref, in_row_ref, cells_ref, cosines_t_ref, *refs):
+    outs, (held, sems) = refs[:3], refs[3:]
     side = cosines_t_ref.shape[0]
-    count = outs[0].shape[0]
+    count = held.shape[1]
+    copies = [pltpu.make_async_copy(held.at[m], outs[m], sems.at[m]) for m in range(3)]
     inner = []
     for b in range(3 * count):
         m, i = b // count, b % count
@@ -196,12 +227,16 @@
         in_row = in_row_ref[b]
         both = dot(jnp.concatenate([in_row * hi, in_row * lo], axis=0), cells_ref[b])
         inner.append(both[:side, :side] + (both[:side, side:] + both[side:, :side]))
-    update = dot3(cosines_t_ref[...], jnp.concatenate(inner, axis=1))
-    for b in range(3 * count):
-        outs[b // count][b % count] = decoded_ref[b] + update[:, b * side : (b + 1) * side]
-
-
-def call(kernel, out_shape, flops, *args, scratch=(), in_place={}):
+    for m in range(3):
+        update = dot3(cosines_t_ref[...], jnp.concatenate(inner[m * count : (m + 1) * count], axis=1))
+        for i in range(count):
+            held[m, i] = decoded_ref[m * count + i] + update[:, i * side : (i + 1) * side]
+        copies[m].start()
+    for copy in copies:
+        copy.wait()
+
+
+def call(kernel, out_shape, flops, *args, scratch=(), in_place={}, out_specs=None):
     moved = sum(a.size * a.dtype.itemsize for a in args)
     specs = [
         pl.BlockSpec(memory_space=in_place.get(k, pltpu.VMEM)) for k in range(len(args))
@@ -210,6 +245,7 @@
         kernel,
         out_shape=out_shape,
         in_specs=specs,
+        **({} if out_specs is None else {"out_specs": out_specs}),
         scratch_shapes=list(scratch),
         compiler_params=pltpu.CompilerParams(vmem_limit_bytes=24 * 1024 * 1024),
         cost_estimate=pl.CostEstimate(flops=flops, bytes_accessed=2 * moved, transcendentals=0),
@@ -255,8 +291,8 @@
     xf, db, df, xb = send(x, forward), send(d, back), send(d, forward), send(x, back)
     xs, ds = [x, xf, xb], [d, df, db]
     partner_weights = [send(w, swap) for w in weights]
-    pause = call(pause_kernel, jax.ShapeDtypeStruct((8, 128), F32), PAUSE_FLOPS)
-    db, pause = lax.optimization_barrier((db, pause))
+    work = pause(PAUSE_FLOPS)
+    db, work = lax.optimization_barrier((db, work))
     arrived = []
 
     def with_weight(value):
@@ -296,7 +332,7 @@
         *ds[:early],
         *weights,
         *partner_weights,
-        pause,
+        work,
         scratch=scratch(early),
     )
     own, partner = call(
@@ -313,20 +349,22 @@
     )
     got = send(partner, swap)
     x_swap, d_swap = send(x_last, swap), send(d_last, swap)
-    in_row, in_col, in_col_t, mask = band_tables(band_index, side, x_last, d_last)
+    in_row, in_col, in_col_t, mask = band_tables(band_index, side, partner)
+    late_flops = 24 * rows * width * side
+    base = call(
+        base_kernel, shapes[0], late_flops, x_last, d_last, wgu, wd, own, *momenta
+    )
     moments = call(
         late_kernel,
         shapes,
-        10**9,
-        x_last,
+        late_flops,
+        pause(LAST_FLOPS, x_last, d_last),
         x_swap,
-        d_last,
         d_swap,
         wgu,
         wd,
-        own,
         got,
-        *momenta,
+        base,
         in_row,
         in_col,
         mask,
@@ -433,7 +471,16 @@
         cosines_t,
     )
     updates = call(
-        update_kernel, (result,) * 3, flops, decoded, other, in_row, cells, cosines_t
+        update_kernel,
+        (result,) * 3,
+        flops,
+        decoded,
+        other,
+        in_row,
+        cells,
+        cosines_t,
+        scratch=(pltpu.VMEM((3, *result.shape), F32), pltpu.SemaphoreType.DMA((3,))),
+        out_specs=[pl.BlockSpec(memory_space=pl.ANY)] * 3,
     )
     return (*(r[None] for r in residuals), *updates)
 

time: 36.7 us -> 36.9 us (level)
  waiting for transfers between devices: 9.83 us -> 8.97 us
  Pallas kernels: 8.85 us -> 9.38 us
  local copies, waits for them, and re-layouts: 0.06 us -> 0.49 us
    ppermute x20, waiting for transfers between devices: 9.1 us -> 8.24 us  [send(): return lax.ppermute(value, 'fsdp', perm)]
    pallas_call x7 -> x9, Pallas kernels: 8.85 us -> 9.38 us  [call(): pl.pallas_call(kernel, out_shape=out_shape, in_specs=specs, **{} if out_s...]
    unnamed x22, local copies, waits for them, and re-layouts: 0.06 us -> 0.49 us
  transfers between devices with their start and end apart: 21 -> 21, of which waited for: 12 -> 13; matrix products, arithmetic and copies ran while one was open for 0% -> 0% of each run, Pallas kernels for 14% -> 15%
where the time goes in v4:
time: 36.9 us; the launch traced here: 36.7 us
  starting transfers between devices  17.1 us (46%)
  Pallas kernels  9.38 us (25%)
  waiting for transfers between devices  8.97 us (24%)
  between operations  0.79 us (2%)
  local copies, waits for them, and re-layouts  0.49 us (1%)
    ppermute x20, starting transfers between devices, send(): return lax.ppermute(value, 'fsdp', perm)  15.5 us
    pallas_call x9, Pallas kernels, call(): pl.pallas_call(kernel, out_shape=out_shape, in_specs=specs, **{} if out_s...  9.38 us
    ppermute x20, waiting for transfers between devices, send(): return lax.ppermute(value, 'fsdp', perm)  8.24 us
    ppermute x1, starting transfers between devices, per_device(): lax.ppermute(band, 'rep', [(r, (r + s) % reps) for r in range(reps)])  1.59 us
  transfers between devices with their start and end apart: 21, of which 13 were waited for; matrix products, arithmetic and copies ran while one was open for 0% of the time, Pallas kernels for 15%

profile of v4, /device:TPU:0, one launch (start us, length us, event | category | flops | bytes accessed | tf_op | source)
XLA Modules:
  0.0 36.7 jit_solution(1957966098018597929)
XLA Ops:
  0.6 3.0 %collective-permute-start.4 = (bf16[128,512]{1,0:T(8,128)(2,1)}, bf16[128,512]{1,0:T(8,128)(2,1)S(1)}, u32[]{:S(2)}, u32[]{:S(2)}) collective-permute-start(bf16[128,512]{1,0:T(8,128)(2,1)} %bitcast.16), channel_id=1, source_target_pairs={{4,0},{5,1},{8,4},{9,5},{12,8},{13,9},{14,12},{15,13},{10,14},{11,... | collective-permute-start | bytes 393224 | tf_op jit(solution)/shard_map/ppermute | solution.py:289
  3.6 0.0 collective-permute-start.5
  3.6 0.0 copy-start.6
  3.6 0.0 copy-start.7
  3.7 0.2 collective-permute-start
  3.9 1.8 %collective-permute-start.13 = (bf16[128,512]{1,0:T(8,128)(2,1)}, bf16[128,512]{1,0:T(8,128)(2,1)S(1)}, u32[]{:S(2)}, u32[]{:S(2)}) collective-permute-start(bf16[128,512]{1,0:T(8,128)(2,1)} %bitcast.14), channel_id=1, source_target_pairs={{4,0},{5,1},{8,4},{9,5},{12,8},{13,9},{14,12},{15,13},{10,14},{11,... | collective-permute-start | bytes 393224 | tf_op jit(solution)/shard_map/ppermute | solution.py:289
  5.7 0.2 collective-permute-start.15
  5.9 1.7 %collective-permute-done.4.refs_7_ = bf16[128,512]{1,0:T(8,128)(2,1)S(1)} collective-permute-done((bf16[128,512]{1,0:T(8,128)(2,1)}, bf16[128,512]{1,0:T(8,128)(2,1)S(1)}, u32[]{:S(2)}, u32[]{:S(2)}) %collective-permute-start.4) | collective-permute-done | bytes 131104 | tf_op jit(solution)/shard_map/ppermute | solution.py:289
  7.6 0.0 copy-done.8
  7.6 0.0 collective-permute-start.7
  7.6 0.0 collective-permute-done.5.refs_13_
  7.6 1.8 %collective-permute-start.6 = (bf16[128,512]{1,0:T(8,128)(2,1)S(1)}, bf16[128,512]{1,0:T(8,128)(2,1)S(1)}, u32[]{:S(2)}, u32[]{:S(2)}) collective-permute-start(bf16[128,512]{1,0:T(8,128)(2,1)S(1)} %collective-permute-done.4.refs_7_), channel_id=1, source_target_pairs={{4,0},{5,1},{8,4},{9,5},{12,8},{13,9},{14,12},{15,13},{10,14},{11,... | collective-permute-start | bytes 393224 | tf_op jit(solution)/shard_map/ppermute | solution.py:289
  9.4 0.8 %collective-permute-done.refs_1_ = bf16[128,512]{1,0:T(8,128)(2,1)S(1)} collective-permute-done((bf16[128,512]{1,0:T(8,128)(2,1)}, bf16[128,512]{1,0:T(8,128)(2,1)S(1)}, u32[]{:S(2)}, u32[]{:S(2)}) %collective-permute-start) | collective-permute-done | bytes 131104 | tf_op jit(solution)/shard_map/ppermute | solution.py:289
  10.2 0.2 collective-permute-start.1
  10.4 0.0 collective-permute-done.13.refs_2_
  10.4 1.8 %collective-permute-start.14 = (bf16[128,512]{1,0:T(8,128)(2,1)S(1)}, bf16[128,512]{1,0:T(8,128)(2,1)S(1)}, u32[]{:S(2)}, u32[]{:S(2)}) collective-permute-start(bf16[128,512]{1,0:T(8,128)(2,1)S(1)} %collective-permute-done.13.refs_2_), channel_id=1, source_target_pairs={{4,0},{5,1},{8,4},{9,5},{12,8},{13,9},{14,12},{15,13},{10,14},{11,... | collective-permute-start | bytes 393224 | tf_op jit(solution)/shard_map/ppermute | solution.py:289
  12.2 0.8 %collective-permute-done.15.refs_6_ = bf16[128,512]{1,0:T(8,128)(2,1)S(1)} collective-permute-done((bf16[128,512]{1,0:T(8,128)(2,1)}, bf16[128,512]{1,0:T(8,128)(2,1)S(1)}, u32[]{:S(2)}, u32[]{:S(2)}) %collective-permute-start.15) | collective-permute-done | bytes 131104 | tf_op jit(solution)/shard_map/ppermute | solution.py:289
  13.0 0.2 collective-permute-start.16
  13.2 0.0 collective-permute-done.7.refs_14_
  13.2 0.0 copy-done.9
  13.2 0.0 collective-permute-start.9
  13.2 0.8 %collective-permute-done.6.refs_9_ = bf16[128,512]{1,0:T(8,128)(2,1)S(1)} collective-permute-done((bf16[128,512]{1,0:T(8,128)(2,1)S(1)}, bf16[128,512]{1,0:T(8,128)(2,1)S(1)}, u32[]{:S(2)}, u32[]{:S(2)}) %collective-permute-start.6) | collective-permute-done | bytes 131104 | tf_op jit(solution)/shard_map/ppermute | solution.py:289
  14.0 1.7 %collective-permute-start.8 = (bf16[128,512]{1,0:T(8,128)(2,1)S(1)}, bf16[128,512]{1,0:T(8,128)(2,1)S(1)}, u32[]{:S(2)}, u32[]{:S(2)}) collective-permute-start(bf16[128,512]{1,0:T(8,128)(2,1)S(1)} %collective-permute-done.6.refs_9_), channel_id=1, source_target_pairs={{4,0},{5,1},{8,4},{9,5},{12,8},{13,9},{14,12},{15,13},{10,14},{11,... | collective-permute-start | bytes 393224 | tf_op jit(solution)/shard_map/ppermute | solution.py:289
  15.7 0.2 collective-permute-done.1.refs_3_
  15.9 0.2 collective-permute-start.2
  16.1 0.3 collective-permute-done.14.refs_4_
  16.4 1.7 %collective-permute-start.17 = (bf16[128,512]{1,0:T(8,128)(2,1)S(1)}, bf16[128,512]{1,0:T(8,128)(2,1)S(1)}, u32[]{:S(2)}, u32[]{:S(2)}) collective-permute-start(bf16[128,512]{1,0:T(8,128)(2,1)S(1)} %collective-permute-done.14.refs_4_), channel_id=1, source_target_pairs={{4,0},{5,1},{8,4},{9,5},{12,8},{13,9},{14,12},{15,13},{10,14},{11,... | collective-permute-start | bytes 393224 | tf_op jit(solution)/shard_map/ppermute | solution.py:289
  18.1 0.5 %collective-permute-done.16.refs_8_ = bf16[128,512]{1,0:T(8,128)(2,1)S(1)} collective-permute-done((bf16[128,512]{1,0:T(8,128)(2,1)S(1)}, bf16[128,512]{1,0:T(8,128)(2,1)S(1)}, u32[]{:S(2)}, u32[]{:S(2)}) %collective-permute-start.16) | collective-permute-done | bytes 131104 | tf_op jit(solution)/shard_map/ppermute | solution.py:289
  18.6 0.1 collective-permute-start.18
  18.7 0.0 collective-permute-done.9.refs_15_
  18.7 1.2 %collective-permute-done.8.refs_3_ = bf16[128,512]{1,0:T(8,128)(2,1)S(1)} collective-permute-done((bf16[128,512]{1,0:T(8,128)(2,1)S(1)}, bf16[128,512]{1,0:T(8,128)(2,1)S(1)}, u32[]{:S(2)}, u32[]{:S(2)}) %collective-permute-start.8) | collective-permute-done | bytes 131104 | tf_op jit(solution)/shard_map/ppermute | solution.py:289
  19.9 1.9 %collective-permute-start.10 = (bf16[128,512]{1,0:T(8,128)(2,1)S(1)}, bf16[128,512]{1,0:T(8,128)(2,1)S(1)}, u32[]{:S(2)}, u32[]{:S(2)}) collective-permute-start(bf16[128,512]{1,0:T(8,128)(2,1)S(1)} %collective-permute-done.8.refs_3_), channel_id=1, source_target_pairs={{4,0},{5,1},{8,4},{9,5},{12,8},{13,9},{14,12},{15,13},{10,14},{11,... | collective-permute-start | bytes 393224 | tf_op jit(solution)/shard_map/ppermute | solution.py:289
  21.8 0.4 %collective-permute-done.2.refs_0_ = bf16[128,512]{1,0:T(8,128)(2,1)S(1)} collective-permute-done((bf16[128,512]{1,0:T(8,128)(2,1)S(1)}, bf16[128,512]{1,0:T(8,128)(2,1)S(1)}, u32[]{:S(2)}, u32[]{:S(2)}) %collective-permute-start.2) | collective-permute-done | bytes 131104 | tf_op jit(solution)/shard_map/ppermute | solution.py:289
  22.2 0.0 collective-permute-start.3
  22.2 0.0 copy-done.5
  22.2 0.0 copy-done.6
  22.3 0.0 copy-done.7
  22.3 1.5 %shard_map.156 = (f32[3,128,512]{2,1,0:T(8,128)S(1)}, f32[3,128,512]{2,1,0:T(8,128)S(1)}, bf16[512,512]{1,0:T(8,128)(2,1)S(1)}, bf16[256,512]{1,0:T(8,128)(2,1)S(1)}) custom-call(bf16[128,512]{1,0:T(8,128)(2,1)S(1)} %bitcast.15, bf16[128,512]{1,0:T(8,128)(2,1)S(1)} %collective-permute-done.refs_1_, bf16[128,512]{1,0:T(8,128)(2,1)S(1)} %collective-permute-done.13.refs_2_, ...), custom_call_target="tpu_custom_call" | custom-call | flops 1006632960 | bytes 4202496 | tf_op jit(solution)/shard_map/pallas_call | solution.py:244
  23.8 0.0 copy-start.10
  23.8 0.0 collective-permute-done.17.refs_1_
  23.8 1.2 %collective-permute-done.18.refs_2_ = bf16[128,512]{1,0:T(8,128)(2,1)S(1)} collective-permute-done((bf16[128,512]{1,0:T(8,128)(2,1)S(1)}, bf16[128,512]{1,0:T(8,128)(2,1)S(1)}, u32[]{:S(2)}, u32[]{:S(2)}) %collective-permute-start.18) | collective-permute-done | bytes 131104 | tf_op jit(solution)/shard_map/ppermute | solution.py:289
  25.0 0.9 %shard_map.157 = (f32[3,128,512]{2,1,0:T(8,128)S(1)}, f32[3,128,512]{2,1,0:T(8,128)S(1)}) custom-call(bf16[128,512]{1,0:T(8,128)(2,1)S(1)} %collective-permute-done.2.refs_0_, bf16[128,512]{1,0:T(8,128)(2,1)S(1)} %collective-permute-done.17.refs_1_, bf16[128,512]{1,0:T(8,128)(2,1)S(1)} %collective-permute-done.18.refs_2_, ...), custom_call_target="tpu_custom_call" | custom-call | flops 402653184 | bytes 5767168 | tf_op jit(solution)/shard_map/pallas_call | solution.py:244
  25.9 0.1 collective-permute-start.19
  26.0 1.1 %shard_map.159 = (bf16[12,128,512]{2,1,0:T(8,128)(2,1)S(1)}, bf16[12,128,512]{2,1,0:T(8,128)(2,1)S(1)}, bf16[12,512,128]{2,1,0:T(8,128)(2,1)S(1)}, bf16[12,128,128]{2,1,0:T(8,128)(2,1)S(1)}) custom-call(s32[3,4,512]{2,1,0:T(4,128)S(1)} %copy-done.10, f32[3,128,512]{2,1,0:T(8,128)S(1)} %get-tuple-element.47.refs_0_), custom_call_target="tpu_custom_call" | custom-call | flops 1000000000 | bytes 1622016 | tf_op jit(solution)/shard_map/pallas_call | solution.py:244
  27.1 0.0 copy-start.2
  27.1 0.0 copy-start.3
  27.1 0.0 copy-start.4
  27.1 0.1 collective-permute-done.3.refs_0_.x_ref
  27.2 0.5 %collective-permute-start.11 = (bf16[128,512]{1,0:T(8,128)(2,1)S(1)}, bf16[128,512]{1,0:T(8,128)(2,1)S(1)}, u32[]{:S(2)}, u32[]{:S(2)}) collective-permute-start(bf16[128,512]{1,0:T(8,128)(2,1)S(1)} %collective-permute-done.3.refs_0_.x_ref), channel_id=1, source_target_pairs={{0,1},{1,0},{2,3},{3,2},{4,5},{5,4},{6,7},{7,6},{8,9},{9,8},{10,11... | collective-permute-start | bytes 393224 | tf_op jit(solution)/shard_map/ppermute | solution.py:289
  27.7 0.0 collective-permute-done.10.refs_1_.d_ref
  27.7 0.1 collective-permute-start.12
  27.8 0.3 copy-done.2
  28.1 0.1 copy-done.3
  28.1 0.1 copy-done.4
  28.2 0.6 %shard_map.158.base_ref = f32[12,128,128]{2,1,0:T(8,128)S(1)} custom-call(bf16[128,512]{1,0:T(8,128)(2,1)S(1)} %collective-permute-done.3.refs_0_.x_ref, bf16[128,512]{1,0:T(8,128)(2,1)S(1)} %collective-permute-done.10.refs_1_.d_ref, bf16[512,512]{1,0:T(8,128)(2,1)S(1)} %get-tuple-element.43.refs_4_.wgu_ref, ...), custom_call_target="tpu_custom_call" | custom-call | flops 201326592 | bytes 5242880 | tf_op jit(solution)/shard_map/pallas_call | solution.py:244
  28.8 0.0 collective-permute-done.11.x_ref
  28.8 0.2 collective-permute-done.12.d_ref
  29.1 0.0 collective-permute-done.19.got_ref
  29.1 0.0 copy-done.1
  29.1 1.7 %shard_map.160 = (f32[12,128,128]{2,1,0:T(8,128)S(1)}, f32[12,128,128]{2,1,0:T(8,128)S(1)}, f32[3,4,512]{2,1,0:T(4,128)S(1)}) custom-call(f32[8,128]{1,0:T(8,128)S(1)} %shard_map.155._, bf16[128,512]{1,0:T(8,128)(2,1)S(1)} %collective-permute-done.11.x_ref, bf16[128,512]{1,0:T(8,128)(2,1)S(1)} %collective-permute-done.12.d_ref, ...), custom_call_target="tpu_custom_call" | custom-call | flops 201326592 | bytes 12591104 | tf_op jit(solution)/shard_map/pallas_call | solution.py:244
  30.8 1.6 %collective-permute-start.20 = (f32[3,4,512]{2,1,0:T(4,128)S(1)}, f32[3,4,512]{2,1,0:T(4,128)S(1)}, u32[]{:S(2)}, u32[]{:S(2)}) collective-permute-start(f32[3,4,512]{2,1,0:T(4,128)S(1)} %get-tuple-element.59), channel_id=1, source_target_pairs={{0,16},{16,0},{1,17},{17,1},{2,18},{18,2},{3,19},{19,3},{4,20},{20... | collective-permute-start | bytes 73736 | tf_op jit(solution)/shard_map/ppermute | solution.py:457
  32.4 1.6 %shard_map.161 = (f32[4,128,128]{2,1,0:T(8,128)}, f32[4,128,128]{2,1,0:T(8,128)}, f32[4,128,128]{2,1,0:T(8,128)}, f32[12,128,128]{2,1,0:T(8,128)S(1)}, bf16[12,512,256]{2,1,0:T(8,128)(2,1)S(1)}) custom-call(f32[12,128,128]{2,1,0:T(8,128)S(1)} %get-tuple-element.52.moment_ref, f32[12,128,128]{2,1,0:T(8,128)S(1)} %get-tuple-element.53.kept_ref, ...), custom_call_target="tpu_custom_call" | custom-call | flops 301989888 | bytes 6553600 | tf_op jit(solution)/shard_map/pallas_call | solution.py:244
  34.0 0.7 %collective-permute-done.20 = f32[3,4,512]{2,1,0:T(4,128)S(1)} collective-permute-done((f32[3,4,512]{2,1,0:T(4,128)S(1)}, f32[3,4,512]{2,1,0:T(4,128)S(1)}, u32[]{:S(2)}, u32[]{:S(2)}) %collective-permute-start.20) | collective-permute-done | bytes 24608 | tf_op jit(solution)/shard_map/ppermute | solution.py:457
  34.7 2.0 %shard_map.162 = (f32[4,128,128]{2,1,0:T(8,128)}, f32[4,128,128]{2,1,0:T(8,128)}, f32[4,128,128]{2,1,0:T(8,128)}) custom-call(f32[12,128,128]{2,1,0:T(8,128)S(1)} %get-tuple-element.58.decoded_ref, f32[1,3,4,512]{3,2,1,0:T(4,128)S(1)} %bitcast.12, bf16[12,128,512]{2,1,0:T(8,128)(2,1)S(1)} %get-tuple-element.49.refs_0_.in_row_ref, ...), custom_call_target="tpu_custom_call" | custom-call | flops 301989888 | bytes 11190272 | tf_op jit(solution)/shard_map/pallas_call | solution.py:244
  (9 shorter events, 0.0 us)
Async XLA Ops:
  0.6 7.0 %collective-permute-start.4 = (bf16[128,512]{1,0:T(8,128)(2,1)}, bf16[128,512]{1,0:T(8,128)(2,1)S(1)}, u32[]{:S(2)}, u32[]{:S(2)}) collective-permute-start(bf16[128,512]{1,0:T(8,128)(2,1)} %bitcast.16), channel_id=1, source_target_pairs={{4,0},{5,1},{8,4},{9,5},{12,8},{13,9},{14,12},{15,13},{10,14},{11,... | collective-permute-start | bytes 393224 | tf_op jit(solution)/shard_map/ppermute | solution.py:289
  3.6 4.0 %collective-permute-start.5 = (bf16[4,128,128]{2,1,0:T(8,128)(2,1)}, bf16[4,128,128]{2,1,0:T(8,128)(2,1)S(1)}, u32[]{:S(2)}, u32[]{:S(2)}) collective-permute-start(bf16[4,128,128]{2,1,0:T(8,128)(2,1)} %refs_10_.1), channel_id=1, source_target_pairs={{0,1},{1,0},{2,3},{3,2},{4,5},{5,4},{6,7},{7,6},{8,9},{9,8},{10,11... | collective-permute-start | bytes 393224 | tf_op jit(solution)/shard_map/ppermute | solution.py:289
  3.6 4.0 %copy-start.8 = (bf16[4,128,128]{2,1,0:T(8,128)(2,1)S(1)}, bf16[4,128,128]{2,1,0:T(8,128)(2,1)}, u32[]{:S(2)}) copy-start(bf16[4,128,128]{2,1,0:T(8,128)(2,1)} %refs_11_.1) | copy-start | bytes 393220
  3.6 9.6 %copy-start.9 = (bf16[4,128,128]{2,1,0:T(8,128)(2,1)S(1)}, bf16[4,128,128]{2,1,0:T(8,128)(2,1)}, u32[]{:S(2)}) copy-start(bf16[4,128,128]{2,1,0:T(8,128)(2,1)} %refs_12_.1) | copy-start | bytes 393220
  3.6 18.6 %copy-start.5 = (bf16[1,128,512]{2,1,0:T(8,128)(2,1)S(1)}, bf16[1,128,512]{2,1,0:T(8,128)(2,1)}, u32[]{:S(2)}) copy-start(bf16[1,128,512]{2,1,0:T(8,128)(2,1)} %param.11) | copy-start | bytes 393220
  3.6 18.6 %copy-start.6 = (bf16[1,128,512]{2,1,0:T(8,128)(2,1)S(1)}, bf16[1,128,512]{2,1,0:T(8,128)(2,1)}, u32[]{:S(2)}) copy-start(bf16[1,128,512]{2,1,0:T(8,128)(2,1)} %param.12) | copy-start | bytes 393220
  3.6 18.6 %copy-start.7 = (bf16[4,128,128]{2,1,0:T(8,128)(2,1)S(1)}, bf16[4,128,128]{2,1,0:T(8,128)(2,1)}, u32[]{:S(2)}) copy-start(bf16[4,128,128]{2,1,0:T(8,128)(2,1)} %refs_10_.1) | copy-start | bytes 393220
  3.7 6.6 %collective-permute-start = (bf16[128,512]{1,0:T(8,128)(2,1)}, bf16[128,512]{1,0:T(8,128)(2,1)S(1)}, u32[]{:S(2)}, u32[]{:S(2)}) collective-permute-start(bf16[128,512]{1,0:T(8,128)(2,1)} %bitcast.13), channel_id=1, source_target_pairs={{0,4},{1,5},{4,8},{5,9},{8,12},{9,13},{12,14},{13,15},{14,10},{15,... | collective-permute-start | bytes 393224 | tf_op jit(solution)/shard_map/ppermute | solution.py:289
  3.9 6.5 %collective-permute-start.13 = (bf16[128,512]{1,0:T(8,128)(2,1)}, bf16[128,512]{1,0:T(8,128)(2,1)S(1)}, u32[]{:S(2)}, u32[]{:S(2)}) collective-permute-start(bf16[128,512]{1,0:T(8,128)(2,1)} %bitcast.14), channel_id=1, source_target_pairs={{4,0},{5,1},{8,4},{9,5},{12,8},{13,9},{14,12},{15,13},{10,14},{11,... | collective-permute-start | bytes 393224 | tf_op jit(solution)/shard_map/ppermute | solution.py:289
  5.7 7.3 %collective-permute-start.15 = (bf16[128,512]{1,0:T(8,128)(2,1)}, bf16[128,512]{1,0:T(8,128)(2,1)S(1)}, u32[]{:S(2)}, u32[]{:S(2)}) collective-permute-start(bf16[128,512]{1,0:T(8,128)(2,1)} %bitcast.17), channel_id=1, source_target_pairs={{0,4},{1,5},{4,8},{5,9},{8,12},{9,13},{12,14},{13,15},{14,10},{15,... | collective-permute-start | bytes 393224 | tf_op jit(solution)/shard_map/ppermute | solution.py:289
  7.6 5.6 %collective-permute-start.7 = (bf16[4,128,128]{2,1,0:T(8,128)(2,1)S(1)}, bf16[4,128,128]{2,1,0:T(8,128)(2,1)S(1)}, u32[]{:S(2)}, u32[]{:S(2)}) collective-permute-start(bf16[4,128,128]{2,1,0:T(8,128)(2,1)S(1)} %copy-done.8), channel_id=1, source_target_pairs={{0,1},{1,0},{2,3},{3,2},{4,5},{5,4},{6,7},{7,6},{8,9},{9,8},{10,11... | collective-permute-start | bytes 393224 | tf_op jit(solution)/shard_map/ppermute | solution.py:289
  7.6 6.3 %collective-permute-start.6 = (bf16[128,512]{1,0:T(8,128)(2,1)S(1)}, bf16[128,512]{1,0:T(8,128)(2,1)S(1)}, u32[]{:S(2)}, u32[]{:S(2)}) collective-permute-start(bf16[128,512]{1,0:T(8,128)(2,1)S(1)} %collective-permute-done.4.refs_7_), channel_id=1, source_target_pairs={{4,0},{5,1},{8,4},{9,5},{12,8},{13,9},{14,12},{15,13},{10,14},{11,... | collective-permute-start | bytes 393224 | tf_op jit(solution)/shard_map/ppermute | solution.py:289
  10.2 5.7 %collective-permute-start.1 = (bf16[128,512]{1,0:T(8,128)(2,1)S(1)}, bf16[128,512]{1,0:T(8,128)(2,1)S(1)}, u32[]{:S(2)}, u32[]{:S(2)}) collective-permute-start(bf16[128,512]{1,0:T(8,128)(2,1)S(1)} %collective-permute-done.refs_1_), channel_id=1, source_target_pairs={{0,4},{1,5},{4,8},{5,9},{8,12},{9,13},{12,14},{13,15},{14,10},{15,... | collective-permute-start | bytes 393224 | tf_op jit(solution)/shard_map/ppermute | solution.py:289
  10.4 6.0 %collective-permute-start.14 = (bf16[128,512]{1,0:T(8,128)(2,1)S(1)}, bf16[128,512]{1,0:T(8,128)(2,1)S(1)}, u32[]{:S(2)}, u32[]{:S(2)}) collective-permute-start(bf16[128,512]{1,0:T(8,128)(2,1)S(1)} %collective-permute-done.13.refs_2_), channel_id=1, source_target_pairs={{4,0},{5,1},{8,4},{9,5},{12,8},{13,9},{14,12},{15,13},{10,14},{11,... | collective-permute-start | bytes 393224 | tf_op jit(solution)/shard_map/ppermute | solution.py:289
  13.0 5.6 %collective-permute-start.16 = (bf16[128,512]{1,0:T(8,128)(2,1)S(1)}, bf16[128,512]{1,0:T(8,128)(2,1)S(1)}, u32[]{:S(2)}, u32[]{:S(2)}) collective-permute-start(bf16[128,512]{1,0:T(8,128)(2,1)S(1)} %collective-permute-done.15.refs_6_), channel_id=1, source_target_pairs={{0,4},{1,5},{4,8},{5,9},{8,12},{9,13},{12,14},{13,15},{14,10},{15,... | collective-permute-start | bytes 393224 | tf_op jit(solution)/shard_map/ppermute | solution.py:289
  13.2 5.5 %collective-permute-start.9 = (bf16[4,128,128]{2,1,0:T(8,128)(2,1)S(1)}, bf16[4,128,128]{2,1,0:T(8,128)(2,1)S(1)}, u32[]{:S(2)}, u32[]{:S(2)}) collective-permute-start(bf16[4,128,128]{2,1,0:T(8,128)(2,1)S(1)} %copy-done.9), channel_id=1, source_target_pairs={{0,1},{1,0},{2,3},{3,2},{4,5},{5,4},{6,7},{7,6},{8,9},{9,8},{10,11... | collective-permute-start | bytes 393224 | tf_op jit(solution)/shard_map/ppermute | solution.py:289
  14.0 5.9 %collective-permute-start.8 = (bf16[128,512]{1,0:T(8,128)(2,1)S(1)}, bf16[128,512]{1,0:T(8,128)(2,1)S(1)}, u32[]{:S(2)}, u32[]{:S(2)}) collective-permute-start(bf16[128,512]{1,0:T(8,128)(2,1)S(1)} %collective-permute-done.6.refs_9_), channel_id=1, source_target_pairs={{4,0},{5,1},{8,4},{9,5},{12,8},{13,9},{14,12},{15,13},{10,14},{11,... | collective-permute-start | bytes 393224 | tf_op jit(solution)/shard_map/ppermute | solution.py:289
  15.9 6.3 %collective-permute-start.2 = (bf16[128,512]{1,0:T(8,128)(2,1)S(1)}, bf16[128,512]{1,0:T(8,128)(2,1)S(1)}, u32[]{:S(2)}, u32[]{:S(2)}) collective-permute-start(bf16[128,512]{1,0:T(8,128)(2,1)S(1)} %collective-permute-done.1.refs_3_), channel_id=1, source_target_pairs={{0,4},{1,5},{4,8},{5,9},{8,12},{9,13},{12,14},{13,15},{14,10},{15,... | collective-permute-start | bytes 393224 | tf_op jit(solution)/shard_map/ppermute | solution.py:289
  16.4 7.4 %collective-permute-start.17 = (bf16[128,512]{1,0:T(8,128)(2,1)S(1)}, bf16[128,512]{1,0:T(8,128)(2,1)S(1)}, u32[]{:S(2)}, u32[]{:S(2)}) collective-permute-start(bf16[128,512]{1,0:T(8,128)(2,1)S(1)} %collective-permute-done.14.refs_4_), channel_id=1, source_target_pairs={{4,0},{5,1},{8,4},{9,5},{12,8},{13,9},{14,12},{15,13},{10,14},{11,... | collective-permute-start | bytes 393224 | tf_op jit(solution)/shard_map/ppermute | solution.py:289
  18.6 6.5 %collective-permute-start.18 = (bf16[128,512]{1,0:T(8,128)(2,1)S(1)}, bf16[128,512]{1,0:T(8,128)(2,1)S(1)}, u32[]{:S(2)}, u32[]{:S(2)}) collective-permute-start(bf16[128,512]{1,0:T(8,128)(2,1)S(1)} %collective-permute-done.16.refs_8_), channel_id=1, source_target_pairs={{0,4},{1,5},{4,8},{5,9},{8,12},{9,13},{12,14},{13,15},{14,10},{15,... | collective-permute-start | bytes 393224 | tf_op jit(solution)/shard_map/ppermute | solution.py:289
  19.9 7.8 %collective-permute-start.10 = (bf16[128,512]{1,0:T(8,128)(2,1)S(1)}, bf16[128,512]{1,0:T(8,128)(2,1)S(1)}, u32[]{:S(2)}, u32[]{:S(2)}) collective-permute-start(bf16[128,512]{1,0:T(8,128)(2,1)S(1)} %collective-permute-done.8.refs_3_), channel_id=1, source_target_pairs={{4,0},{5,1},{8,4},{9,5},{12,8},{13,9},{14,12},{15,13},{10,14},{11,... | collective-permute-start | bytes 393224 | tf_op jit(solution)/shard_map/ppermute | solution.py:289
  22.2 5.0 %collective-permute-start.3 = (bf16[128,512]{1,0:T(8,128)(2,1)S(1)}, bf16[128,512]{1,0:T(8,128)(2,1)S(1)}, u32[]{:S(2)}, u32[]{:S(2)}) collective-permute-start(bf16[128,512]{1,0:T(8,128)(2,1)S(1)} %collective-permute-done.2.refs_0_), channel_id=1, source_target_pairs={{0,4},{1,5},{4,8},{5,9},{8,12},{9,13},{12,14},{13,15},{14,10},{15,... | collective-permute-start | bytes 393224 | tf_op jit(solution)/shard_map/ppermute | solution.py:289
  23.8 2.2 %copy-start.10 = (s32[3,4,512]{2,1,0:T(4,128)S(1)}, s32[3,4,512]{2,1,0:T(4,128)}, u32[]{:S(2)}) copy-start(s32[3,4,512]{2,1,0:T(4,128)} %index_ref.1) | copy-start | bytes 73732
  25.9 3.2 %collective-permute-start.19 = (f32[3,128,512]{2,1,0:T(8,128)S(1)}, f32[3,128,512]{2,1,0:T(8,128)S(1)}, u32[]{:S(2)}, u32[]{:S(2)}) collective-permute-start(f32[3,128,512]{2,1,0:T(8,128)S(1)} %get-tuple-element.47.refs_0_), channel_id=1, source_target_pairs={{0,1},{1,0},{2,3},{3,2},{4,5},{5,4},{6,7},{7,6},{8,9},{9,8},{10,11... | collective-permute-start | bytes 2359304 | tf_op jit(solution)/shard_map/ppermute | solution.py:289
  27.1 1.0 %copy-start.2 = (f32[1,4,128,128]{3,2,1,0:T(8,128)S(1)}, f32[1,4,128,128]{3,2,1,0:T(8,128)}, u32[]{:S(2)}) copy-start(f32[1,4,128,128]{3,2,1,0:T(8,128)} %param.16) | copy-start | bytes 786436
  27.1 1.0 %copy-start.3 = (f32[1,4,128,128]{3,2,1,0:T(8,128)S(1)}, f32[1,4,128,128]{3,2,1,0:T(8,128)}, u32[]{:S(2)}) copy-start(f32[1,4,128,128]{3,2,1,0:T(8,128)} %param.17) | copy-start | bytes 786436
  27.1 1.1 %copy-start.4 = (f32[1,4,128,128]{3,2,1,0:T(8,128)S(1)}, f32[1,4,128,128]{3,2,1,0:T(8,128)}, u32[]{:S(2)}) copy-start(f32[1,4,128,128]{3,2,1,0:T(8,128)} %param.18) | copy-start | bytes 786436
  27.2 1.6 %collective-permute-start.11 = (bf16[128,512]{1,0:T(8,128)(2,1)S(1)}, bf16[128,512]{1,0:T(8,128)(2,1)S(1)}, u32[]{:S(2)}, u32[]{:S(2)}) collective-permute-start(bf16[128,512]{1,0:T(8,128)(2,1)S(1)} %collective-permute-done.3.refs_0_.x_ref), channel_id=1, source_target_pairs={{0,1},{1,0},{2,3},{3,2},{4,5},{5,4},{6,7},{7,6},{8,9},{9,8},{10,11... | collective-permute-start | bytes 393224 | tf_op jit(solution)/shard_map/ppermute | solution.py:289
  27.7 1.3 %collective-permute-start.12 = (bf16[128,512]{1,0:T(8,128)(2,1)S(1)}, bf16[128,512]{1,0:T(8,128)(2,1)S(1)}, u32[]{:S(2)}, u32[]{:S(2)}) collective-permute-start(bf16[128,512]{1,0:T(8,128)(2,1)S(1)} %collective-permute-done.10.refs_1_.d_ref), channel_id=1, source_target_pairs={{0,1},{1,0},{2,3},{3,2},{4,5},{5,4},{6,7},{7,6},{8,9},{9,8},{10,11... | collective-permute-start | bytes 393224 | tf_op jit(solution)/shard_map/ppermute | solution.py:289
  28.2 0.8 %copy-start = (f32[128,128]{1,0:T(8,128)S(1)}, f32[128,128]{1,0:T(8,128)}, u32[]{:S(2)}) copy-start(f32[128,128]{1,0:T(8,128)} %constant.5.clone.refs_4_.cosines_t_ref) | copy-start | bytes 196612
  28.2 0.9 %copy-start.1 = (f32[128,128]{1,0:T(8,128)S(1)}, f32[128,128]{1,0:T(8,128)}, u32[]{:S(2)}) copy-start(f32[128,128]{1,0:T(8,128)} %constant.4.clone.refs_3_.cosines_ref) | copy-start | bytes 196612
  30.8 3.9 %collective-permute-start.20 = (f32[3,4,512]{2,1,0:T(4,128)S(1)}, f32[3,4,512]{2,1,0:T(4,128)S(1)}, u32[]{:S(2)}, u32[]{:S(2)}) collective-permute-start(f32[3,4,512]{2,1,0:T(4,128)S(1)} %get-tuple-element.59), channel_id=1, source_target_pairs={{0,16},{16,0},{1,17},{17,1},{2,18},{18,2},{3,19},{19,3},{4,20},{20... | collective-permute-start | bytes 73736 | tf_op jit(solution)/shard_map/ppermute | solution.py:457

commit v5 on v3

--- a/solution.py
+++ b/solution.py
@@ -9,8 +9,8 @@
 from jax.sharding import PartitionSpec as P
 
 MOMENTUM_DECAY = 0.999
-
 TABLES_FLOPS = 10**10
+COLUMNS_FLOPS = 10**9
 PAUSE_FLOPS = 10**9
 F32 = jnp.float32
 BF16 = jnp.bfloat16
@@ -52,29 +52,36 @@
     pre = dot_nt(wgu, x)
     dh = dot_nt(wd, d)
     gate, up = pre[: wd.shape[0]], pre[wd.shape[0] :]
-    sig = 1.0 / (1.0 + jnp.exp(-gate))
+    sig = jax.nn.sigmoid(gate)
     swish = gate * sig
     d_gate = (dh * up * sig * (1.0 + gate * (1.0 - sig))).astype(BF16)
     return d_gate, (dh * swish).astype(BF16), (swish * up).astype(BF16)
 
 
+def one_hot(numbers, lines):
+    return jnp.where(numbers == lines, 1.0, 0.0).astype(BF16)
+
+
 def tables_kernel(index_ref, *refs):
-    in_row_ref, in_col_ref, in_col_t_ref, mask_ref = refs[-4:]
-    side = mask_ref.shape[1]
+    in_row_ref, in_col_ref = refs[-2:]
+    blocks, side, keep = in_row_ref.shape
+    count = index_ref.shape[1]
     shift = int(np.log2(side))
-    matrices, count, keep = index_ref.shape
     lines = lax.broadcasted_iota(jnp.int32, (side, keep), 0)
-    for m in range(matrices):
-        for i in range(count):
-            b = m * count + i
-            index = index_ref[m, i : i + 1, :]
-            in_row = jnp.where((index >> shift) == lines, 1.0, 0.0).astype(BF16)
-            in_col = jnp.where((index & (side - 1)) == lines, 1.0, 0.0).astype(BF16)
-            in_col_t = in_col.T
-            in_row_ref[b] = in_row
-            in_col_ref[b] = in_col
-            in_col_t_ref[b] = in_col_t
-            mask_ref[b] = dot(in_row, in_col_t).astype(BF16)
+    for b in range(blocks):
+        index = index_ref[b // count, b % count : b % count + 1, :]
+        in_row_ref[b] = one_hot(index >> shift, lines)
+        in_col_ref[b] = one_hot(index & (side - 1), lines)
+
+
+def columns_kernel(index_ref, *refs):
+    out_ref = refs[-1]
+    blocks, keep, side = out_ref.shape
+    count = index_ref.shape[1]
+    lines = lax.broadcasted_iota(jnp.int32, (side, keep), 0)
+    for b in range(blocks):
+        index = index_ref[b // count, b % count : b % count + 1, :]
+        out_ref[b] = one_hot(index & (side - 1), lines).T
 
 
 def pause_kernel(out_ref):
@@ -124,7 +131,7 @@
 
 
 def moment_step(
-    grads, mom_refs, in_row_ref, in_col_ref, mask_ref, cosines_ref, cosines_t_ref, moment_ref, kept_ref, band_ref
+    grads, mom_refs, in_row_ref, in_col_ref, cosines_ref, cosines_t_ref, moment_ref, coeffs_ref, band_ref
 ):
     side = cosines_ref.shape[0]
     count = mom_refs[0].shape[0]
@@ -143,7 +150,7 @@
         for i in range(count):
             b = m * count + i
             block = coeffs[b * side : (b + 1) * side]
-            kept_ref[b] = block * mask_ref[b].astype(F32)
+            coeffs_ref[b] = block
             hi, lo = split2(block)
             in_col = in_col_ref[b]
             at_col = dot(jnp.concatenate([hi, lo], axis=1), jnp.concatenate([in_col, in_col], axis=0))
@@ -168,13 +175,14 @@
     moment_step([grad_ref[m] for m in range(3)], refs[:3], *refs[3:])
 
 
-def residual_kernel(moment_ref, kept_ref, in_col_t_ref, cosines_ref, cosines_t_ref, *outs):
+def residual_kernel(moment_ref, coeffs_ref, in_row_ref, in_col_t_ref, cosines_ref, cosines_t_ref, *outs):
     *residuals, decoded_ref, cells_ref = outs
     side = cosines_ref.shape[0]
     count = residuals[0].shape[0]
     blocks = range(3 * count)
     cosines = cosines_ref[...]
-    inner = dot3(jnp.concatenate([kept_ref[b] for b in blocks], axis=0), cosines)
+    band = [coeffs_ref[b] * dot(in_row_ref[b], in_col_t_ref[b]) for b in blocks]
+    inner = dot3(jnp.concatenate(band, axis=0), cosines)
     inner = jnp.concatenate([inner[b * side : (b + 1) * side] for b in blocks], axis=1)
     decoded = dot3(cosines_t_ref[...], inner)
     for b in blocks:
@@ -225,21 +233,21 @@
     return forward, [(b, a) for a, b in forward], chips
 
 
+def after(kernel, out_shape, flops, band_index, *ahead):
+    in_place = dict.fromkeys(range(1, 1 + len(ahead)), pl.ANY)
+    return call(kernel, out_shape, flops, band_index, *ahead, in_place=in_place)
+
+
 def band_tables(band_index, side, *ahead):
     blocks, keep = band_index.shape[0] * band_index.shape[1], band_index.shape[2]
-    return call(
-        tables_kernel,
-        (
-            jax.ShapeDtypeStruct((blocks, side, keep), BF16),
-            jax.ShapeDtypeStruct((blocks, side, keep), BF16),
-            jax.ShapeDtypeStruct((blocks, keep, side), BF16),
-            jax.ShapeDtypeStruct((blocks, side, side), BF16),
-        ),
-        TABLES_FLOPS,
-        band_index,
-        *ahead,
-        in_place=dict.fromkeys(range(1, 1 + len(ahead)), pl.ANY),
-    )
+    hots = jax.ShapeDtypeStruct((blocks, side, keep), BF16)
+    return after(tables_kernel, (hots, hots), TABLES_FLOPS, band_index, *ahead)
+
+
+def band_columns(band_index, side, *ahead):
+    blocks, keep = band_index.shape[0] * band_index.shape[1], band_index.shape[2]
+    hots = jax.ShapeDtypeStruct((blocks, keep, side), BF16)
+    return after(columns_kernel, hots, COLUMNS_FLOPS, band_index, *ahead)
 
 
 def column_moments(x, d, weights, momenta, band_index, cosines, cosines_t, shapes):
@@ -313,7 +321,8 @@
     )
     got = send(partner, swap)
     x_swap, d_swap = send(x_last, swap), send(d_last, swap)
-    in_row, in_col, in_col_t, mask = band_tables(band_index, side, x_last, d_last)
+    in_col_t = band_columns(band_index, side, partner)
+    in_row, in_col = band_tables(band_index, side, x_last, d_last)
     moments = call(
         late_kernel,
         shapes,
@@ -329,7 +338,6 @@
         *momenta,
         in_row,
         in_col,
-        mask,
         cosines,
         cosines_t,
     )
@@ -339,7 +347,8 @@
 def shared_column_moments(x, d, weights, momenta, band_index, cosines, cosines_t, shapes):
     gate_weight, up_weight, down_weight = weights
     own = shared_column_grads(x, d, gate_weight, up_weight, down_weight)
-    in_row, in_col, in_col_t, mask = band_tables(band_index, cosines.shape[0], own)
+    in_col_t = band_columns(band_index, cosines.shape[0], own)
+    in_row, in_col = band_tables(band_index, cosines.shape[0], own)
     moments = call(
         moment_kernel,
         shapes,
@@ -348,7 +357,6 @@
         *momenta,
         in_row,
         in_col,
-        mask,
         cosines,
         cosines_t,
     )
@@ -403,7 +411,7 @@
     cosines, cosines_t = jnp.asarray(dct_table(side)), jnp.asarray(dct_table(side).T)
     blocks = 3 * blk_dev
     dense = jax.ShapeDtypeStruct((blocks, side, side), F32)
-    (moment, kept, band), in_row, in_col_t = step(
+    (moment, coeffs, band), in_row, in_col_t = step(
         x_in[0],
         d_out[0],
         (gate_weight, up_weight, down_weight),
@@ -427,7 +435,8 @@
         (result,) * 3 + (dense, jax.ShapeDtypeStruct((*in_col_t.shape[:2], 2 * side), BF16)),
         flops,
         moment,
-        kept,
+        coeffs,
+        in_row,
         in_col_t,
         cosines,
         cosines_t,

time: 36.7 us -> 36.5 us (level)
  waiting for transfers between devices: 9.83 us -> 9.44 us
    ppermute x1, waiting for transfers between devices: 0.73 us -> 0.35 us  [per_device(): lax.ppermute(band, 'rep', [(r, (r + s) % reps) for r in range(reps)])]
    pallas_call x7 -> x8, Pallas kernels: 8.85 us -> 9.05 us  [call(): pl.pallas_call(kernel, out_shape=out_shape, in_specs=specs, scratch_shape...]
  transfers between devices with their start and end apart: 21 -> 21, of which waited for: 12 -> 14; matrix products, arithmetic and copies ran while one was open for 0% -> 0% of each run, Pallas kernels for 14% -> 15%
where the time goes in v5:
time: 36.5 us; the launch traced here: 36.4 us
  starting transfers between devices  17 us (47%)
  waiting for transfers between devices  9.44 us (26%)
  Pallas kernels  9.05 us (25%)
  between operations  0.82 us (2%)
    ppermute x20, starting transfers between devices, send(): return lax.ppermute(value, 'fsdp', perm)  15.4 us
    ppermute x20, waiting for transfers between devices, send(): return lax.ppermute(value, 'fsdp', perm)  9.1 us
    pallas_call x8, Pallas kernels, call(): pl.pallas_call(kernel, out_shape=out_shape, in_specs=specs, scratch_shape...  9.05 us
    ppermute x1, starting transfers between devices, per_device(): lax.ppermute(band, 'rep', [(r, (r + s) % reps) for r in range(reps)])  1.58 us
  transfers between devices with their start and end apart: 21, of which 14 were waited for; matrix products, arithmetic and copies ran while one was open for 0% of the time, Pallas kernels for 15%

profile of v5, /device:TPU:0, one launch (start us, length us, event | category | flops | bytes accessed | tf_op | source)
XLA Modules:
  0.0 36.4 jit_solution(14277215420768895047)
XLA Ops:
  0.6 3.0 %collective-permute-start.5 = (bf16[128,512]{1,0:T(8,128)(2,1)}, bf16[128,512]{1,0:T(8,128)(2,1)S(1)}, u32[]{:S(2)}, u32[]{:S(2)}) collective-permute-start(bf16[128,512]{1,0:T(8,128)(2,1)} %bitcast.16), channel_id=1, source_target_pairs={{4,0},{5,1},{8,4},{9,5},{12,8},{13,9},{14,12},{15,13},{10,14},{11,... | collective-permute-start | bytes 393224 | tf_op jit(solution)/shard_map/ppermute | solution.py:261
  3.6 0.0 collective-permute-start.6
  3.6 0.0 copy-start.6
  3.6 0.0 copy-start.7
  3.7 0.2 collective-permute-start
  3.9 1.8 %collective-permute-start.13 = (bf16[128,512]{1,0:T(8,128)(2,1)}, bf16[128,512]{1,0:T(8,128)(2,1)S(1)}, u32[]{:S(2)}, u32[]{:S(2)}) collective-permute-start(bf16[128,512]{1,0:T(8,128)(2,1)} %bitcast.14), channel_id=1, source_target_pairs={{4,0},{5,1},{8,4},{9,5},{12,8},{13,9},{14,12},{15,13},{10,14},{11,... | collective-permute-start | bytes 393224 | tf_op jit(solution)/shard_map/ppermute | solution.py:261
  5.7 0.2 collective-permute-start.15
  5.9 1.7 %collective-permute-done.5.refs_7_ = bf16[128,512]{1,0:T(8,128)(2,1)S(1)} collective-permute-done((bf16[128,512]{1,0:T(8,128)(2,1)}, bf16[128,512]{1,0:T(8,128)(2,1)S(1)}, u32[]{:S(2)}, u32[]{:S(2)}) %collective-permute-start.5) | collective-permute-done | bytes 131104 | tf_op jit(solution)/shard_map/ppermute | solution.py:261
  7.6 0.0 copy-done.8
  7.6 0.0 collective-permute-start.8
  7.6 0.0 collective-permute-done.6.refs_13_
  7.6 1.8 %collective-permute-start.7 = (bf16[128,512]{1,0:T(8,128)(2,1)S(1)}, bf16[128,512]{1,0:T(8,128)(2,1)S(1)}, u32[]{:S(2)}, u32[]{:S(2)}) collective-permute-start(bf16[128,512]{1,0:T(8,128)(2,1)S(1)} %collective-permute-done.5.refs_7_), channel_id=1, source_target_pairs={{4,0},{5,1},{8,4},{9,5},{12,8},{13,9},{14,12},{15,13},{10,14},{11,... | collective-permute-start | bytes 393224 | tf_op jit(solution)/shard_map/ppermute | solution.py:261
  9.4 0.8 %collective-permute-done.refs_1_ = bf16[128,512]{1,0:T(8,128)(2,1)S(1)} collective-permute-done((bf16[128,512]{1,0:T(8,128)(2,1)}, bf16[128,512]{1,0:T(8,128)(2,1)S(1)}, u32[]{:S(2)}, u32[]{:S(2)}) %collective-permute-start) | collective-permute-done | bytes 131104 | tf_op jit(solution)/shard_map/ppermute | solution.py:261
  10.2 0.2 collective-permute-start.1
  10.4 0.0 collective-permute-done.13.refs_2_
  10.4 1.8 %collective-permute-start.14 = (bf16[128,512]{1,0:T(8,128)(2,1)S(1)}, bf16[128,512]{1,0:T(8,128)(2,1)S(1)}, u32[]{:S(2)}, u32[]{:S(2)}) collective-permute-start(bf16[128,512]{1,0:T(8,128)(2,1)S(1)} %collective-permute-done.13.refs_2_), channel_id=1, source_target_pairs={{4,0},{5,1},{8,4},{9,5},{12,8},{13,9},{14,12},{15,13},{10,14},{11,... | collective-permute-start | bytes 393224 | tf_op jit(solution)/shard_map/ppermute | solution.py:261
  12.2 0.8 %collective-permute-done.15.refs_6_ = bf16[128,512]{1,0:T(8,128)(2,1)S(1)} collective-permute-done((bf16[128,512]{1,0:T(8,128)(2,1)}, bf16[128,512]{1,0:T(8,128)(2,1)S(1)}, u32[]{:S(2)}, u32[]{:S(2)}) %collective-permute-start.15) | collective-permute-done | bytes 131104 | tf_op jit(solution)/shard_map/ppermute | solution.py:261
  13.0 0.2 collective-permute-start.16
  13.2 0.0 collective-permute-done.8.refs_14_
  13.2 0.0 copy-done.9
  13.2 0.0 collective-permute-start.10
  13.2 0.8 %collective-permute-done.7.refs_9_ = bf16[128,512]{1,0:T(8,128)(2,1)S(1)} collective-permute-done((bf16[128,512]{1,0:T(8,128)(2,1)S(1)}, bf16[128,512]{1,0:T(8,128)(2,1)S(1)}, u32[]{:S(2)}, u32[]{:S(2)}) %collective-permute-start.7) | collective-permute-done | bytes 131104 | tf_op jit(solution)/shard_map/ppermute | solution.py:261
  14.0 1.7 %collective-permute-start.9 = (bf16[128,512]{1,0:T(8,128)(2,1)S(1)}, bf16[128,512]{1,0:T(8,128)(2,1)S(1)}, u32[]{:S(2)}, u32[]{:S(2)}) collective-permute-start(bf16[128,512]{1,0:T(8,128)(2,1)S(1)} %collective-permute-done.7.refs_9_), channel_id=1, source_target_pairs={{4,0},{5,1},{8,4},{9,5},{12,8},{13,9},{14,12},{15,13},{10,14},{11,... | collective-permute-start | bytes 393224 | tf_op jit(solution)/shard_map/ppermute | solution.py:261
  15.7 0.2 collective-permute-done.1.refs_3_
  15.9 0.2 collective-permute-start.2
  16.1 0.3 collective-permute-done.14.refs_4_
  16.4 1.7 %collective-permute-start.17 = (bf16[128,512]{1,0:T(8,128)(2,1)S(1)}, bf16[128,512]{1,0:T(8,128)(2,1)S(1)}, u32[]{:S(2)}, u32[]{:S(2)}) collective-permute-start(bf16[128,512]{1,0:T(8,128)(2,1)S(1)} %collective-permute-done.14.refs_4_), channel_id=1, source_target_pairs={{4,0},{5,1},{8,4},{9,5},{12,8},{13,9},{14,12},{15,13},{10,14},{11,... | collective-permute-start | bytes 393224 | tf_op jit(solution)/shard_map/ppermute | solution.py:261
  18.1 0.5 %collective-permute-done.16.refs_8_ = bf16[128,512]{1,0:T(8,128)(2,1)S(1)} collective-permute-done((bf16[128,512]{1,0:T(8,128)(2,1)S(1)}, bf16[128,512]{1,0:T(8,128)(2,1)S(1)}, u32[]{:S(2)}, u32[]{:S(2)}) %collective-permute-start.16) | collective-permute-done | bytes 131104 | tf_op jit(solution)/shard_map/ppermute | solution.py:261
  18.6 0.1 collective-permute-start.18
  18.7 0.0 collective-permute-done.10.refs_15_
  18.7 1.2 %collective-permute-done.9.refs_3_ = bf16[128,512]{1,0:T(8,128)(2,1)S(1)} collective-permute-done((bf16[128,512]{1,0:T(8,128)(2,1)S(1)}, bf16[128,512]{1,0:T(8,128)(2,1)S(1)}, u32[]{:S(2)}, u32[]{:S(2)}) %collective-permute-start.9) | collective-permute-done | bytes 131104 | tf_op jit(solution)/shard_map/ppermute | solution.py:261
  19.9 1.9 %collective-permute-start.11 = (bf16[128,512]{1,0:T(8,128)(2,1)S(1)}, bf16[128,512]{1,0:T(8,128)(2,1)S(1)}, u32[]{:S(2)}, u32[]{:S(2)}) collective-permute-start(bf16[128,512]{1,0:T(8,128)(2,1)S(1)} %collective-permute-done.9.refs_3_), channel_id=1, source_target_pairs={{4,0},{5,1},{8,4},{9,5},{12,8},{13,9},{14,12},{15,13},{10,14},{11,... | collective-permute-start | bytes 393224 | tf_op jit(solution)/shard_map/ppermute | solution.py:261
  21.8 0.4 %collective-permute-done.2.refs_0_ = bf16[128,512]{1,0:T(8,128)(2,1)S(1)} collective-permute-done((bf16[128,512]{1,0:T(8,128)(2,1)S(1)}, bf16[128,512]{1,0:T(8,128)(2,1)S(1)}, u32[]{:S(2)}, u32[]{:S(2)}) %collective-permute-start.2) | collective-permute-done | bytes 131104 | tf_op jit(solution)/shard_map/ppermute | solution.py:261
  22.2 0.0 collective-permute-start.3
  22.3 0.0 copy-done.7
  22.3 1.6 %shard_map.155 = (f32[3,128,512]{2,1,0:T(8,128)S(1)}, f32[3,128,512]{2,1,0:T(8,128)S(1)}, bf16[512,512]{1,0:T(8,128)(2,1)S(1)}, bf16[256,512]{1,0:T(8,128)(2,1)S(1)}) custom-call(bf16[128,512]{1,0:T(8,128)(2,1)S(1)} %bitcast.15, bf16[128,512]{1,0:T(8,128)(2,1)S(1)} %collective-permute-done.refs_1_, bf16[128,512]{1,0:T(8,128)(2,1)S(1)} %collective-permute-done.13.refs_2_, ...), custom_call_target="tpu_custom_call" | custom-call | flops 1006632960 | bytes 4202496 | tf_op jit(solution)/shard_map/pallas_call | solution.py:217
  23.8 0.0 copy-start.10
  23.8 0.0 collective-permute-done.17.refs_1_
  23.8 1.2 %collective-permute-done.18.refs_2_ = bf16[128,512]{1,0:T(8,128)(2,1)S(1)} collective-permute-done((bf16[128,512]{1,0:T(8,128)(2,1)S(1)}, bf16[128,512]{1,0:T(8,128)(2,1)S(1)}, u32[]{:S(2)}, u32[]{:S(2)}) %collective-permute-start.18) | collective-permute-done | bytes 131104 | tf_op jit(solution)/shard_map/ppermute | solution.py:261
  25.0 0.9 %shard_map.156 = (f32[3,128,512]{2,1,0:T(8,128)S(1)}, f32[3,128,512]{2,1,0:T(8,128)S(1)}) custom-call(bf16[128,512]{1,0:T(8,128)(2,1)S(1)} %collective-permute-done.2.refs_0_, bf16[128,512]{1,0:T(8,128)(2,1)S(1)} %collective-permute-done.17.refs_1_, bf16[128,512]{1,0:T(8,128)(2,1)S(1)} %collective-permute-done.18.refs_2_, ...), custom_call_target="tpu_custom_call" | custom-call | flops 402653184 | bytes 5767168 | tf_op jit(solution)/shard_map/pallas_call | solution.py:217
  25.9 0.1 collective-permute-start.19
  26.0 0.5 %shard_map.159.in_col_t_ref = bf16[12,512,128]{2,1,0:T(8,128)(2,1)S(1)} custom-call(s32[3,4,512]{2,1,0:T(4,128)S(1)} %copy-done.10, f32[3,128,512]{2,1,0:T(8,128)S(1)} %get-tuple-element.46.refs_0_), custom_call_target="tpu_custom_call" | custom-call | flops 1000000000 | bytes 1622016 | tf_op jit(solution)/shard_map/pallas_call | solution.py:217
  26.5 0.0 copy-start
  26.5 0.0 copy-start.1
  26.5 0.0 copy-start.2
  26.5 0.0 copy-start.3
  26.5 0.0 copy-start.4
  26.5 0.7 %collective-permute-done.3.refs_0_ = bf16[128,512]{1,0:T(8,128)(2,1)S(1)} collective-permute-done((bf16[128,512]{1,0:T(8,128)(2,1)S(1)}, bf16[128,512]{1,0:T(8,128)(2,1)S(1)}, u32[]{:S(2)}, u32[]{:S(2)}) %collective-permute-start.3) | collective-permute-done | bytes 131104 | tf_op jit(solution)/shard_map/ppermute | solution.py:261
  27.2 0.0 collective-permute-start.4
  27.2 0.0 collective-permute-done.11.refs_1_.refs_2_
  27.2 0.5 %collective-permute-start.12 = (bf16[128,512]{1,0:T(8,128)(2,1)S(1)}, bf16[128,512]{1,0:T(8,128)(2,1)S(1)}, u32[]{:S(2)}, u32[]{:S(2)}) collective-permute-start(bf16[128,512]{1,0:T(8,128)(2,1)S(1)} %collective-permute-done.11.refs_1_.refs_2_), channel_id=1, source_target_pairs={{0,1},{1,0},{2,3},{3,2},{4,5},{5,4},{6,7},{7,6},{8,9},{9,8},{10,11... | collective-permute-start | bytes 393224 | tf_op jit(solution)/shard_map/ppermute | solution.py:261
  27.7 0.5 %shard_map.157 = (bf16[12,128,512]{2,1,0:T(8,128)(2,1)S(1)}, bf16[12,128,512]{2,1,0:T(8,128)(2,1)S(1)}) custom-call(s32[3,4,512]{2,1,0:T(4,128)S(1)} %copy-done.10, bf16[128,512]{1,0:T(8,128)(2,1)S(1)} %collective-permute-done.3.refs_0_, bf16[128,512]{1,0:T(8,128)(2,1)S(1)} %collective-permute-done.11.refs_1_.refs_2_), custom_call_target="tpu_custom_call" | custom-call | flops 10000000000 | bytes 573440 | tf_op jit(solution)/shard_map/pallas_call | solution.py:217
  28.2 0.3 collective-permute-done.4.refs_1_
  28.5 0.2 collective-permute-done.12.refs_3_
  28.7 0.0 collective-permute-done.19.refs_7_
  28.7 0.0 copy-done.1
  28.7 0.0 copy-done.2
  28.8 0.0 copy-done.3
  28.8 0.0 copy-done.4
  28.8 1.7 %shard_map.158 = (f32[12,128,128]{2,1,0:T(8,128)S(1)}, f32[12,128,128]{2,1,0:T(8,128)S(1)}, f32[3,4,512]{2,1,0:T(4,128)S(1)}) custom-call(bf16[128,512]{1,0:T(8,128)(2,1)S(1)} %collective-permute-done.3.refs_0_, bf16[128,512]{1,0:T(8,128)(2,1)S(1)} %collective-permute-done.4.refs_1_, bf16[128,512]{1,0:T(8,128)(2,1)S(1)} %collective-permute-done.11.refs_1_.refs_2_, ...), custom_call_target="tpu_custom_call" | custom-call | flops 1000000000 | bytes 13893632 | tf_op jit(solution)/shard_map/pallas_call | solution.py:217
  30.5 1.6 %collective-permute-start.20 = (f32[3,4,512]{2,1,0:T(4,128)S(1)}, f32[3,4,512]{2,1,0:T(4,128)S(1)}, u32[]{:S(2)}, u32[]{:S(2)}) collective-permute-start(f32[3,4,512]{2,1,0:T(4,128)S(1)} %get-tuple-element.55), channel_id=1, source_target_pairs={{0,16},{16,0},{1,17},{17,1},{2,18},{18,2},{3,19},{19,3},{4,20},{20... | collective-permute-start | bytes 73736 | tf_op jit(solution)/shard_map/ppermute | solution.py:427
  32.1 2.0 %shard_map.160 = (f32[4,128,128]{2,1,0:T(8,128)}, f32[4,128,128]{2,1,0:T(8,128)}, f32[4,128,128]{2,1,0:T(8,128)}, f32[12,128,128]{2,1,0:T(8,128)S(1)}, bf16[12,512,256]{2,1,0:T(8,128)(2,1)S(1)}) custom-call(f32[12,128,128]{2,1,0:T(8,128)S(1)} %get-tuple-element.49.moment_ref, f32[12,128,128]{2,1,0:T(8,128)S(1)} %get-tuple-element.50.coeffs_ref, ...), custom_call_target="tpu_custom_call" | custom-call | flops 301989888 | bytes 9699328 | tf_op jit(solution)/shard_map/pallas_call | solution.py:217
  34.1 0.3 collective-permute-done.20
  34.4 2.0 %shard_map.161 = (f32[4,128,128]{2,1,0:T(8,128)}, f32[4,128,128]{2,1,0:T(8,128)}, f32[4,128,128]{2,1,0:T(8,128)}) custom-call(f32[12,128,128]{2,1,0:T(8,128)S(1)} %get-tuple-element.54.decoded_ref, f32[1,3,4,512]{3,2,1,0:T(4,128)S(1)} %bitcast.12, bf16[12,128,512]{2,1,0:T(8,128)(2,1)S(1)} %get-tuple-element.47.refs_11_.in_row_ref, ...), custom_call_target="tpu_custom_call" | custom-call | flops 301989888 | bytes 11190272 | tf_op jit(solution)/shard_map/pallas_call | solution.py:217
  (8 shorter events, 0.0 us)
Async XLA Ops:
  0.6 7.0 %collective-permute-start.5 = (bf16[128,512]{1,0:T(8,128)(2,1)}, bf16[128,512]{1,0:T(8,128)(2,1)S(1)}, u32[]{:S(2)}, u32[]{:S(2)}) collective-permute-start(bf16[128,512]{1,0:T(8,128)(2,1)} %bitcast.16), channel_id=1, source_target_pairs={{4,0},{5,1},{8,4},{9,5},{12,8},{13,9},{14,12},{15,13},{10,14},{11,... | collective-permute-start | bytes 393224 | tf_op jit(solution)/shard_map/ppermute | solution.py:261
  3.6 4.0 %collective-permute-start.6 = (bf16[4,128,128]{2,1,0:T(8,128)(2,1)}, bf16[4,128,128]{2,1,0:T(8,128)(2,1)S(1)}, u32[]{:S(2)}, u32[]{:S(2)}) collective-permute-start(bf16[4,128,128]{2,1,0:T(8,128)(2,1)} %refs_10_.1), channel_id=1, source_target_pairs={{0,1},{1,0},{2,3},{3,2},{4,5},{5,4},{6,7},{7,6},{8,9},{9,8},{10,11... | collective-permute-start | bytes 393224 | tf_op jit(solution)/shard_map/ppermute | solution.py:261
  3.6 4.0 %copy-start.8 = (bf16[4,128,128]{2,1,0:T(8,128)(2,1)S(1)}, bf16[4,128,128]{2,1,0:T(8,128)(2,1)}, u32[]{:S(2)}) copy-start(bf16[4,128,128]{2,1,0:T(8,128)(2,1)} %refs_11_.1) | copy-start | bytes 393220
  3.6 9.6 %copy-start.9 = (bf16[4,128,128]{2,1,0:T(8,128)(2,1)S(1)}, bf16[4,128,128]{2,1,0:T(8,128)(2,1)}, u32[]{:S(2)}) copy-start(bf16[4,128,128]{2,1,0:T(8,128)(2,1)} %refs_12_.1) | copy-start | bytes 393220
  3.6 18.6 %copy-start.5 = (bf16[1,128,512]{2,1,0:T(8,128)(2,1)S(1)}, bf16[1,128,512]{2,1,0:T(8,128)(2,1)}, u32[]{:S(2)}) copy-start(bf16[1,128,512]{2,1,0:T(8,128)(2,1)} %param.11) | copy-start | bytes 393220
  3.6 18.6 %copy-start.6 = (bf16[1,128,512]{2,1,0:T(8,128)(2,1)S(1)}, bf16[1,128,512]{2,1,0:T(8,128)(2,1)}, u32[]{:S(2)}) copy-start(bf16[1,128,512]{2,1,0:T(8,128)(2,1)} %param.12) | copy-start | bytes 393220
  3.6 18.6 %copy-start.7 = (bf16[4,128,128]{2,1,0:T(8,128)(2,1)S(1)}, bf16[4,128,128]{2,1,0:T(8,128)(2,1)}, u32[]{:S(2)}) copy-start(bf16[4,128,128]{2,1,0:T(8,128)(2,1)} %refs_10_.1) | copy-start | bytes 393220
  3.7 6.6 %collective-permute-start = (bf16[128,512]{1,0:T(8,128)(2,1)}, bf16[128,512]{1,0:T(8,128)(2,1)S(1)}, u32[]{:S(2)}, u32[]{:S(2)}) collective-permute-start(bf16[128,512]{1,0:T(8,128)(2,1)} %bitcast.13), channel_id=1, source_target_pairs={{0,4},{1,5},{4,8},{5,9},{8,12},{9,13},{12,14},{13,15},{14,10},{15,... | collective-permute-start | bytes 393224 | tf_op jit(solution)/shard_map/ppermute | solution.py:261
  3.9 6.5 %collective-permute-start.13 = (bf16[128,512]{1,0:T(8,128)(2,1)}, bf16[128,512]{1,0:T(8,128)(2,1)S(1)}, u32[]{:S(2)}, u32[]{:S(2)}) collective-permute-start(bf16[128,512]{1,0:T(8,128)(2,1)} %bitcast.14), channel_id=1, source_target_pairs={{4,0},{5,1},{8,4},{9,5},{12,8},{13,9},{14,12},{15,13},{10,14},{11,... | collective-permute-start | bytes 393224 | tf_op jit(solution)/shard_map/ppermute | solution.py:261
  5.7 7.3 %collective-permute-start.15 = (bf16[128,512]{1,0:T(8,128)(2,1)}, bf16[128,512]{1,0:T(8,128)(2,1)S(1)}, u32[]{:S(2)}, u32[]{:S(2)}) collective-permute-start(bf16[128,512]{1,0:T(8,128)(2,1)} %bitcast.17), channel_id=1, source_target_pairs={{0,4},{1,5},{4,8},{5,9},{8,12},{9,13},{12,14},{13,15},{14,10},{15,... | collective-permute-start | bytes 393224 | tf_op jit(solution)/shard_map/ppermute | solution.py:261
  7.6 5.6 %collective-permute-start.8 = (bf16[4,128,128]{2,1,0:T(8,128)(2,1)S(1)}, bf16[4,128,128]{2,1,0:T(8,128)(2,1)S(1)}, u32[]{:S(2)}, u32[]{:S(2)}) collective-permute-start(bf16[4,128,128]{2,1,0:T(8,128)(2,1)S(1)} %copy-done.8), channel_id=1, source_target_pairs={{0,1},{1,0},{2,3},{3,2},{4,5},{5,4},{6,7},{7,6},{8,9},{9,8},{10,11... | collective-permute-start | bytes 393224 | tf_op jit(solution)/shard_map/ppermute | solution.py:261
  7.6 6.3 %collective-permute-start.7 = (bf16[128,512]{1,0:T(8,128)(2,1)S(1)}, bf16[128,512]{1,0:T(8,128)(2,1)S(1)}, u32[]{:S(2)}, u32[]{:S(2)}) collective-permute-start(bf16[128,512]{1,0:T(8,128)(2,1)S(1)} %collective-permute-done.5.refs_7_), channel_id=1, source_target_pairs={{4,0},{5,1},{8,4},{9,5},{12,8},{13,9},{14,12},{15,13},{10,14},{11,... | collective-permute-start | bytes 393224 | tf_op jit(solution)/shard_map/ppermute | solution.py:261
  10.2 5.7 %collective-permute-start.1 = (bf16[128,512]{1,0:T(8,128)(2,1)S(1)}, bf16[128,512]{1,0:T(8,128)(2,1)S(1)}, u32[]{:S(2)}, u32[]{:S(2)}) collective-permute-start(bf16[128,512]{1,0:T(8,128)(2,1)S(1)} %collective-permute-done.refs_1_), channel_id=1, source_target_pairs={{0,4},{1,5},{4,8},{5,9},{8,12},{9,13},{12,14},{13,15},{14,10},{15,... | collective-permute-start | bytes 393224 | tf_op jit(solution)/shard_map/ppermute | solution.py:261
  10.4 6.0 %collective-permute-start.14 = (bf16[128,512]{1,0:T(8,128)(2,1)S(1)}, bf16[128,512]{1,0:T(8,128)(2,1)S(1)}, u32[]{:S(2)}, u32[]{:S(2)}) collective-permute-start(bf16[128,512]{1,0:T(8,128)(2,1)S(1)} %collective-permute-done.13.refs_2_), channel_id=1, source_target_pairs={{4,0},{5,1},{8,4},{9,5},{12,8},{13,9},{14,12},{15,13},{10,14},{11,... | collective-permute-start | bytes 393224 | tf_op jit(solution)/shard_map/ppermute | solution.py:261
  13.0 5.6 %collective-permute-start.16 = (bf16[128,512]{1,0:T(8,128)(2,1)S(1)}, bf16[128,512]{1,0:T(8,128)(2,1)S(1)}, u32[]{:S(2)}, u32[]{:S(2)}) collective-permute-start(bf16[128,512]{1,0:T(8,128)(2,1)S(1)} %collective-permute-done.15.refs_6_), channel_id=1, source_target_pairs={{0,4},{1,5},{4,8},{5,9},{8,12},{9,13},{12,14},{13,15},{14,10},{15,... | collective-permute-start | bytes 393224 | tf_op jit(solution)/shard_map/ppermute | solution.py:261
  13.2 5.5 %collective-permute-start.10 = (bf16[4,128,128]{2,1,0:T(8,128)(2,1)S(1)}, bf16[4,128,128]{2,1,0:T(8,128)(2,1)S(1)}, u32[]{:S(2)}, u32[]{:S(2)}) collective-permute-start(bf16[4,128,128]{2,1,0:T(8,128)(2,1)S(1)} %copy-done.9), channel_id=1, source_target_pairs={{0,1},{1,0},{2,3},{3,2},{4,5},{5,4},{6,7},{7,6},{8,9},{9,8},{10,11... | collective-permute-start | bytes 393224 | tf_op jit(solution)/shard_map/ppermute | solution.py:261
  14.0 5.9 %collective-permute-start.9 = (bf16[128,512]{1,0:T(8,128)(2,1)S(1)}, bf16[128,512]{1,0:T(8,128)(2,1)S(1)}, u32[]{:S(2)}, u32[]{:S(2)}) collective-permute-start(bf16[128,512]{1,0:T(8,128)(2,1)S(1)} %collective-permute-done.7.refs_9_), channel_id=1, source_target_pairs={{4,0},{5,1},{8,4},{9,5},{12,8},{13,9},{14,12},{15,13},{10,14},{11,... | collective-permute-start | bytes 393224 | tf_op jit(solution)/shard_map/ppermute | solution.py:261
  15.9 6.3 %collective-permute-start.2 = (bf16[128,512]{1,0:T(8,128)(2,1)S(1)}, bf16[128,512]{1,0:T(8,128)(2,1)S(1)}, u32[]{:S(2)}, u32[]{:S(2)}) collective-permute-start(bf16[128,512]{1,0:T(8,128)(2,1)S(1)} %collective-permute-done.1.refs_3_), channel_id=1, source_target_pairs={{0,4},{1,5},{4,8},{5,9},{8,12},{9,13},{12,14},{13,15},{14,10},{15,... | collective-permute-start | bytes 393224 | tf_op jit(solution)/shard_map/ppermute | solution.py:261
  16.4 7.4 %collective-permute-start.17 = (bf16[128,512]{1,0:T(8,128)(2,1)S(1)}, bf16[128,512]{1,0:T(8,128)(2,1)S(1)}, u32[]{:S(2)}, u32[]{:S(2)}) collective-permute-start(bf16[128,512]{1,0:T(8,128)(2,1)S(1)} %collective-permute-done.14.refs_4_), channel_id=1, source_target_pairs={{4,0},{5,1},{8,4},{9,5},{12,8},{13,9},{14,12},{15,13},{10,14},{11,... | collective-permute-start | bytes 393224 | tf_op jit(solution)/shard_map/ppermute | solution.py:261
  18.6 6.5 %collective-permute-start.18 = (bf16[128,512]{1,0:T(8,128)(2,1)S(1)}, bf16[128,512]{1,0:T(8,128)(2,1)S(1)}, u32[]{:S(2)}, u32[]{:S(2)}) collective-permute-start(bf16[128,512]{1,0:T(8,128)(2,1)S(1)} %collective-permute-done.16.refs_8_), channel_id=1, source_target_pairs={{0,4},{1,5},{4,8},{5,9},{8,12},{9,13},{12,14},{13,15},{14,10},{15,... | collective-permute-start | bytes 393224 | tf_op jit(solution)/shard_map/ppermute | solution.py:261
  19.9 7.3 %collective-permute-start.11 = (bf16[128,512]{1,0:T(8,128)(2,1)S(1)}, bf16[128,512]{1,0:T(8,128)(2,1)S(1)}, u32[]{:S(2)}, u32[]{:S(2)}) collective-permute-start(bf16[128,512]{1,0:T(8,128)(2,1)S(1)} %collective-permute-done.9.refs_3_), channel_id=1, source_target_pairs={{4,0},{5,1},{8,4},{9,5},{12,8},{13,9},{14,12},{15,13},{10,14},{11,... | collective-permute-start | bytes 393224 | tf_op jit(solution)/shard_map/ppermute | solution.py:261
  22.2 5.0 %collective-permute-start.3 = (bf16[128,512]{1,0:T(8,128)(2,1)S(1)}, bf16[128,512]{1,0:T(8,128)(2,1)S(1)}, u32[]{:S(2)}, u32[]{:S(2)}) collective-permute-start(bf16[128,512]{1,0:T(8,128)(2,1)S(1)} %collective-permute-done.2.refs_0_), channel_id=1, source_target_pairs={{0,4},{1,5},{4,8},{5,9},{8,12},{9,13},{12,14},{13,15},{14,10},{15,... | collective-permute-start | bytes 393224 | tf_op jit(solution)/shard_map/ppermute | solution.py:261
  23.8 2.2 %copy-start.10 = (s32[3,4,512]{2,1,0:T(4,128)S(1)}, s32[3,4,512]{2,1,0:T(4,128)}, u32[]{:S(2)}) copy-start(s32[3,4,512]{2,1,0:T(4,128)} %index_ref.3) | copy-start | bytes 73732
  25.9 2.8 %collective-permute-start.19 = (f32[3,128,512]{2,1,0:T(8,128)S(1)}, f32[3,128,512]{2,1,0:T(8,128)S(1)}, u32[]{:S(2)}, u32[]{:S(2)}) collective-permute-start(f32[3,128,512]{2,1,0:T(8,128)S(1)} %get-tuple-element.46.refs_0_), channel_id=1, source_target_pairs={{0,1},{1,0},{2,3},{3,2},{4,5},{5,4},{6,7},{7,6},{8,9},{9,8},{10,11... | collective-permute-start | bytes 2359304 | tf_op jit(solution)/shard_map/ppermute | solution.py:261
  26.5 2.3 %copy-start = (f32[128,128]{1,0:T(8,128)S(1)}, f32[128,128]{1,0:T(8,128)}, u32[]{:S(2)}) copy-start(f32[128,128]{1,0:T(8,128)} %constant.5.clone.refs_14_.cosines_t_ref) | copy-start | bytes 196612
  26.5 2.3 %copy-start.1 = (f32[128,128]{1,0:T(8,128)S(1)}, f32[128,128]{1,0:T(8,128)}, u32[]{:S(2)}) copy-start(f32[128,128]{1,0:T(8,128)} %constant.4.clone.refs_13_.cosines_ref) | copy-start | bytes 196612
  26.5 2.3 %copy-start.2 = (f32[1,4,128,128]{3,2,1,0:T(8,128)S(1)}, f32[1,4,128,128]{3,2,1,0:T(8,128)}, u32[]{:S(2)}) copy-start(f32[1,4,128,128]{3,2,1,0:T(8,128)} %param.16) | copy-start | bytes 786436
  26.5 2.3 %copy-start.3 = (f32[1,4,128,128]{3,2,1,0:T(8,128)S(1)}, f32[1,4,128,128]{3,2,1,0:T(8,128)}, u32[]{:S(2)}) copy-start(f32[1,4,128,128]{3,2,1,0:T(8,128)} %param.17) | copy-start | bytes 786436
  26.5 2.3 %copy-start.4 = (f32[1,4,128,128]{3,2,1,0:T(8,128)S(1)}, f32[1,4,128,128]{3,2,1,0:T(8,128)}, u32[]{:S(2)}) copy-start(f32[1,4,128,128]{3,2,1,0:T(8,128)} %param.18) | copy-start | bytes 786436
  27.2 1.3 %collective-permute-start.4 = (bf16[128,512]{1,0:T(8,128)(2,1)S(1)}, bf16[128,512]{1,0:T(8,128)(2,1)S(1)}, u32[]{:S(2)}, u32[]{:S(2)}) collective-permute-start(bf16[128,512]{1,0:T(8,128)(2,1)S(1)} %collective-permute-done.3.refs_0_), channel_id=1, source_target_pairs={{0,1},{1,0},{2,3},{3,2},{4,5},{5,4},{6,7},{7,6},{8,9},{9,8},{10,11... | collective-permute-start | bytes 393224 | tf_op jit(solution)/shard_map/ppermute | solution.py:261
  27.2 1.5 %collective-permute-start.12 = (bf16[128,512]{1,0:T(8,128)(2,1)S(1)}, bf16[128,512]{1,0:T(8,128)(2,1)S(1)}, u32[]{:S(2)}, u32[]{:S(2)}) collective-permute-start(bf16[128,512]{1,0:T(8,128)(2,1)S(1)} %collective-permute-done.11.refs_1_.refs_2_), channel_id=1, source_target_pairs={{0,1},{1,0},{2,3},{3,2},{4,5},{5,4},{6,7},{7,6},{8,9},{9,8},{10,11... | collective-permute-start | bytes 393224 | tf_op jit(solution)/shard_map/ppermute | solution.py:261
  30.5 3.9 %collective-permute-start.20 = (f32[3,4,512]{2,1,0:T(4,128)S(1)}, f32[3,4,512]{2,1,0:T(4,128)S(1)}, u32[]{:S(2)}, u32[]{:S(2)}) collective-permute-start(f32[3,4,512]{2,1,0:T(4,128)S(1)} %get-tuple-element.55), channel_id=1, source_target_pairs={{0,16},{16,0},{1,17},{17,1},{2,18},{18,2},{3,19},{19,3},{4,20},{20... | collective-permute-start | bytes 73736 | tf_op jit(solution)/shard_map/ppermute | solution.py:427

commit v6 on v5

--- a/solution.py
+++ b/solution.py
@@ -125,9 +125,16 @@
     xs, ds = refs[:shards], refs[shards : 2 * shards]
     wgu_ref, wd_ref, own_in, par_in, own_ref, par_ref, *scratch = refs[2 * shards :]
     side = own_ref.shape[1]
+    count = own_ref.shape[0] // 3
     for m, grad in enumerate(column_grads(xs, ds, wgu_ref[...], wd_ref[...], *scratch)):
-        own_ref[m] = own_in[m] + grad[:side]
-        par_ref[m] = par_in[m] + grad[side:]
+        for add_ref, out_ref, part in (
+            (own_in, own_ref, grad[:side]),
+            (par_in, par_ref, grad[side:]),
+        ):
+            total = add_ref[m] + part
+            for i in range(count):
+                piece = total[:, i * side : (i + 1) * side]
+                out_ref[m * count + i] = piece.T if m < 2 else piece
 
 
 def moment_step(
@@ -136,14 +143,10 @@
     side = cosines_ref.shape[0]
     count = mom_refs[0].shape[0]
     blocks = []
-    for m in range(3):
-        for i in range(count):
-            piece = grads[m][:, i * side : (i + 1) * side]
-            if m < 2:
-                piece = piece.T
-            block = MOMENTUM_DECAY * mom_refs[m][i] + piece
-            moment_ref[m * count + i] = block
-            blocks.append(block)
+    for b, grad in enumerate(grads):
+        block = MOMENTUM_DECAY * mom_refs[b // count][b % count] + grad
+        moment_ref[b] = block
+        blocks.append(block)
     inner = dot3(cosines_ref[...], jnp.concatenate(blocks, axis=1))
     coeffs = dot3(lanes_to_rows(inner, side), cosines_t_ref[...])
     for m in range(3):
@@ -162,17 +165,26 @@
 def late_kernel(*refs):
     xs, ds, wgu_ref, wd_ref, own_ref, got_ref = refs[:2], refs[2:4], *refs[4:8]
     side = own_ref.shape[1]
+    count = own_ref.shape[0] // 3
     x = jnp.concatenate([ref[...] for ref in xs], axis=0)
     d = jnp.concatenate([ref[...] for ref in ds], axis=0)
+    x_t = x.T
     wgu = jnp.concatenate([wgu_ref[:side, :], wgu_ref[2 * side : 3 * side, :]], axis=0)
     d_gate, d_up, hidden = activations(wgu, wd_ref[:side, :], x, d)
-    late = (dot(d_gate, x), dot(d_up, x), dot(hidden, d))
-    grads = [late[m] + (own_ref[m] + got_ref[m]) for m in range(3)]
+    g_in = dot_nt(x_t, jnp.concatenate([d_gate, d_up], axis=0))
+    g_out = dot(hidden, d)
+    late = [
+        g_in[i * side : (i + 1) * side, m * side : (m + 1) * side]
+        for m in range(2)
+        for i in range(count)
+    ]
+    late += [g_out[:, i * side : (i + 1) * side] for i in range(count)]
+    grads = [late[b] + (own_ref[b] + got_ref[b]) for b in range(3 * count)]
     moment_step(grads, refs[8:11], *refs[11:])
 
 
 def moment_kernel(grad_ref, *refs):
-    moment_step([grad_ref[m] for m in range(3)], refs[:3], *refs[3:])
+    moment_step([grad_ref[b] for b in range(grad_ref.shape[0])], refs[:3], *refs[3:])
 
 
 def residual_kernel(moment_ref, coeffs_ref, in_row_ref, in_col_t_ref, cosines_ref, cosines_t_ref, *outs):
@@ -309,7 +321,7 @@
     )
     own, partner = call(
         functools.partial(middle_kernel, 2),
-        (part, part),
+        (shapes[0], shapes[0]),
         24 * 2 * rows * width * side,
         *xs[early:],
         *ds[early:],
@@ -347,6 +359,10 @@
 def shared_column_moments(x, d, weights, momenta, band_index, cosines, cosines_t, shapes):
     gate_weight, up_weight, down_weight = weights
     own = shared_column_grads(x, d, gate_weight, up_weight, down_weight)
+    side = cosines.shape[0]
+    cut = own.reshape(3, side, -1, side)
+    own = jnp.concatenate([cut[:2].transpose(0, 2, 3, 1), cut[2:].transpose(0, 2, 1, 3)], axis=0)
+    own = own.reshape(-1, side, side)
     in_col_t = band_columns(band_index, cosines.shape[0], own)
     in_row, in_col = band_tables(band_index, cosines.shape[0], own)
     moments = call(

time: 36.5 us -> 36.6 us (level)
  no operation moved by 1% of the time
where the time goes in v6:
time: 36.6 us; the launch traced here: 36.5 us
  starting transfers between devices  17 us (46%)
  waiting for transfers between devices  9.38 us (26%)
  Pallas kernels  9.2 us (25%)
  between operations  0.82 us (2%)
    ppermute x20, starting transfers between devices, send(): return lax.ppermute(value, 'fsdp', perm)  15.4 us
    pallas_call x8, Pallas kernels, call(): pl.pallas_call(kernel, out_shape=out_shape, in_specs=specs, scratch_shape...  9.2 us
    ppermute x20, waiting for transfers between devices, send(): return lax.ppermute(value, 'fsdp', perm)  9.03 us
    ppermute x1, starting transfers between devices, per_device(): lax.ppermute(band, 'rep', [(r, (r + s) % reps) for r in range(reps)])  1.58 us
  transfers between devices with their start and end apart: 21, of which 14 were waited for; matrix products, arithmetic and copies ran while one was open for 0% of the time, Pallas kernels for 15%

profile of v6, /device:TPU:0, one launch (start us, length us, event | category | flops | bytes accessed | tf_op | source)
XLA Modules:
  0.0 36.5 jit_solution(2768740986208187535)
XLA Ops:
  0.6 3.0 %collective-permute-start.5 = (bf16[128,512]{1,0:T(8,128)(2,1)}, bf16[128,512]{1,0:T(8,128)(2,1)S(1)}, u32[]{:S(2)}, u32[]{:S(2)}) collective-permute-start(bf16[128,512]{1,0:T(8,128)(2,1)} %bitcast.16), channel_id=1, source_target_pairs={{4,0},{5,1},{8,4},{9,5},{12,8},{13,9},{14,12},{15,13},{10,14},{11,... | collective-permute-start | bytes 393224 | tf_op jit(solution)/shard_map/ppermute | solution.py:273
  3.6 0.0 collective-permute-start.6
  3.6 0.0 copy-start.6
  3.6 0.0 copy-start.7
  3.7 0.2 collective-permute-start
  3.9 1.8 %collective-permute-start.13 = (bf16[128,512]{1,0:T(8,128)(2,1)}, bf16[128,512]{1,0:T(8,128)(2,1)S(1)}, u32[]{:S(2)}, u32[]{:S(2)}) collective-permute-start(bf16[128,512]{1,0:T(8,128)(2,1)} %bitcast.14), channel_id=1, source_target_pairs={{4,0},{5,1},{8,4},{9,5},{12,8},{13,9},{14,12},{15,13},{10,14},{11,... | collective-permute-start | bytes 393224 | tf_op jit(solution)/shard_map/ppermute | solution.py:273
  5.7 0.2 collective-permute-start.15
  5.9 1.7 %collective-permute-done.5.refs_7_ = bf16[128,512]{1,0:T(8,128)(2,1)S(1)} collective-permute-done((bf16[128,512]{1,0:T(8,128)(2,1)}, bf16[128,512]{1,0:T(8,128)(2,1)S(1)}, u32[]{:S(2)}, u32[]{:S(2)}) %collective-permute-start.5) | collective-permute-done | bytes 131104 | tf_op jit(solution)/shard_map/ppermute | solution.py:273
  7.6 0.0 copy-done.8
  7.6 0.0 collective-permute-start.8
  7.6 0.0 collective-permute-done.6.refs_13_
  7.6 1.8 %collective-permute-start.7 = (bf16[128,512]{1,0:T(8,128)(2,1)S(1)}, bf16[128,512]{1,0:T(8,128)(2,1)S(1)}, u32[]{:S(2)}, u32[]{:S(2)}) collective-permute-start(bf16[128,512]{1,0:T(8,128)(2,1)S(1)} %collective-permute-done.5.refs_7_), channel_id=1, source_target_pairs={{4,0},{5,1},{8,4},{9,5},{12,8},{13,9},{14,12},{15,13},{10,14},{11,... | collective-permute-start | bytes 393224 | tf_op jit(solution)/shard_map/ppermute | solution.py:273
  9.4 0.8 %collective-permute-done.refs_1_ = bf16[128,512]{1,0:T(8,128)(2,1)S(1)} collective-permute-done((bf16[128,512]{1,0:T(8,128)(2,1)}, bf16[128,512]{1,0:T(8,128)(2,1)S(1)}, u32[]{:S(2)}, u32[]{:S(2)}) %collective-permute-start) | collective-permute-done | bytes 131104 | tf_op jit(solution)/shard_map/ppermute | solution.py:273
  10.2 0.2 collective-permute-start.1
  10.4 0.0 collective-permute-done.13.refs_2_
  10.4 1.8 %collective-permute-start.14 = (bf16[128,512]{1,0:T(8,128)(2,1)S(1)}, bf16[128,512]{1,0:T(8,128)(2,1)S(1)}, u32[]{:S(2)}, u32[]{:S(2)}) collective-permute-start(bf16[128,512]{1,0:T(8,128)(2,1)S(1)} %collective-permute-done.13.refs_2_), channel_id=1, source_target_pairs={{4,0},{5,1},{8,4},{9,5},{12,8},{13,9},{14,12},{15,13},{10,14},{11,... | collective-permute-start | bytes 393224 | tf_op jit(solution)/shard_map/ppermute | solution.py:273
  12.2 0.8 %collective-permute-done.15.refs_6_ = bf16[128,512]{1,0:T(8,128)(2,1)S(1)} collective-permute-done((bf16[128,512]{1,0:T(8,128)(2,1)}, bf16[128,512]{1,0:T(8,128)(2,1)S(1)}, u32[]{:S(2)}, u32[]{:S(2)}) %collective-permute-start.15) | collective-permute-done | bytes 131104 | tf_op jit(solution)/shard_map/ppermute | solution.py:273
  13.0 0.2 collective-permute-start.16
  13.2 0.0 collective-permute-done.8.refs_14_
  13.2 0.0 copy-done.9
  13.2 0.0 collective-permute-start.10
  13.2 0.8 %collective-permute-done.7.refs_9_ = bf16[128,512]{1,0:T(8,128)(2,1)S(1)} collective-permute-done((bf16[128,512]{1,0:T(8,128)(2,1)S(1)}, bf16[128,512]{1,0:T(8,128)(2,1)S(1)}, u32[]{:S(2)}, u32[]{:S(2)}) %collective-permute-start.7) | collective-permute-done | bytes 131104 | tf_op jit(solution)/shard_map/ppermute | solution.py:273
  14.0 1.7 %collective-permute-start.9 = (bf16[128,512]{1,0:T(8,128)(2,1)S(1)}, bf16[128,512]{1,0:T(8,128)(2,1)S(1)}, u32[]{:S(2)}, u32[]{:S(2)}) collective-permute-start(bf16[128,512]{1,0:T(8,128)(2,1)S(1)} %collective-permute-done.7.refs_9_), channel_id=1, source_target_pairs={{4,0},{5,1},{8,4},{9,5},{12,8},{13,9},{14,12},{15,13},{10,14},{11,... | collective-permute-start | bytes 393224 | tf_op jit(solution)/shard_map/ppermute | solution.py:273
  15.7 0.2 collective-permute-done.1.refs_3_
  15.9 0.2 collective-permute-start.2
  16.1 0.3 collective-permute-done.14.refs_4_
  16.4 1.7 %collective-permute-start.17 = (bf16[128,512]{1,0:T(8,128)(2,1)S(1)}, bf16[128,512]{1,0:T(8,128)(2,1)S(1)}, u32[]{:S(2)}, u32[]{:S(2)}) collective-permute-start(bf16[128,512]{1,0:T(8,128)(2,1)S(1)} %collective-permute-done.14.refs_4_), channel_id=1, source_target_pairs={{4,0},{5,1},{8,4},{9,5},{12,8},{13,9},{14,12},{15,13},{10,14},{11,... | collective-permute-start | bytes 393224 | tf_op jit(solution)/shard_map/ppermute | solution.py:273
  18.1 0.5 %collective-permute-done.16.refs_8_ = bf16[128,512]{1,0:T(8,128)(2,1)S(1)} collective-permute-done((bf16[128,512]{1,0:T(8,128)(2,1)S(1)}, bf16[128,512]{1,0:T(8,128)(2,1)S(1)}, u32[]{:S(2)}, u32[]{:S(2)}) %collective-permute-start.16) | collective-permute-done | bytes 131104 | tf_op jit(solution)/shard_map/ppermute | solution.py:273
  18.6 0.1 collective-permute-start.18
  18.7 0.0 collective-permute-done.10.refs_15_
  18.7 1.2 %collective-permute-done.9.refs_3_ = bf16[128,512]{1,0:T(8,128)(2,1)S(1)} collective-permute-done((bf16[128,512]{1,0:T(8,128)(2,1)S(1)}, bf16[128,512]{1,0:T(8,128)(2,1)S(1)}, u32[]{:S(2)}, u32[]{:S(2)}) %collective-permute-start.9) | collective-permute-done | bytes 131104 | tf_op jit(solution)/shard_map/ppermute | solution.py:273
  19.9 1.9 %collective-permute-start.11 = (bf16[128,512]{1,0:T(8,128)(2,1)S(1)}, bf16[128,512]{1,0:T(8,128)(2,1)S(1)}, u32[]{:S(2)}, u32[]{:S(2)}) collective-permute-start(bf16[128,512]{1,0:T(8,128)(2,1)S(1)} %collective-permute-done.9.refs_3_), channel_id=1, source_target_pairs={{4,0},{5,1},{8,4},{9,5},{12,8},{13,9},{14,12},{15,13},{10,14},{11,... | collective-permute-start | bytes 393224 | tf_op jit(solution)/shard_map/ppermute | solution.py:273
  21.8 0.4 %collective-permute-done.2.refs_0_ = bf16[128,512]{1,0:T(8,128)(2,1)S(1)} collective-permute-done((bf16[128,512]{1,0:T(8,128)(2,1)S(1)}, bf16[128,512]{1,0:T(8,128)(2,1)S(1)}, u32[]{:S(2)}, u32[]{:S(2)}) %collective-permute-start.2) | collective-permute-done | bytes 131104 | tf_op jit(solution)/shard_map/ppermute | solution.py:273
  22.2 0.0 collective-permute-start.3
  22.2 0.0 copy-done.5
  22.2 0.0 copy-done.6
  22.3 0.0 copy-done.7
  22.3 1.6 %shard_map.155 = (f32[3,128,512]{2,1,0:T(8,128)S(1)}, f32[3,128,512]{2,1,0:T(8,128)S(1)}, bf16[512,512]{1,0:T(8,128)(2,1)S(1)}, bf16[256,512]{1,0:T(8,128)(2,1)S(1)}) custom-call(bf16[128,512]{1,0:T(8,128)(2,1)S(1)} %bitcast.15, bf16[128,512]{1,0:T(8,128)(2,1)S(1)} %collective-permute-done.refs_1_, bf16[128,512]{1,0:T(8,128)(2,1)S(1)} %collective-permute-done.13.refs_2_, ...), custom_call_target="tpu_custom_call" | custom-call | flops 1006632960 | bytes 4202496 | tf_op jit(solution)/shard_map/pallas_call | solution.py:229
  23.8 0.0 copy-start.10
  23.8 0.0 collective-permute-done.17.refs_1_
  23.8 1.2 %collective-permute-done.18.refs_2_ = bf16[128,512]{1,0:T(8,128)(2,1)S(1)} collective-permute-done((bf16[128,512]{1,0:T(8,128)(2,1)S(1)}, bf16[128,512]{1,0:T(8,128)(2,1)S(1)}, u32[]{:S(2)}, u32[]{:S(2)}) %collective-permute-start.18) | collective-permute-done | bytes 131104 | tf_op jit(solution)/shard_map/ppermute | solution.py:273
  25.0 0.9 %shard_map.156 = (f32[12,128,128]{2,1,0:T(8,128)S(1)}, f32[12,128,128]{2,1,0:T(8,128)S(1)}) custom-call(bf16[128,512]{1,0:T(8,128)(2,1)S(1)} %collective-permute-done.2.refs_0_, bf16[128,512]{1,0:T(8,128)(2,1)S(1)} %collective-permute-done.17.refs_1_, bf16[128,512]{1,0:T(8,128)(2,1)S(1)} %collective-permute-done.18.refs_2_, ...), custom_call_target="tpu_custom_call" | custom-call | flops 402653184 | bytes 5767168 | tf_op jit(solution)/shard_map/pallas_call | solution.py:229
  26.0 0.1 collective-permute-start.19
  26.0 0.0 copy-done.10
  26.1 0.5 %shard_map.159.in_col_t_ref = bf16[12,512,128]{2,1,0:T(8,128)(2,1)S(1)} custom-call(s32[3,4,512]{2,1,0:T(4,128)S(1)} %copy-done.10, f32[12,128,128]{2,1,0:T(8,128)S(1)} %get-tuple-element.46.refs_0_), custom_call_target="tpu_custom_call" | custom-call | flops 1000000000 | bytes 1622016 | tf_op jit(solution)/shard_map/pallas_call | solution.py:229
  26.5 0.0 copy-start
  26.5 0.0 copy-start.1
  26.5 0.0 copy-start.2
  26.6 0.0 copy-start.3
  26.6 0.0 copy-start.4
  26.6 0.6 %collective-permute-done.3.refs_0_ = bf16[128,512]{1,0:T(8,128)(2,1)S(1)} collective-permute-done((bf16[128,512]{1,0:T(8,128)(2,1)S(1)}, bf16[128,512]{1,0:T(8,128)(2,1)S(1)}, u32[]{:S(2)}, u32[]{:S(2)}) %collective-permute-start.3) | collective-permute-done | bytes 131104 | tf_op jit(solution)/shard_map/ppermute | solution.py:273
  27.2 0.0 collective-permute-start.4
  27.2 0.0 collective-permute-done.11.refs_1_.refs_2_
  27.2 0.5 %collective-permute-start.12 = (bf16[128,512]{1,0:T(8,128)(2,1)S(1)}, bf16[128,512]{1,0:T(8,128)(2,1)S(1)}, u32[]{:S(2)}, u32[]{:S(2)}) collective-permute-start(bf16[128,512]{1,0:T(8,128)(2,1)S(1)} %collective-permute-done.11.refs_1_.refs_2_), channel_id=1, source_target_pairs={{0,1},{1,0},{2,3},{3,2},{4,5},{5,4},{6,7},{7,6},{8,9},{9,8},{10,11... | collective-permute-start | bytes 393224 | tf_op jit(solution)/shard_map/ppermute | solution.py:273
  27.7 0.5 %shard_map.157 = (bf16[12,128,512]{2,1,0:T(8,128)(2,1)S(1)}, bf16[12,128,512]{2,1,0:T(8,128)(2,1)S(1)}) custom-call(s32[3,4,512]{2,1,0:T(4,128)S(1)} %copy-done.10, bf16[128,512]{1,0:T(8,128)(2,1)S(1)} %collective-permute-done.3.refs_0_, bf16[128,512]{1,0:T(8,128)(2,1)S(1)} %collective-permute-done.11.refs_1_.refs_2_), custom_call_target="tpu_custom_call" | custom-call | flops 10000000000 | bytes 573440 | tf_op jit(solution)/shard_map/pallas_call | solution.py:229
  28.2 0.3 collective-permute-done.4.refs_1_
  28.5 0.2 collective-permute-done.12.refs_3_
  28.7 0.0 collective-permute-done.19.refs_7_
  28.7 0.0 copy-done
  28.8 1.8 %shard_map.158 = (f32[12,128,128]{2,1,0:T(8,128)S(1)}, f32[12,128,128]{2,1,0:T(8,128)S(1)}, f32[3,4,512]{2,1,0:T(4,128)S(1)}) custom-call(bf16[128,512]{1,0:T(8,128)(2,1)S(1)} %collective-permute-done.3.refs_0_, bf16[128,512]{1,0:T(8,128)(2,1)S(1)} %collective-permute-done.4.refs_1_, bf16[128,512]{1,0:T(8,128)(2,1)S(1)} %collective-permute-done.11.refs_1_.refs_2_, ...), custom_call_target="tpu_custom_call" | custom-call | flops 1000000000 | bytes 13893632 | tf_op jit(solution)/shard_map/pallas_call | solution.py:229
  30.6 1.6 %collective-permute-start.20 = (f32[3,4,512]{2,1,0:T(4,128)S(1)}, f32[3,4,512]{2,1,0:T(4,128)S(1)}, u32[]{:S(2)}, u32[]{:S(2)}) collective-permute-start(f32[3,4,512]{2,1,0:T(4,128)S(1)} %get-tuple-element.55), channel_id=1, source_target_pairs={{0,16},{16,0},{1,17},{17,1},{2,18},{18,2},{3,19},{19,3},{4,20},{20... | collective-permute-start | bytes 73736 | tf_op jit(solution)/shard_map/ppermute | solution.py:443
  32.2 2.0 %shard_map.160 = (f32[4,128,128]{2,1,0:T(8,128)}, f32[4,128,128]{2,1,0:T(8,128)}, f32[4,128,128]{2,1,0:T(8,128)}, f32[12,128,128]{2,1,0:T(8,128)S(1)}, bf16[12,512,256]{2,1,0:T(8,128)(2,1)S(1)}) custom-call(f32[12,128,128]{2,1,0:T(8,128)S(1)} %get-tuple-element.49.moment_ref, f32[12,128,128]{2,1,0:T(8,128)S(1)} %get-tuple-element.50.coeffs_ref, ...), custom_call_target="tpu_custom_call" | custom-call | flops 301989888 | bytes 9699328 | tf_op jit(solution)/shard_map/pallas_call | solution.py:229
  34.2 0.3 collective-permute-done.20
  34.5 1.9 %shard_map.161 = (f32[4,128,128]{2,1,0:T(8,128)}, f32[4,128,128]{2,1,0:T(8,128)}, f32[4,128,128]{2,1,0:T(8,128)}) custom-call(f32[12,128,128]{2,1,0:T(8,128)S(1)} %get-tuple-element.54.decoded_ref, f32[1,3,4,512]{3,2,1,0:T(4,128)S(1)} %bitcast.12, bf16[12,128,512]{2,1,0:T(8,128)(2,1)S(1)} %get-tuple-element.47.refs_11_.in_row_ref, ...), custom_call_target="tpu_custom_call" | custom-call | flops 301989888 | bytes 11190272 | tf_op jit(solution)/shard_map/pallas_call | solution.py:229
  (8 shorter events, 0.0 us)
Async XLA Ops:
  0.6 7.0 %collective-permute-start.5 = (bf16[128,512]{1,0:T(8,128)(2,1)}, bf16[128,512]{1,0:T(8,128)(2,1)S(1)}, u32[]{:S(2)}, u32[]{:S(2)}) collective-permute-start(bf16[128,512]{1,0:T(8,128)(2,1)} %bitcast.16), channel_id=1, source_target_pairs={{4,0},{5,1},{8,4},{9,5},{12,8},{13,9},{14,12},{15,13},{10,14},{11,... | collective-permute-start | bytes 393224 | tf_op jit(solution)/shard_map/ppermute | solution.py:273
  3.6 4.0 %collective-permute-start.6 = (bf16[4,128,128]{2,1,0:T(8,128)(2,1)}, bf16[4,128,128]{2,1,0:T(8,128)(2,1)S(1)}, u32[]{:S(2)}, u32[]{:S(2)}) collective-permute-start(bf16[4,128,128]{2,1,0:T(8,128)(2,1)} %refs_10_.1), channel_id=1, source_target_pairs={{0,1},{1,0},{2,3},{3,2},{4,5},{5,4},{6,7},{7,6},{8,9},{9,8},{10,11... | collective-permute-start | bytes 393224 | tf_op jit(solution)/shard_map/ppermute | solution.py:273
  3.6 4.0 %copy-start.8 = (bf16[4,128,128]{2,1,0:T(8,128)(2,1)S(1)}, bf16[4,128,128]{2,1,0:T(8,128)(2,1)}, u32[]{:S(2)}) copy-start(bf16[4,128,128]{2,1,0:T(8,128)(2,1)} %refs_11_.1) | copy-start | bytes 393220
  3.6 9.6 %copy-start.9 = (bf16[4,128,128]{2,1,0:T(8,128)(2,1)S(1)}, bf16[4,128,128]{2,1,0:T(8,128)(2,1)}, u32[]{:S(2)}) copy-start(bf16[4,128,128]{2,1,0:T(8,128)(2,1)} %refs_12_.1) | copy-start | bytes 393220
  3.6 18.6 %copy-start.5 = (bf16[1,128,512]{2,1,0:T(8,128)(2,1)S(1)}, bf16[1,128,512]{2,1,0:T(8,128)(2,1)}, u32[]{:S(2)}) copy-start(bf16[1,128,512]{2,1,0:T(8,128)(2,1)} %param.11) | copy-start | bytes 393220
  3.6 18.6 %copy-start.6 = (bf16[1,128,512]{2,1,0:T(8,128)(2,1)S(1)}, bf16[1,128,512]{2,1,0:T(8,128)(2,1)}, u32[]{:S(2)}) copy-start(bf16[1,128,512]{2,1,0:T(8,128)(2,1)} %param.12) | copy-start | bytes 393220
  3.6 18.6 %copy-start.7 = (bf16[4,128,128]{2,1,0:T(8,128)(2,1)S(1)}, bf16[4,128,128]{2,1,0:T(8,128)(2,1)}, u32[]{:S(2)}) copy-start(bf16[4,128,128]{2,1,0:T(8,128)(2,1)} %refs_10_.1) | copy-start | bytes 393220
  3.7 6.6 %collective-permute-start = (bf16[128,512]{1,0:T(8,128)(2,1)}, bf16[128,512]{1,0:T(8,128)(2,1)S(1)}, u32[]{:S(2)}, u32[]{:S(2)}) collective-permute-start(bf16[128,512]{1,0:T(8,128)(2,1)} %bitcast.13), channel_id=1, source_target_pairs={{0,4},{1,5},{4,8},{5,9},{8,12},{9,13},{12,14},{13,15},{14,10},{15,... | collective-permute-start | bytes 393224 | tf_op jit(solution)/shard_map/ppermute | solution.py:273
  3.9 6.5 %collective-permute-start.13 = (bf16[128,512]{1,0:T(8,128)(2,1)}, bf16[128,512]{1,0:T(8,128)(2,1)S(1)}, u32[]{:S(2)}, u32[]{:S(2)}) collective-permute-start(bf16[128,512]{1,0:T(8,128)(2,1)} %bitcast.14), channel_id=1, source_target_pairs={{4,0},{5,1},{8,4},{9,5},{12,8},{13,9},{14,12},{15,13},{10,14},{11,... | collective-permute-start | bytes 393224 | tf_op jit(solution)/shard_map/ppermute | solution.py:273
  5.7 7.3 %collective-permute-start.15 = (bf16[128,512]{1,0:T(8,128)(2,1)}, bf16[128,512]{1,0:T(8,128)(2,1)S(1)}, u32[]{:S(2)}, u32[]{:S(2)}) collective-permute-start(bf16[128,512]{1,0:T(8,128)(2,1)} %bitcast.17), channel_id=1, source_target_pairs={{0,4},{1,5},{4,8},{5,9},{8,12},{9,13},{12,14},{13,15},{14,10},{15,... | collective-permute-start | bytes 393224 | tf_op jit(solution)/shard_map/ppermute | solution.py:273
  7.6 5.6 %collective-permute-start.8 = (bf16[4,128,128]{2,1,0:T(8,128)(2,1)S(1)}, bf16[4,128,128]{2,1,0:T(8,128)(2,1)S(1)}, u32[]{:S(2)}, u32[]{:S(2)}) collective-permute-start(bf16[4,128,128]{2,1,0:T(8,128)(2,1)S(1)} %copy-done.8), channel_id=1, source_target_pairs={{0,1},{1,0},{2,3},{3,2},{4,5},{5,4},{6,7},{7,6},{8,9},{9,8},{10,11... | collective-permute-start | bytes 393224 | tf_op jit(solution)/shard_map/ppermute | solution.py:273
  7.6 6.3 %collective-permute-start.7 = (bf16[128,512]{1,0:T(8,128)(2,1)S(1)}, bf16[128,512]{1,0:T(8,128)(2,1)S(1)}, u32[]{:S(2)}, u32[]{:S(2)}) collective-permute-start(bf16[128,512]{1,0:T(8,128)(2,1)S(1)} %collective-permute-done.5.refs_7_), channel_id=1, source_target_pairs={{4,0},{5,1},{8,4},{9,5},{12,8},{13,9},{14,12},{15,13},{10,14},{11,... | collective-permute-start | bytes 393224 | tf_op jit(solution)/shard_map/ppermute | solution.py:273
  10.2 5.7 %collective-permute-start.1 = (bf16[128,512]{1,0:T(8,128)(2,1)S(1)}, bf16[128,512]{1,0:T(8,128)(2,1)S(1)}, u32[]{:S(2)}, u32[]{:S(2)}) collective-permute-start(bf16[128,512]{1,0:T(8,128)(2,1)S(1)} %collective-permute-done.refs_1_), channel_id=1, source_target_pairs={{0,4},{1,5},{4,8},{5,9},{8,12},{9,13},{12,14},{13,15},{14,10},{15,... | collective-permute-start | bytes 393224 | tf_op jit(solution)/shard_map/ppermute | solution.py:273
  10.4 6.0 %collective-permute-start.14 = (bf16[128,512]{1,0:T(8,128)(2,1)S(1)}, bf16[128,512]{1,0:T(8,128)(2,1)S(1)}, u32[]{:S(2)}, u32[]{:S(2)}) collective-permute-start(bf16[128,512]{1,0:T(8,128)(2,1)S(1)} %collective-permute-done.13.refs_2_), channel_id=1, source_target_pairs={{4,0},{5,1},{8,4},{9,5},{12,8},{13,9},{14,12},{15,13},{10,14},{11,... | collective-permute-start | bytes 393224 | tf_op jit(solution)/shard_map/ppermute | solution.py:273
  13.0 5.6 %collective-permute-start.16 = (bf16[128,512]{1,0:T(8,128)(2,1)S(1)}, bf16[128,512]{1,0:T(8,128)(2,1)S(1)}, u32[]{:S(2)}, u32[]{:S(2)}) collective-permute-start(bf16[128,512]{1,0:T(8,128)(2,1)S(1)} %collective-permute-done.15.refs_6_), channel_id=1, source_target_pairs={{0,4},{1,5},{4,8},{5,9},{8,12},{9,13},{12,14},{13,15},{14,10},{15,... | collective-permute-start | bytes 393224 | tf_op jit(solution)/shard_map/ppermute | solution.py:273
  13.2 5.5 %collective-permute-start.10 = (bf16[4,128,128]{2,1,0:T(8,128)(2,1)S(1)}, bf16[4,128,128]{2,1,0:T(8,128)(2,1)S(1)}, u32[]{:S(2)}, u32[]{:S(2)}) collective-permute-start(bf16[4,128,128]{2,1,0:T(8,128)(2,1)S(1)} %copy-done.9), channel_id=1, source_target_pairs={{0,1},{1,0},{2,3},{3,2},{4,5},{5,4},{6,7},{7,6},{8,9},{9,8},{10,11... | collective-permute-start | bytes 393224 | tf_op jit(solution)/shard_map/ppermute | solution.py:273
  14.0 5.9 %collective-permute-start.9 = (bf16[128,512]{1,0:T(8,128)(2,1)S(1)}, bf16[128,512]{1,0:T(8,128)(2,1)S(1)}, u32[]{:S(2)}, u32[]{:S(2)}) collective-permute-start(bf16[128,512]{1,0:T(8,128)(2,1)S(1)} %collective-permute-done.7.refs_9_), channel_id=1, source_target_pairs={{4,0},{5,1},{8,4},{9,5},{12,8},{13,9},{14,12},{15,13},{10,14},{11,... | collective-permute-start | bytes 393224 | tf_op jit(solution)/shard_map/ppermute | solution.py:273
  15.9 6.3 %collective-permute-start.2 = (bf16[128,512]{1,0:T(8,128)(2,1)S(1)}, bf16[128,512]{1,0:T(8,128)(2,1)S(1)}, u32[]{:S(2)}, u32[]{:S(2)}) collective-permute-start(bf16[128,512]{1,0:T(8,128)(2,1)S(1)} %collective-permute-done.1.refs_3_), channel_id=1, source_target_pairs={{0,4},{1,5},{4,8},{5,9},{8,12},{9,13},{12,14},{13,15},{14,10},{15,... | collective-permute-start | bytes 393224 | tf_op jit(solution)/shard_map/ppermute | solution.py:273
  16.4 7.4 %collective-permute-start.17 = (bf16[128,512]{1,0:T(8,128)(2,1)S(1)}, bf16[128,512]{1,0:T(8,128)(2,1)S(1)}, u32[]{:S(2)}, u32[]{:S(2)}) collective-permute-start(bf16[128,512]{1,0:T(8,128)(2,1)S(1)} %collective-permute-done.14.refs_4_), channel_id=1, source_target_pairs={{4,0},{5,1},{8,4},{9,5},{12,8},{13,9},{14,12},{15,13},{10,14},{11,... | collective-permute-start | bytes 393224 | tf_op jit(solution)/shard_map/ppermute | solution.py:273
  18.6 6.5 %collective-permute-start.18 = (bf16[128,512]{1,0:T(8,128)(2,1)S(1)}, bf16[128,512]{1,0:T(8,128)(2,1)S(1)}, u32[]{:S(2)}, u32[]{:S(2)}) collective-permute-start(bf16[128,512]{1,0:T(8,128)(2,1)S(1)} %collective-permute-done.16.refs_8_), channel_id=1, source_target_pairs={{0,4},{1,5},{4,8},{5,9},{8,12},{9,13},{12,14},{13,15},{14,10},{15,... | collective-permute-start | bytes 393224 | tf_op jit(solution)/shard_map/ppermute | solution.py:273
  19.9 7.3 %collective-permute-start.11 = (bf16[128,512]{1,0:T(8,128)(2,1)S(1)}, bf16[128,512]{1,0:T(8,128)(2,1)S(1)}, u32[]{:S(2)}, u32[]{:S(2)}) collective-permute-start(bf16[128,512]{1,0:T(8,128)(2,1)S(1)} %collective-permute-done.9.refs_3_), channel_id=1, source_target_pairs={{4,0},{5,1},{8,4},{9,5},{12,8},{13,9},{14,12},{15,13},{10,14},{11,... | collective-permute-start | bytes 393224 | tf_op jit(solution)/shard_map/ppermute | solution.py:273
  22.2 5.0 %collective-permute-start.3 = (bf16[128,512]{1,0:T(8,128)(2,1)S(1)}, bf16[128,512]{1,0:T(8,128)(2,1)S(1)}, u32[]{:S(2)}, u32[]{:S(2)}) collective-permute-start(bf16[128,512]{1,0:T(8,128)(2,1)S(1)} %collective-permute-done.2.refs_0_), channel_id=1, source_target_pairs={{0,4},{1,5},{4,8},{5,9},{8,12},{9,13},{12,14},{13,15},{14,10},{15,... | collective-permute-start | bytes 393224 | tf_op jit(solution)/shard_map/ppermute | solution.py:273
  23.8 2.2 %copy-start.10 = (s32[3,4,512]{2,1,0:T(4,128)S(1)}, s32[3,4,512]{2,1,0:T(4,128)}, u32[]{:S(2)}) copy-start(s32[3,4,512]{2,1,0:T(4,128)} %index_ref.3) | copy-start | bytes 73732
  26.0 2.8 %collective-permute-start.19 = (f32[12,128,128]{2,1,0:T(8,128)S(1)}, f32[12,128,128]{2,1,0:T(8,128)S(1)}, u32[]{:S(2)}, u32[]{:S(2)}) collective-permute-start(f32[12,128,128]{2,1,0:T(8,128)S(1)} %get-tuple-element.46.refs_0_), channel_id=1, source_target_pairs={{0,1},{1,0},{2,3},{3,2},{4,5},{5,4},{6,7},{7,6},{8,9},{9,8},{10,11... | collective-permute-start | bytes 2359304 | tf_op jit(solution)/shard_map/ppermute | solution.py:273
  26.5 2.2 %copy-start = (f32[128,128]{1,0:T(8,128)S(1)}, f32[128,128]{1,0:T(8,128)}, u32[]{:S(2)}) copy-start(f32[128,128]{1,0:T(8,128)} %constant.5.clone.refs_14_.cosines_t_ref) | copy-start | bytes 196612
  26.5 2.2 %copy-start.1 = (f32[128,128]{1,0:T(8,128)S(1)}, f32[128,128]{1,0:T(8,128)}, u32[]{:S(2)}) copy-start(f32[128,128]{1,0:T(8,128)} %constant.4.clone.refs_13_.cosines_ref) | copy-start | bytes 196612
  26.5 2.2 %copy-start.2 = (f32[1,4,128,128]{3,2,1,0:T(8,128)S(1)}, f32[1,4,128,128]{3,2,1,0:T(8,128)}, u32[]{:S(2)}) copy-start(f32[1,4,128,128]{3,2,1,0:T(8,128)} %param.16) | copy-start | bytes 786436
  26.6 2.2 %copy-start.3 = (f32[1,4,128,128]{3,2,1,0:T(8,128)S(1)}, f32[1,4,128,128]{3,2,1,0:T(8,128)}, u32[]{:S(2)}) copy-start(f32[1,4,128,128]{3,2,1,0:T(8,128)} %param.17) | copy-start | bytes 786436
  26.6 2.2 %copy-start.4 = (f32[1,4,128,128]{3,2,1,0:T(8,128)S(1)}, f32[1,4,128,128]{3,2,1,0:T(8,128)}, u32[]{:S(2)}) copy-start(f32[1,4,128,128]{3,2,1,0:T(8,128)} %param.18) | copy-start | bytes 786436
  27.2 1.3 %collective-permute-start.4 = (bf16[128,512]{1,0:T(8,128)(2,1)S(1)}, bf16[128,512]{1,0:T(8,128)(2,1)S(1)}, u32[]{:S(2)}, u32[]{:S(2)}) collective-permute-start(bf16[128,512]{1,0:T(8,128)(2,1)S(1)} %collective-permute-done.3.refs_0_), channel_id=1, source_target_pairs={{0,1},{1,0},{2,3},{3,2},{4,5},{5,4},{6,7},{7,6},{8,9},{9,8},{10,11... | collective-permute-start | bytes 393224 | tf_op jit(solution)/shard_map/ppermute | solution.py:273
  27.2 1.5 %collective-permute-start.12 = (bf16[128,512]{1,0:T(8,128)(2,1)S(1)}, bf16[128,512]{1,0:T(8,128)(2,1)S(1)}, u32[]{:S(2)}, u32[]{:S(2)}) collective-permute-start(bf16[128,512]{1,0:T(8,128)(2,1)S(1)} %collective-permute-done.11.refs_1_.refs_2_), channel_id=1, source_target_pairs={{0,1},{1,0},{2,3},{3,2},{4,5},{5,4},{6,7},{7,6},{8,9},{9,8},{10,11... | collective-permute-start | bytes 393224 | tf_op jit(solution)/shard_map/ppermute | solution.py:273
  30.6 3.9 %collective-permute-start.20 = (f32[3,4,512]{2,1,0:T(4,128)S(1)}, f32[3,4,512]{2,1,0:T(4,128)S(1)}, u32[]{:S(2)}, u32[]{:S(2)}) collective-permute-start(f32[3,4,512]{2,1,0:T(4,128)S(1)} %get-tuple-element.55), channel_id=1, source_target_pairs={{0,16},{16,0},{1,17},{17,1},{2,18},{18,2},{3,19},{19,3},{4,20},{20... | collective-permute-start | bytes 73736 | tf_op jit(solution)/shard_map/ppermute | solution.py:443

commit v7 on v5

--- a/solution.py
+++ b/solution.py
@@ -202,8 +202,10 @@
         m, i = b // count, b % count
         hi, lo = split2(sum(other_ref[g, m, i : i + 1, :] for g in range(other_ref.shape[0])))
         in_row = in_row_ref[b]
-        both = dot(jnp.concatenate([in_row * hi, in_row * lo], axis=0), cells_ref[b])
-        inner.append(both[:side, :side] + (both[:side, side:] + both[side:, :side]))
+        upper = in_row * hi
+        c_hi, c_lo = cells_ref[b, :, :side], cells_ref[b, :, side:]
+        left = jnp.concatenate([upper, in_row * lo, upper], axis=1)
+        inner.append(dot(left, jnp.concatenate([c_hi, c_hi, c_lo], axis=0)))
     update = dot3(cosines_t_ref[...], jnp.concatenate(inner, axis=1))
     for b in range(3 * count):
         outs[b // count][b % count] = decoded_ref[b] + update[:, b * side : (b + 1) * side]

time: 36.5 us -> 36.9 us (1.011)
  Pallas kernels: 9.05 us -> 9.43 us
    pallas_call x8, Pallas kernels: 9.05 us -> 9.43 us  [call(): pl.pallas_call(kernel, out_shape=out_shape, in_specs=specs, scratch_shape...]
where the time goes in v7:
time: 36.9 us; the launch traced here: 36.7 us
  starting transfers between devices  17 us (46%)
  waiting for transfers between devices  9.44 us (26%)
  Pallas kernels  9.43 us (26%)
  between operations  0.82 us (2%)
    ppermute x20, starting transfers between devices, send(): return lax.ppermute(value, 'fsdp', perm)  15.4 us
    pallas_call x8, Pallas kernels, call(): pl.pallas_call(kernel, out_shape=out_shape, in_specs=specs, scratch_shape...  9.43 us
    ppermute x20, waiting for transfers between devices, send(): return lax.ppermute(value, 'fsdp', perm)  9.1 us
    ppermute x1, starting transfers between devices, per_device(): lax.ppermute(band, 'rep', [(r, (r + s) % reps) for r in range(reps)])  1.58 us
  transfers between devices with their start and end apart: 21, of which 14 were waited for; matrix products, arithmetic and copies ran while one was open for 0% of the time, Pallas kernels for 15%

profile of v7, /device:TPU:0, one launch (start us, length us, event | category | flops | bytes accessed | tf_op | source)
XLA Modules:
  0.0 36.7 jit_solution(12566654802319541940)
XLA Ops:
  0.6 3.0 %collective-permute-start.5 = (bf16[128,512]{1,0:T(8,128)(2,1)}, bf16[128,512]{1,0:T(8,128)(2,1)S(1)}, u32[]{:S(2)}, u32[]{:S(2)}) collective-permute-start(bf16[128,512]{1,0:T(8,128)(2,1)} %bitcast.16), channel_id=1, source_target_pairs={{4,0},{5,1},{8,4},{9,5},{12,8},{13,9},{14,12},{15,13},{10,14},{11,... | collective-permute-start | bytes 393224 | tf_op jit(solution)/shard_map/ppermute | solution.py:263
  3.6 0.0 collective-permute-start.6
  3.6 0.0 copy-start.6
  3.6 0.0 copy-start.7
  3.7 0.2 collective-permute-start
  3.9 1.8 %collective-permute-start.13 = (bf16[128,512]{1,0:T(8,128)(2,1)}, bf16[128,512]{1,0:T(8,128)(2,1)S(1)}, u32[]{:S(2)}, u32[]{:S(2)}) collective-permute-start(bf16[128,512]{1,0:T(8,128)(2,1)} %bitcast.14), channel_id=1, source_target_pairs={{4,0},{5,1},{8,4},{9,5},{12,8},{13,9},{14,12},{15,13},{10,14},{11,... | collective-permute-start | bytes 393224 | tf_op jit(solution)/shard_map/ppermute | solution.py:263
  5.7 0.2 collective-permute-start.15
  5.9 1.7 %collective-permute-done.5.refs_7_ = bf16[128,512]{1,0:T(8,128)(2,1)S(1)} collective-permute-done((bf16[128,512]{1,0:T(8,128)(2,1)}, bf16[128,512]{1,0:T(8,128)(2,1)S(1)}, u32[]{:S(2)}, u32[]{:S(2)}) %collective-permute-start.5) | collective-permute-done | bytes 131104 | tf_op jit(solution)/shard_map/ppermute | solution.py:263
  7.6 0.0 copy-done.8
  7.6 0.0 collective-permute-start.8
  7.6 0.0 collective-permute-done.6.refs_13_
  7.6 1.8 %collective-permute-start.7 = (bf16[128,512]{1,0:T(8,128)(2,1)S(1)}, bf16[128,512]{1,0:T(8,128)(2,1)S(1)}, u32[]{:S(2)}, u32[]{:S(2)}) collective-permute-start(bf16[128,512]{1,0:T(8,128)(2,1)S(1)} %collective-permute-done.5.refs_7_), channel_id=1, source_target_pairs={{4,0},{5,1},{8,4},{9,5},{12,8},{13,9},{14,12},{15,13},{10,14},{11,... | collective-permute-start | bytes 393224 | tf_op jit(solution)/shard_map/ppermute | solution.py:263
  9.4 0.8 %collective-permute-done.refs_1_ = bf16[128,512]{1,0:T(8,128)(2,1)S(1)} collective-permute-done((bf16[128,512]{1,0:T(8,128)(2,1)}, bf16[128,512]{1,0:T(8,128)(2,1)S(1)}, u32[]{:S(2)}, u32[]{:S(2)}) %collective-permute-start) | collective-permute-done | bytes 131104 | tf_op jit(solution)/shard_map/ppermute | solution.py:263
  10.2 0.2 collective-permute-start.1
  10.4 0.0 collective-permute-done.13.refs_2_
  10.4 1.8 %collective-permute-start.14 = (bf16[128,512]{1,0:T(8,128)(2,1)S(1)}, bf16[128,512]{1,0:T(8,128)(2,1)S(1)}, u32[]{:S(2)}, u32[]{:S(2)}) collective-permute-start(bf16[128,512]{1,0:T(8,128)(2,1)S(1)} %collective-permute-done.13.refs_2_), channel_id=1, source_target_pairs={{4,0},{5,1},{8,4},{9,5},{12,8},{13,9},{14,12},{15,13},{10,14},{11,... | collective-permute-start | bytes 393224 | tf_op jit(solution)/shard_map/ppermute | solution.py:263
  12.2 0.8 %collective-permute-done.15.refs_6_ = bf16[128,512]{1,0:T(8,128)(2,1)S(1)} collective-permute-done((bf16[128,512]{1,0:T(8,128)(2,1)}, bf16[128,512]{1,0:T(8,128)(2,1)S(1)}, u32[]{:S(2)}, u32[]{:S(2)}) %collective-permute-start.15) | collective-permute-done | bytes 131104 | tf_op jit(solution)/shard_map/ppermute | solution.py:263
  13.0 0.2 collective-permute-start.16
  13.2 0.0 collective-permute-done.8.refs_14_
  13.2 0.0 copy-done.9
  13.2 0.0 collective-permute-start.10
  13.2 0.8 %collective-permute-done.7.refs_9_ = bf16[128,512]{1,0:T(8,128)(2,1)S(1)} collective-permute-done((bf16[128,512]{1,0:T(8,128)(2,1)S(1)}, bf16[128,512]{1,0:T(8,128)(2,1)S(1)}, u32[]{:S(2)}, u32[]{:S(2)}) %collective-permute-start.7) | collective-permute-done | bytes 131104 | tf_op jit(solution)/shard_map/ppermute | solution.py:263
  14.0 1.7 %collective-permute-start.9 = (bf16[128,512]{1,0:T(8,128)(2,1)S(1)}, bf16[128,512]{1,0:T(8,128)(2,1)S(1)}, u32[]{:S(2)}, u32[]{:S(2)}) collective-permute-start(bf16[128,512]{1,0:T(8,128)(2,1)S(1)} %collective-permute-done.7.refs_9_), channel_id=1, source_target_pairs={{4,0},{5,1},{8,4},{9,5},{12,8},{13,9},{14,12},{15,13},{10,14},{11,... | collective-permute-start | bytes 393224 | tf_op jit(solution)/shard_map/ppermute | solution.py:263
  15.7 0.2 collective-permute-done.1.refs_3_
  15.9 0.2 collective-permute-start.2
  16.1 0.3 collective-permute-done.14.refs_4_
  16.4 1.7 %collective-permute-start.17 = (bf16[128,512]{1,0:T(8,128)(2,1)S(1)}, bf16[128,512]{1,0:T(8,128)(2,1)S(1)}, u32[]{:S(2)}, u32[]{:S(2)}) collective-permute-start(bf16[128,512]{1,0:T(8,128)(2,1)S(1)} %collective-permute-done.14.refs_4_), channel_id=1, source_target_pairs={{4,0},{5,1},{8,4},{9,5},{12,8},{13,9},{14,12},{15,13},{10,14},{11,... | collective-permute-start | bytes 393224 | tf_op jit(solution)/shard_map/ppermute | solution.py:263
  18.1 0.5 %collective-permute-done.16.refs_8_ = bf16[128,512]{1,0:T(8,128)(2,1)S(1)} collective-permute-done((bf16[128,512]{1,0:T(8,128)(2,1)S(1)}, bf16[128,512]{1,0:T(8,128)(2,1)S(1)}, u32[]{:S(2)}, u32[]{:S(2)}) %collective-permute-start.16) | collective-permute-done | bytes 131104 | tf_op jit(solution)/shard_map/ppermute | solution.py:263
  18.6 0.1 collective-permute-start.18
  18.7 0.0 collective-permute-done.10.refs_15_
  18.7 1.2 %collective-permute-done.9.refs_3_ = bf16[128,512]{1,0:T(8,128)(2,1)S(1)} collective-permute-done((bf16[128,512]{1,0:T(8,128)(2,1)S(1)}, bf16[128,512]{1,0:T(8,128)(2,1)S(1)}, u32[]{:S(2)}, u32[]{:S(2)}) %collective-permute-start.9) | collective-permute-done | bytes 131104 | tf_op jit(solution)/shard_map/ppermute | solution.py:263
  19.9 1.9 %collective-permute-start.11 = (bf16[128,512]{1,0:T(8,128)(2,1)S(1)}, bf16[128,512]{1,0:T(8,128)(2,1)S(1)}, u32[]{:S(2)}, u32[]{:S(2)}) collective-permute-start(bf16[128,512]{1,0:T(8,128)(2,1)S(1)} %collective-permute-done.9.refs_3_), channel_id=1, source_target_pairs={{4,0},{5,1},{8,4},{9,5},{12,8},{13,9},{14,12},{15,13},{10,14},{11,... | collective-permute-start | bytes 393224 | tf_op jit(solution)/shard_map/ppermute | solution.py:263
  21.8 0.4 %collective-permute-done.2.refs_0_ = bf16[128,512]{1,0:T(8,128)(2,1)S(1)} collective-permute-done((bf16[128,512]{1,0:T(8,128)(2,1)S(1)}, bf16[128,512]{1,0:T(8,128)(2,1)S(1)}, u32[]{:S(2)}, u32[]{:S(2)}) %collective-permute-start.2) | collective-permute-done | bytes 131104 | tf_op jit(solution)/shard_map/ppermute | solution.py:263
  22.2 0.0 collective-permute-start.3
  22.2 0.0 copy-done.5
  22.2 0.0 copy-done.6
  22.3 0.0 copy-done.7
  22.3 1.6 %shard_map.155 = (f32[3,128,512]{2,1,0:T(8,128)S(1)}, f32[3,128,512]{2,1,0:T(8,128)S(1)}, bf16[512,512]{1,0:T(8,128)(2,1)S(1)}, bf16[256,512]{1,0:T(8,128)(2,1)S(1)}) custom-call(bf16[128,512]{1,0:T(8,128)(2,1)S(1)} %bitcast.15, bf16[128,512]{1,0:T(8,128)(2,1)S(1)} %collective-permute-done.refs_1_, bf16[128,512]{1,0:T(8,128)(2,1)S(1)} %collective-permute-done.13.refs_2_, ...), custom_call_target="tpu_custom_call" | custom-call | flops 1006632960 | bytes 4202496 | tf_op jit(solution)/shard_map/pallas_call | solution.py:219
  23.8 0.0 copy-start.10
  23.8 0.0 collective-permute-done.17.refs_1_
  23.8 1.2 %collective-permute-done.18.refs_2_ = bf16[128,512]{1,0:T(8,128)(2,1)S(1)} collective-permute-done((bf16[128,512]{1,0:T(8,128)(2,1)S(1)}, bf16[128,512]{1,0:T(8,128)(2,1)S(1)}, u32[]{:S(2)}, u32[]{:S(2)}) %collective-permute-start.18) | collective-permute-done | bytes 131104 | tf_op jit(solution)/shard_map/ppermute | solution.py:263
  25.0 0.9 %shard_map.156 = (f32[3,128,512]{2,1,0:T(8,128)S(1)}, f32[3,128,512]{2,1,0:T(8,128)S(1)}) custom-call(bf16[128,512]{1,0:T(8,128)(2,1)S(1)} %collective-permute-done.2.refs_0_, bf16[128,512]{1,0:T(8,128)(2,1)S(1)} %collective-permute-done.17.refs_1_, bf16[128,512]{1,0:T(8,128)(2,1)S(1)} %collective-permute-done.18.refs_2_, ...), custom_call_target="tpu_custom_call" | custom-call | flops 402653184 | bytes 5767168 | tf_op jit(solution)/shard_map/pallas_call | solution.py:219
  25.9 0.1 collective-permute-start.19
  26.0 0.0 copy-done.10
  26.0 0.5 %shard_map.159.in_col_t_ref = bf16[12,512,128]{2,1,0:T(8,128)(2,1)S(1)} custom-call(s32[3,4,512]{2,1,0:T(4,128)S(1)} %copy-done.10, f32[3,128,512]{2,1,0:T(8,128)S(1)} %get-tuple-element.46.refs_0_), custom_call_target="tpu_custom_call" | custom-call | flops 1000000000 | bytes 1622016 | tf_op jit(solution)/shard_map/pallas_call | solution.py:219
  26.5 0.0 copy-start
  26.5 0.0 copy-start.1
  26.5 0.0 copy-start.2
  26.5 0.0 copy-start.3
  26.5 0.0 copy-start.4
  26.5 0.7 %collective-permute-done.3.refs_0_ = bf16[128,512]{1,0:T(8,128)(2,1)S(1)} collective-permute-done((bf16[128,512]{1,0:T(8,128)(2,1)S(1)}, bf16[128,512]{1,0:T(8,128)(2,1)S(1)}, u32[]{:S(2)}, u32[]{:S(2)}) %collective-permute-start.3) | collective-permute-done | bytes 131104 | tf_op jit(solution)/shard_map/ppermute | solution.py:263
  27.2 0.0 collective-permute-start.4
  27.2 0.0 collective-permute-done.11.refs_1_.refs_2_
  27.2 0.5 %collective-permute-start.12 = (bf16[128,512]{1,0:T(8,128)(2,1)S(1)}, bf16[128,512]{1,0:T(8,128)(2,1)S(1)}, u32[]{:S(2)}, u32[]{:S(2)}) collective-permute-start(bf16[128,512]{1,0:T(8,128)(2,1)S(1)} %collective-permute-done.11.refs_1_.refs_2_), channel_id=1, source_target_pairs={{0,1},{1,0},{2,3},{3,2},{4,5},{5,4},{6,7},{7,6},{8,9},{9,8},{10,11... | collective-permute-start | bytes 393224 | tf_op jit(solution)/shard_map/ppermute | solution.py:263
  27.7 0.5 %shard_map.157 = (bf16[12,128,512]{2,1,0:T(8,128)(2,1)S(1)}, bf16[12,128,512]{2,1,0:T(8,128)(2,1)S(1)}) custom-call(s32[3,4,512]{2,1,0:T(4,128)S(1)} %copy-done.10, bf16[128,512]{1,0:T(8,128)(2,1)S(1)} %collective-permute-done.3.refs_0_, bf16[128,512]{1,0:T(8,128)(2,1)S(1)} %collective-permute-done.11.refs_1_.refs_2_), custom_call_target="tpu_custom_call" | custom-call | flops 10000000000 | bytes 573440 | tf_op jit(solution)/shard_map/pallas_call | solution.py:219
  28.2 0.3 collective-permute-done.4.refs_1_
  28.5 0.2 collective-permute-done.12.refs_3_
  28.7 0.0 collective-permute-done.19.refs_7_
  28.7 0.0 copy-done
  28.8 1.7 %shard_map.158 = (f32[12,128,128]{2,1,0:T(8,128)S(1)}, f32[12,128,128]{2,1,0:T(8,128)S(1)}, f32[3,4,512]{2,1,0:T(4,128)S(1)}) custom-call(bf16[128,512]{1,0:T(8,128)(2,1)S(1)} %collective-permute-done.3.refs_0_, bf16[128,512]{1,0:T(8,128)(2,1)S(1)} %collective-permute-done.4.refs_1_, bf16[128,512]{1,0:T(8,128)(2,1)S(1)} %collective-permute-done.11.refs_1_.refs_2_, ...), custom_call_target="tpu_custom_call" | custom-call | flops 1000000000 | bytes 13893632 | tf_op jit(solution)/shard_map/pallas_call | solution.py:219
  30.5 1.6 %collective-permute-start.20 = (f32[3,4,512]{2,1,0:T(4,128)S(1)}, f32[3,4,512]{2,1,0:T(4,128)S(1)}, u32[]{:S(2)}, u32[]{:S(2)}) collective-permute-start(f32[3,4,512]{2,1,0:T(4,128)S(1)} %get-tuple-element.55), channel_id=1, source_target_pairs={{0,16},{16,0},{1,17},{17,1},{2,18},{18,2},{3,19},{19,3},{4,20},{20... | collective-permute-start | bytes 73736 | tf_op jit(solution)/shard_map/ppermute | solution.py:429
  32.1 2.0 %shard_map.160 = (f32[4,128,128]{2,1,0:T(8,128)}, f32[4,128,128]{2,1,0:T(8,128)}, f32[4,128,128]{2,1,0:T(8,128)}, f32[12,128,128]{2,1,0:T(8,128)S(1)}, bf16[12,512,256]{2,1,0:T(8,128)(2,1)S(1)}) custom-call(f32[12,128,128]{2,1,0:T(8,128)S(1)} %get-tuple-element.49.moment_ref, f32[12,128,128]{2,1,0:T(8,128)S(1)} %get-tuple-element.50.coeffs_ref, ...), custom_call_target="tpu_custom_call" | custom-call | flops 301989888 | bytes 9699328 | tf_op jit(solution)/shard_map/pallas_call | solution.py:219
  34.1 0.3 collective-permute-done.20
  34.4 2.3 %shard_map.161 = (f32[4,128,128]{2,1,0:T(8,128)}, f32[4,128,128]{2,1,0:T(8,128)}, f32[4,128,128]{2,1,0:T(8,128)}) custom-call(f32[12,128,128]{2,1,0:T(8,128)S(1)} %get-tuple-element.54.decoded_ref, f32[1,3,4,512]{3,2,1,0:T(4,128)S(1)} %bitcast.12, bf16[12,128,512]{2,1,0:T(8,128)(2,1)S(1)} %get-tuple-element.47.refs_11_.in_row_ref, ...), custom_call_target="tpu_custom_call" | custom-call | flops 301989888 | bytes 11190272 | tf_op jit(solution)/shard_map/pallas_call | solution.py:219
  (8 shorter events, 0.0 us)
Async XLA Ops:
  0.6 7.0 %collective-permute-start.5 = (bf16[128,512]{1,0:T(8,128)(2,1)}, bf16[128,512]{1,0:T(8,128)(2,1)S(1)}, u32[]{:S(2)}, u32[]{:S(2)}) collective-permute-start(bf16[128,512]{1,0:T(8,128)(2,1)} %bitcast.16), channel_id=1, source_target_pairs={{4,0},{5,1},{8,4},{9,5},{12,8},{13,9},{14,12},{15,13},{10,14},{11,... | collective-permute-start | bytes 393224 | tf_op jit(solution)/shard_map/ppermute | solution.py:263
  3.6 4.0 %collective-permute-start.6 = (bf16[4,128,128]{2,1,0:T(8,128)(2,1)}, bf16[4,128,128]{2,1,0:T(8,128)(2,1)S(1)}, u32[]{:S(2)}, u32[]{:S(2)}) collective-permute-start(bf16[4,128,128]{2,1,0:T(8,128)(2,1)} %refs_10_.1), channel_id=1, source_target_pairs={{0,1},{1,0},{2,3},{3,2},{4,5},{5,4},{6,7},{7,6},{8,9},{9,8},{10,11... | collective-permute-start | bytes 393224 | tf_op jit(solution)/shard_map/ppermute | solution.py:263
  3.6 4.0 %copy-start.8 = (bf16[4,128,128]{2,1,0:T(8,128)(2,1)S(1)}, bf16[4,128,128]{2,1,0:T(8,128)(2,1)}, u32[]{:S(2)}) copy-start(bf16[4,128,128]{2,1,0:T(8,128)(2,1)} %refs_11_.1) | copy-start | bytes 393220
  3.6 9.6 %copy-start.9 = (bf16[4,128,128]{2,1,0:T(8,128)(2,1)S(1)}, bf16[4,128,128]{2,1,0:T(8,128)(2,1)}, u32[]{:S(2)}) copy-start(bf16[4,128,128]{2,1,0:T(8,128)(2,1)} %refs_12_.1) | copy-start | bytes 393220
  3.6 18.6 %copy-start.5 = (bf16[1,128,512]{2,1,0:T(8,128)(2,1)S(1)}, bf16[1,128,512]{2,1,0:T(8,128)(2,1)}, u32[]{:S(2)}) copy-start(bf16[1,128,512]{2,1,0:T(8,128)(2,1)} %param.11) | copy-start | bytes 393220
  3.6 18.6 %copy-start.6 = (bf16[1,128,512]{2,1,0:T(8,128)(2,1)S(1)}, bf16[1,128,512]{2,1,0:T(8,128)(2,1)}, u32[]{:S(2)}) copy-start(bf16[1,128,512]{2,1,0:T(8,128)(2,1)} %param.12) | copy-start | bytes 393220
  3.6 18.6 %copy-start.7 = (bf16[4,128,128]{2,1,0:T(8,128)(2,1)S(1)}, bf16[4,128,128]{2,1,0:T(8,128)(2,1)}, u32[]{:S(2)}) copy-start(bf16[4,128,128]{2,1,0:T(8,128)(2,1)} %refs_10_.1) | copy-start | bytes 393220
  3.7 6.6 %collective-permute-start = (bf16[128,512]{1,0:T(8,128)(2,1)}, bf16[128,512]{1,0:T(8,128)(2,1)S(1)}, u32[]{:S(2)}, u32[]{:S(2)}) collective-permute-start(bf16[128,512]{1,0:T(8,128)(2,1)} %bitcast.13), channel_id=1, source_target_pairs={{0,4},{1,5},{4,8},{5,9},{8,12},{9,13},{12,14},{13,15},{14,10},{15,... | collective-permute-start | bytes 393224 | tf_op jit(solution)/shard_map/ppermute | solution.py:263
  3.9 6.5 %collective-permute-start.13 = (bf16[128,512]{1,0:T(8,128)(2,1)}, bf16[128,512]{1,0:T(8,128)(2,1)S(1)}, u32[]{:S(2)}, u32[]{:S(2)}) collective-permute-start(bf16[128,512]{1,0:T(8,128)(2,1)} %bitcast.14), channel_id=1, source_target_pairs={{4,0},{5,1},{8,4},{9,5},{12,8},{13,9},{14,12},{15,13},{10,14},{11,... | collective-permute-start | bytes 393224 | tf_op jit(solution)/shard_map/ppermute | solution.py:263
  5.7 7.3 %collective-permute-start.15 = (bf16[128,512]{1,0:T(8,128)(2,1)}, bf16[128,512]{1,0:T(8,128)(2,1)S(1)}, u32[]{:S(2)}, u32[]{:S(2)}) collective-permute-start(bf16[128,512]{1,0:T(8,128)(2,1)} %bitcast.17), channel_id=1, source_target_pairs={{0,4},{1,5},{4,8},{5,9},{8,12},{9,13},{12,14},{13,15},{14,10},{15,... | collective-permute-start | bytes 393224 | tf_op jit(solution)/shard_map/ppermute | solution.py:263
  7.6 5.6 %collective-permute-start.8 = (bf16[4,128,128]{2,1,0:T(8,128)(2,1)S(1)}, bf16[4,128,128]{2,1,0:T(8,128)(2,1)S(1)}, u32[]{:S(2)}, u32[]{:S(2)}) collective-permute-start(bf16[4,128,128]{2,1,0:T(8,128)(2,1)S(1)} %copy-done.8), channel_id=1, source_target_pairs={{0,1},{1,0},{2,3},{3,2},{4,5},{5,4},{6,7},{7,6},{8,9},{9,8},{10,11... | collective-permute-start | bytes 393224 | tf_op jit(solution)/shard_map/ppermute | solution.py:263
  7.6 6.3 %collective-permute-start.7 = (bf16[128,512]{1,0:T(8,128)(2,1)S(1)}, bf16[128,512]{1,0:T(8,128)(2,1)S(1)}, u32[]{:S(2)}, u32[]{:S(2)}) collective-permute-start(bf16[128,512]{1,0:T(8,128)(2,1)S(1)} %collective-permute-done.5.refs_7_), channel_id=1, source_target_pairs={{4,0},{5,1},{8,4},{9,5},{12,8},{13,9},{14,12},{15,13},{10,14},{11,... | collective-permute-start | bytes 393224 | tf_op jit(solution)/shard_map/ppermute | solution.py:263
  10.2 5.7 %collective-permute-start.1 = (bf16[128,512]{1,0:T(8,128)(2,1)S(1)}, bf16[128,512]{1,0:T(8,128)(2,1)S(1)}, u32[]{:S(2)}, u32[]{:S(2)}) collective-permute-start(bf16[128,512]{1,0:T(8,128)(2,1)S(1)} %collective-permute-done.refs_1_), channel_id=1, source_target_pairs={{0,4},{1,5},{4,8},{5,9},{8,12},{9,13},{12,14},{13,15},{14,10},{15,... | collective-permute-start | bytes 393224 | tf_op jit(solution)/shard_map/ppermute | solution.py:263
  10.4 6.0 %collective-permute-start.14 = (bf16[128,512]{1,0:T(8,128)(2,1)S(1)}, bf16[128,512]{1,0:T(8,128)(2,1)S(1)}, u32[]{:S(2)}, u32[]{:S(2)}) collective-permute-start(bf16[128,512]{1,0:T(8,128)(2,1)S(1)} %collective-permute-done.13.refs_2_), channel_id=1, source_target_pairs={{4,0},{5,1},{8,4},{9,5},{12,8},{13,9},{14,12},{15,13},{10,14},{11,... | collective-permute-start | bytes 393224 | tf_op jit(solution)/shard_map/ppermute | solution.py:263
  13.0 5.6 %collective-permute-start.16 = (bf16[128,512]{1,0:T(8,128)(2,1)S(1)}, bf16[128,512]{1,0:T(8,128)(2,1)S(1)}, u32[]{:S(2)}, u32[]{:S(2)}) collective-permute-start(bf16[128,512]{1,0:T(8,128)(2,1)S(1)} %collective-permute-done.15.refs_6_), channel_id=1, source_target_pairs={{0,4},{1,5},{4,8},{5,9},{8,12},{9,13},{12,14},{13,15},{14,10},{15,... | collective-permute-start | bytes 393224 | tf_op jit(solution)/shard_map/ppermute | solution.py:263
  13.2 5.5 %collective-permute-start.10 = (bf16[4,128,128]{2,1,0:T(8,128)(2,1)S(1)}, bf16[4,128,128]{2,1,0:T(8,128)(2,1)S(1)}, u32[]{:S(2)}, u32[]{:S(2)}) collective-permute-start(bf16[4,128,128]{2,1,0:T(8,128)(2,1)S(1)} %copy-done.9), channel_id=1, source_target_pairs={{0,1},{1,0},{2,3},{3,2},{4,5},{5,4},{6,7},{7,6},{8,9},{9,8},{10,11... | collective-permute-start | bytes 393224 | tf_op jit(solution)/shard_map/ppermute | solution.py:263
  14.0 5.9 %collective-permute-start.9 = (bf16[128,512]{1,0:T(8,128)(2,1)S(1)}, bf16[128,512]{1,0:T(8,128)(2,1)S(1)}, u32[]{:S(2)}, u32[]{:S(2)}) collective-permute-start(bf16[128,512]{1,0:T(8,128)(2,1)S(1)} %collective-permute-done.7.refs_9_), channel_id=1, source_target_pairs={{4,0},{5,1},{8,4},{9,5},{12,8},{13,9},{14,12},{15,13},{10,14},{11,... | collective-permute-start | bytes 393224 | tf_op jit(solution)/shard_map/ppermute | solution.py:263
  15.9 6.3 %collective-permute-start.2 = (bf16[128,512]{1,0:T(8,128)(2,1)S(1)}, bf16[128,512]{1,0:T(8,128)(2,1)S(1)}, u32[]{:S(2)}, u32[]{:S(2)}) collective-permute-start(bf16[128,512]{1,0:T(8,128)(2,1)S(1)} %collective-permute-done.1.refs_3_), channel_id=1, source_target_pairs={{0,4},{1,5},{4,8},{5,9},{8,12},{9,13},{12,14},{13,15},{14,10},{15,... | collective-permute-start | bytes 393224 | tf_op jit(solution)/shard_map/ppermute | solution.py:263
  16.4 7.4 %collective-permute-start.17 = (bf16[128,512]{1,0:T(8,128)(2,1)S(1)}, bf16[128,512]{1,0:T(8,128)(2,1)S(1)}, u32[]{:S(2)}, u32[]{:S(2)}) collective-permute-start(bf16[128,512]{1,0:T(8,128)(2,1)S(1)} %collective-permute-done.14.refs_4_), channel_id=1, source_target_pairs={{4,0},{5,1},{8,4},{9,5},{12,8},{13,9},{14,12},{15,13},{10,14},{11,... | collective-permute-start | bytes 393224 | tf_op jit(solution)/shard_map/ppermute | solution.py:263
  18.6 6.5 %collective-permute-start.18 = (bf16[128,512]{1,0:T(8,128)(2,1)S(1)}, bf16[128,512]{1,0:T(8,128)(2,1)S(1)}, u32[]{:S(2)}, u32[]{:S(2)}) collective-permute-start(bf16[128,512]{1,0:T(8,128)(2,1)S(1)} %collective-permute-done.16.refs_8_), channel_id=1, source_target_pairs={{0,4},{1,5},{4,8},{5,9},{8,12},{9,13},{12,14},{13,15},{14,10},{15,... | collective-permute-start | bytes 393224 | tf_op jit(solution)/shard_map/ppermute | solution.py:263
  19.9 7.3 %collective-permute-start.11 = (bf16[128,512]{1,0:T(8,128)(2,1)S(1)}, bf16[128,512]{1,0:T(8,128)(2,1)S(1)}, u32[]{:S(2)}, u32[]{:S(2)}) collective-permute-start(bf16[128,512]{1,0:T(8,128)(2,1)S(1)} %collective-permute-done.9.refs_3_), channel_id=1, source_target_pairs={{4,0},{5,1},{8,4},{9,5},{12,8},{13,9},{14,12},{15,13},{10,14},{11,... | collective-permute-start | bytes 393224 | tf_op jit(solution)/shard_map/ppermute | solution.py:263
  22.2 5.0 %collective-permute-start.3 = (bf16[128,512]{1,0:T(8,128)(2,1)S(1)}, bf16[128,512]{1,0:T(8,128)(2,1)S(1)}, u32[]{:S(2)}, u32[]{:S(2)}) collective-permute-start(bf16[128,512]{1,0:T(8,128)(2,1)S(1)} %collective-permute-done.2.refs_0_), channel_id=1, source_target_pairs={{0,4},{1,5},{4,8},{5,9},{8,12},{9,13},{12,14},{13,15},{14,10},{15,... | collective-permute-start | bytes 393224 | tf_op jit(solution)/shard_map/ppermute | solution.py:263
  23.8 2.2 %copy-start.10 = (s32[3,4,512]{2,1,0:T(4,128)S(1)}, s32[3,4,512]{2,1,0:T(4,128)}, u32[]{:S(2)}) copy-start(s32[3,4,512]{2,1,0:T(4,128)} %index_ref.3) | copy-start | bytes 73732
  25.9 2.8 %collective-permute-start.19 = (f32[3,128,512]{2,1,0:T(8,128)S(1)}, f32[3,128,512]{2,1,0:T(8,128)S(1)}, u32[]{:S(2)}, u32[]{:S(2)}) collective-permute-start(f32[3,128,512]{2,1,0:T(8,128)S(1)} %get-tuple-element.46.refs_0_), channel_id=1, source_target_pairs={{0,1},{1,0},{2,3},{3,2},{4,5},{5,4},{6,7},{7,6},{8,9},{9,8},{10,11... | collective-permute-start | bytes 2359304 | tf_op jit(solution)/shard_map/ppermute | solution.py:263
  26.5 2.3 %copy-start = (f32[128,128]{1,0:T(8,128)S(1)}, f32[128,128]{1,0:T(8,128)}, u32[]{:S(2)}) copy-start(f32[128,128]{1,0:T(8,128)} %constant.5.clone.refs_14_.cosines_t_ref) | copy-start | bytes 196612
  26.5 2.3 %copy-start.1 = (f32[128,128]{1,0:T(8,128)S(1)}, f32[128,128]{1,0:T(8,128)}, u32[]{:S(2)}) copy-start(f32[128,128]{1,0:T(8,128)} %constant.4.clone.refs_13_.cosines_ref) | copy-start | bytes 196612
  26.5 2.3 %copy-start.2 = (f32[1,4,128,128]{3,2,1,0:T(8,128)S(1)}, f32[1,4,128,128]{3,2,1,0:T(8,128)}, u32[]{:S(2)}) copy-start(f32[1,4,128,128]{3,2,1,0:T(8,128)} %param.16) | copy-start | bytes 786436
  26.5 2.3 %copy-start.3 = (f32[1,4,128,128]{3,2,1,0:T(8,128)S(1)}, f32[1,4,128,128]{3,2,1,0:T(8,128)}, u32[]{:S(2)}) copy-start(f32[1,4,128,128]{3,2,1,0:T(8,128)} %param.17) | copy-start | bytes 786436
  26.5 2.3 %copy-start.4 = (f32[1,4,128,128]{3,2,1,0:T(8,128)S(1)}, f32[1,4,128,128]{3,2,1,0:T(8,128)}, u32[]{:S(2)}) copy-start(f32[1,4,128,128]{3,2,1,0:T(8,128)} %param.18) | copy-start | bytes 786436
  27.2 1.3 %collective-permute-start.4 = (bf16[128,512]{1,0:T(8,128)(2,1)S(1)}, bf16[128,512]{1,0:T(8,128)(2,1)S(1)}, u32[]{:S(2)}, u32[]{:S(2)}) collective-permute-start(bf16[128,512]{1,0:T(8,128)(2,1)S(1)} %collective-permute-done.3.refs_0_), channel_id=1, source_target_pairs={{0,1},{1,0},{2,3},{3,2},{4,5},{5,4},{6,7},{7,6},{8,9},{9,8},{10,11... | collective-permute-start | bytes 393224 | tf_op jit(solution)/shard_map/ppermute | solution.py:263
  27.2 1.5 %collective-permute-start.12 = (bf16[128,512]{1,0:T(8,128)(2,1)S(1)}, bf16[128,512]{1,0:T(8,128)(2,1)S(1)}, u32[]{:S(2)}, u32[]{:S(2)}) collective-permute-start(bf16[128,512]{1,0:T(8,128)(2,1)S(1)} %collective-permute-done.11.refs_1_.refs_2_), channel_id=1, source_target_pairs={{0,1},{1,0},{2,3},{3,2},{4,5},{5,4},{6,7},{7,6},{8,9},{9,8},{10,11... | collective-permute-start | bytes 393224 | tf_op jit(solution)/shard_map/ppermute | solution.py:263
  30.5 3.9 %collective-permute-start.20 = (f32[3,4,512]{2,1,0:T(4,128)S(1)}, f32[3,4,512]{2,1,0:T(4,128)S(1)}, u32[]{:S(2)}, u32[]{:S(2)}) collective-permute-start(f32[3,4,512]{2,1,0:T(4,128)S(1)} %get-tuple-element.55), channel_id=1, source_target_pairs={{0,16},{16,0},{1,17},{17,1},{2,18},{18,2},{3,19},{19,3},{4,20},{20... | collective-permute-start | bytes 73736 | tf_op jit(solution)/shard_map/ppermute | solution.py:429
